TPU v7x, 32 devices: a whole 2x2x4 slice. The times are simulated.
32 devices in a mesh: node: 16 (over z, x, core), term: 2 (over y).
Axes of the slice: x: 2, y: 2, z: 4, core: 2. Of those that a mesh axis runs over, the one named last changes fastest.
Arguments:
- node_tensors: bfloat16 [16, 64, 4096], P('node'), may hold values from -0.046875 to 1.046875
- prim_ops: bfloat16 [16, 8, 2, 64, 64], P('node', 'term'), may hold values from -3.8 to 3.8, as said below
- active: int32 [16, 8, 2], P('node', 'term'), may hold values 0 or 1
- top_field: bfloat16 [8, 64, 64], P('term'), may hold values from -0.95 to 0.95, as said below
- node_map: int32 [16], replicated, may hold values from 0 to 15, as said below
Outputs:
- derivative: bfloat16 [16, 64, 4096], P('node', 'term')
Inputs may be any that keep to these rules, and one draw needn't show every extreme that they name: node_map holds every position 0 to 15 once; position 15 is no node; the slot of position 1 is the slot of position 0 plus 16 // 2, counted round. `prim_ops`: each operator is symmetric. `top_field`: each matrix is symmetric.
All inputs are finite; a program needn't handle non-finite values. No bound on the sum of `active` on one device may be relied on, other than what follows from the above.
Results may differ from a plain program's by a relative error of at most 0.025.
The roundings to bfloat16 on the way count: a program that leaves them out, or rounds other values in their place, can miss the bound.
Values may be sent and summed in bfloat16 or wider, within the bound.
No kernel may reach another device: no remote copies, remote signals or barrier semaphores. Data moves between devices by JAX's collectives and lax.ppermute only.
A program may use at most 64 MiB of HBM per device.

v0:
```python
import functools
import math

import jax
import jax.numpy as jnp
from jax import lax
from jax.experimental import pallas as pl
from jax.experimental.pallas import tpu as pltpu
from jax.sharding import PartitionSpec as P

LANES = 128
WIDE = 256
BATCH = 2
PAD = 16
KEPT = 2**18


def dot(left, right):
    return jnp.dot(left, right, preferred_element_type=jnp.float32)


def iota(shape, dim):
    return lax.broadcasted_iota(jnp.int32, shape, dim)


def split_terms(packed, extent):
    per = LANES // extent
    wide = packed.astype(jnp.float32)
    out = []
    for term in range(per * packed.shape[0] // extent):
        block = wide[(term // per) * extent : (term // per + 1) * extent]
        mine = lax.div(iota(block.shape, 1), extent) == term % per
        out.append(jnp.where(mine, block, 0.0).astype(jnp.bfloat16))
    return out


def rows_spread(tensor_ref, mats, spread_ref, extent):
    per = LANES // extent
    half = extent // per
    stack = jnp.concatenate(mats, axis=0)
    for chunk in range(extent * extent // WIDE):
        piece = tensor_ref[:, chunk * WIDE : (chunk + 1) * WIDE]
        result = dot(stack, jnp.concatenate([piece] * per, axis=0))
        for part in range(WIDE // LANES):
            i = chunk * (WIDE // LANES) + part
            for term in range(len(mats)):
                spread_ref[term, pl.ds(i, extent, stride=half), :] = result[
                    term * extent : (term + 1) * extent, part * LANES : (part + 1) * LANES
                ]


SUB = 8


def rows_apply(tensor_ref, mats, mixed_ref, extent):
    per = LANES // extent
    quads = WIDE // extent
    halves = SUB // quads
    count = 2 * halves
    stack = jnp.concatenate(mats, axis=0)
    row = iota((extent // SUB, SUB, LANES), 1)
    for first in range(0, extent // per, count):
        piece = tensor_ref[:, first * LANES : (first + count) * LANES]
        result = dot(stack, jnp.concatenate([piece] * per, axis=0))
        for term in range(len(mats)):
            tiles = [
                result[term * extent : (term + 1) * extent, k * LANES : (k + 1) * LANES].reshape(row.shape)
                for k in range(count)
            ]
            for half in range(halves):
                wanted = []
                for start in range(0, count, halves):
                    block = None
                    for k in range(halves):
                        shift = (k - half) * quads % SUB
                        moved = pltpu.roll(tiles[start + k], shift, 1) if shift else tiles[start + k]
                        block = moved if block is None else jnp.where(lax.div(row, quads) == k, moved, block)
                    wanted.append(block)
                packed = jnp.concatenate(wanted, axis=1).astype(jnp.bfloat16)
                for m in range(extent // SUB):
                    base = (m * halves + half) * (extent // per) * quads + first * quads
                    mixed_ref[term, base : base + count * quads, :] = packed[m]


def block_diagonals(mats, extent):
    per = LANES // extent
    quads = WIDE // extent
    rows = lax.rem(iota((LANES, WIDE), 0), extent)
    lanes = iota((LANES, WIDE), 1)
    wanted = per * lax.div(lax.rem(lanes, WIDE // per), quads) + lax.div(lanes, WIDE // per)
    pick = jnp.where(rows == wanted, 1.0, 0.0).astype(jnp.bfloat16)
    spread = dot(jnp.concatenate(mats, axis=0), pick)
    lanes = iota((WIDE, WIDE), 1)
    same = lax.div(iota((WIDE, WIDE), 0), extent) == lax.rem(lanes, quads)
    out = []
    for term in range(len(mats)):
        block = spread[term * extent : (term + 1) * extent]
        out.append(jnp.where(same, jnp.concatenate([block] * quads, axis=0), 0.0).astype(jnp.bfloat16))
    return out


def tall(tensor_ref):
    width = tensor_ref.shape[1]
    return jnp.concatenate([tensor_ref[:, j : j + WIDE] for j in range(0, width, WIDE)], axis=0)


def pair_up(accs, extent):
    per = LANES // extent
    out = []
    for first in range(0, len(accs), per):
        blocks = None
        for lo in range(per):
            acc = accs[first + lo]
            group = lax.div(iota((extent, LANES), 1), extent)
            kept = jnp.zeros((extent, LANES), jnp.float32)
            for p in range(per):
                kept = jnp.where(group == p, acc[p * extent : (p + 1) * extent], kept)
            total = kept
            for p in range(1, per):
                total = total + pltpu.roll(kept, p * extent, 1)
            blocks = total if blocks is None else jnp.where(group == lo, total, blocks)
        out.append(blocks)
    return out


def below_diagonal(shape, extent):
    rows, lanes = iota(shape, 0), lax.rem(iota(shape, 1), extent)
    return rows > lanes, rows == lanes


def fold(blocks):
    extent = blocks[0].shape[0]
    below, on = below_diagonal(blocks[0].shape, extent)
    out = []
    for first in range(0, len(blocks), 2):
        lower, upper = blocks[first], blocks[min(first + 1, len(blocks) - 1)]
        out.append(jnp.where(jnp.logical_or(below, on), lower, upper))
        row = jnp.sum(jnp.where(on, upper, 0.0), axis=0, keepdims=True)
        out.append(jnp.broadcast_to(row, (PAD, LANES)))
    return jnp.concatenate(out, axis=0).astype(jnp.bfloat16)


def unfold(message, pairs):
    height = message.shape[0] // (-(-pairs // 2))
    extent = height - PAD
    wide = message.astype(jnp.float32)
    out = []
    for base in range(0, message.shape[0], height):
        body, row = wide[base : base + extent], wide[base + extent : base + extent + 1]
        below, on = below_diagonal(body.shape, extent)
        turned = body.T
        parts = [turned[k : k + extent] for k in range(0, LANES, extent)]
        turned = jnp.concatenate(parts, axis=1)
        out.append(jnp.where(jnp.logical_or(below, on), body, turned))
        out.append(jnp.where(below, turned, jnp.where(on, row, body)))
    return jnp.concatenate(out[:pairs], axis=0).astype(jnp.bfloat16)


def apply_lanes(stacked, diagonals, extent):
    per = LANES // extent
    groups = stacked.shape[0] // extent
    lefts = []
    for diagonal in diagonals:
        moved = dot(stacked, diagonal).astype(jnp.bfloat16)
        for p in range(per):
            lanes = slice(p * (WIDE // per), (p + 1) * (WIDE // per))
            lefts.append(jnp.concatenate([moved[j * extent : (j + 1) * extent, lanes] for j in range(groups)], axis=1))
    return lefts


def contract(lefts, mixed, extent):
    per = LANES // extent
    accs = []
    for first in range(0, len(lefts) // per, BATCH):
        left = jnp.concatenate(lefts[first * per : (first + BATCH) * per], axis=0)
        right = jnp.concatenate([mixed[term] for term in range(first, first + BATCH)], axis=1)
        result = dot(left, right)
        for k in range(BATCH):
            accs.append(result[k * LANES : (k + 1) * LANES, k * LANES : (k + 1) * LANES])
    return fold(pair_up(accs, extent))


def swap(value, turn_ref, out_ref, extent):
    per = LANES // extent
    half = extent // per
    rows = iota((extent, extent), 0)
    wanted = per * lax.rem(rows, half) + lax.div(rows, half)
    order = jnp.where(iota((extent, extent), 1) == wanted, 1.0, 0.0).astype(jnp.bfloat16)
    sorted_rows = dot(order, value)
    group = lax.div(iota((half, LANES), 1), extent)
    for j in range(extent // per):
        given = [sorted_rows[p * half : (p + 1) * half, j * LANES : (j + 1) * LANES] for p in range(per)]
        for q in range(per):
            row = None
            for p in range(per):
                shift = (p - q) * extent % LANES
                moved = pltpu.roll(given[p], shift, 1) if shift else given[p]
                row = moved if row is None else jnp.where(group == p, moved, row)
            turn_ref[pl.ds(per * j + q, half, stride=extent), :] = row
    for i in range(half):
        out_ref[:, i * LANES : (i + 1) * LANES] = turn_ref[i * extent : (i + 1) * extent, :].astype(jnp.bfloat16)


def flip(value, extent):
    per = LANES // extent
    wide = value.astype(jnp.float32)
    tiles = []
    for j in range(extent // per):
        turned = wide[:, j * LANES : (j + 1) * LANES].T
        tiles.append(jnp.concatenate([turned[p * extent : (p + 1) * extent] for p in range(per)], axis=1))
    return jnp.concatenate(tiles, axis=1).astype(jnp.bfloat16)


DEPTH, FROM_LEFT, FROM_RIGHT, FROM_PARENT, POSITION, GROUP, APART, UP_RELAY, DOWN_RELAY, TABLE = *range(7), 8, 16, 24
LOW = 4


def entry(table_ref, row):
    return table_ref[row : row + 1, :]


def fill_table(map_ref, me, inverse_ref, table_ref):
    def put(row, value):
        table_ref[row : row + 1, :] = jnp.full((1, LANES), value, jnp.int32)

    nodes = map_ref.shape[0]

    def note(slot, carry):
        inverse_ref[map_ref[slot]] = slot
        return carry

    lax.fori_loop(0, nodes, note, 0)
    low = lax.rem(me, LOW)
    high = lax.div(me, LOW)

    def routes(slot):
        position = map_ref[slot]
        last = jnp.int32(nodes - 1)
        left = inverse_ref[jnp.minimum(2 * position + 1, last)]
        right = inverse_ref[jnp.minimum(2 * position + 2, last)]
        parent = inverse_ref[lax.div(jnp.maximum(position - 1, 0), 2)]
        return position, left, right, parent

    position, left, right, parent = routes(me)
    depth = jnp.int32(0)
    for power in range(1, nodes.bit_length() - 1):
        depth = depth + jnp.where(position + 1 >= 2**power, 1, 0)
    put(DEPTH, jnp.where(position >= nodes - 1, -1, depth))
    put(POSITION, position)
    put(GROUP, lax.axis_index("term"))
    put(APART, inverse_ref[0] ^ inverse_ref[2])
    put(FROM_LEFT, lax.rem(left, LOW) ^ low)
    put(FROM_RIGHT, lax.rem(right, LOW) ^ low)
    put(FROM_PARENT, lax.rem(parent, LOW) ^ low)
    for j in range(LOW):
        position, left, right, parent = routes(high * LOW + (low ^ j))
        put(UP_RELAY + 2 * j, lax.div(left, LOW) ^ high)
        put(UP_RELAY + 2 * j + 1, lax.div(right, LOW) ^ high)
        put(DOWN_RELAY + j, 2 * (lax.div(parent, LOW) ^ high) + lax.rem(position + 1, 2))


def choose(index, choices):
    out = choices[0]().astype(jnp.float32)
    for k in range(1, len(choices)):
        out = jnp.where(index == k, choices[k]().astype(jnp.float32), out)
    return out.astype(jnp.bfloat16)


def either(mask, old, new):
    return choose(jnp.where(mask, 1, 0), [old, new])


def loads(refs, *where):
    return [lambda ref=ref: ref[where] if where else ref[...] for ref in refs]


def start_kernel(
    tensor_hbm, prim_hbm, active_hbm, top_hbm, map_hbm,
    abc_ref, bac_ref, cba_ref, left_ref, right_ref, field_ref, out_ref, table_ref,
    prim_ref, active_ref, top_ref, map_ref, mixed_ref, turn_ref, inverse_ref, sems,
):
    given = (tensor_hbm.at[0], prim_hbm, top_hbm, active_hbm, map_hbm)
    held = (abc_ref, prim_ref, top_ref, active_ref, map_ref)
    copies = [pltpu.make_async_copy(*pair, sems.at[i]) for i, pair in enumerate(zip(given, held))]
    for copy in copies:
        copy.start()
    extent = abc_ref.shape[0]
    per = LANES // extent
    terms = prim_ref.shape[1]
    for copy in copies[:0:-1]:
        copy.wait()
        if copy is copies[-1]:
            fill_table(map_ref, lax.axis_index("node"), inverse_ref, table_ref)
    eye = jnp.where(iota((extent, extent), 0) == iota((extent, extent), 1), 1.0, 0.0)

    def operator(term, side):
        return jnp.where(active_ref[0, side, term] == 1, prim_ref[0, term, side].astype(jnp.float32), eye)

    for first in range(0, terms, per):
        rows = pl.ds(first // per * extent, extent)
        for side, ref in ((0, left_ref), (1, right_ref)):
            side_by_side = [operator(first + lo, side) for lo in range(per)]
            ref[rows, :] = jnp.concatenate(side_by_side, axis=1).astype(jnp.bfloat16)
        fields = [top_ref[first + lo].astype(jnp.float32) for lo in range(per)]
        field_ref[rows, :] = jnp.concatenate(fields, axis=1).astype(jnp.bfloat16)
    diagonals = block_diagonals(split_terms(left_ref[...], extent), extent)
    copies[0].wait()
    swap(abc_ref[...], turn_ref, bac_ref, extent)
    cba_ref[...] = flip(abc_ref[...], extent)
    rows_apply(bac_ref, split_terms(right_ref[...], extent), mixed_ref, extent)
    out_ref[...] = contract(apply_lanes(tall(cba_ref), diagonals, extent), mixed_ref, extent)


def turn_kernel(bac_ref, cba_ref, table_ref, turned_ref, apart_ref, turn_ref):
    extent = bac_ref.shape[0]
    apart_ref[0] = jnp.max(entry(table_ref, APART)) - 1
    swap(cba_ref[...], turn_ref, turned_ref.at[0], extent)
    swap(flip(bac_ref[...], extent), turn_ref, turned_ref.at[1], extent)


def relay_up_kernel(*refs):
    parts, table_ref, outs = refs[:-5], refs[-5], refs[-4:]
    for j, out in enumerate(outs):
        for side in range(2):
            out[side] = choose(entry(table_ref, UP_RELAY + 2 * j + side), loads(parts))


def relay_down_kernel(*refs):
    parts, table_ref, outs = refs[:-5], refs[-5], refs[-4:]
    choices = [f for part in parts for side in range(2) for f in loads([part], side)]
    for j, out in enumerate(outs):
        out[...] = choose(entry(table_ref, DOWN_RELAY + j), choices)


def up_kernel(depth, *refs):
    came, (bac_ref, cba_ref, old_left_ref, old_right_ref, table_ref) = refs[:LOW], refs[LOW : LOW + 5]
    left_ref, right_ref, out_ref, mixed_ref = refs[LOW + 5 :]
    extent = bac_ref.shape[0]
    now = entry(table_ref, DEPTH) == depth
    pairs = old_left_ref.shape[0] // extent
    left = unfold(choose(entry(table_ref, FROM_LEFT), loads(came, 0)), pairs)
    right = unfold(choose(entry(table_ref, FROM_RIGHT), loads(came, 1)), pairs)
    left_ref[...] = either(now, lambda: old_left_ref[...], lambda: left)
    right_ref[...] = either(now, lambda: old_right_ref[...], lambda: right)
    rows_apply(bac_ref, split_terms(right_ref[...], extent), mixed_ref, extent)
    diagonals = block_diagonals(split_terms(left_ref[...], extent), extent)
    out_ref[...] = contract(apply_lanes(tall(cba_ref), diagonals, extent), mixed_ref, extent)


def fetch(came, held, sems):
    copies = [pltpu.make_async_copy(*pair, sems.at[k]) for k, pair in enumerate(zip(came, held))]
    for copy in copies:
        copy.start()
    return copies


def top_kernel(
    came_left_hbm, came_right_hbm, abc_ref, bac_ref, turned_ref, field_ref, old_left_ref, old_right_ref, table_ref,
    sides_ref, out_ref, mixed_ref, came_left_ref, came_right_ref, sems,
):
    copies = fetch((came_left_hbm, came_right_hbm), (came_left_ref, came_right_ref), sems)
    extent = bac_ref.shape[0]
    now = entry(table_ref, DEPTH) == 0
    diagonals = block_diagonals(split_terms(field_ref[...], extent), extent)
    left_lanes = apply_lanes(tall(abc_ref), diagonals, extent)
    for copy in copies:
        copy.wait()
    pairs = old_left_ref.shape[0] // extent
    sides_ref[0] = either(now, lambda: old_left_ref[...], lambda: unfold(came_left_ref[...], pairs))
    sides_ref[1] = either(now, lambda: old_right_ref[...], lambda: unfold(came_right_ref[...], pairs))
    mix(turned_ref, sides_ref, mixed_ref)
    out_ref[0] = contract(left_lanes, mixed_ref.at[0], extent)
    out_ref[1] = contract(apply_lanes(tall(bac_ref), diagonals, extent), mixed_ref.at[1], extent)


def below_top_kernel(
    came_left_ref, came_right_ref, abc_ref, bac_ref, turned_ref, old_ref, sides_ref, table_ref,
    field_ref, out_ref, mixed_ref,
):
    position = entry(table_ref, POSITION)
    came = unfold(either(position == 2, *loads([came_left_ref, came_right_ref])), old_ref.shape[0] // abc_ref.shape[0])
    now = jnp.logical_or(position == 1, position == 2)
    field_ref[...] = either(now, lambda: old_ref[...], lambda: came)
    mix(turned_ref, sides_ref, mixed_ref)
    spread_down(abc_ref, bac_ref, field_ref, out_ref, mixed_ref)


def down_kernel(depth, *refs):
    came, (abc_ref, bac_ref, turned_ref, old_ref, sides_ref, table_ref) = refs[:LOW], refs[LOW : LOW + 6]
    field_ref, out_ref, mixed_ref = refs[LOW + 6 :]
    arrive(depth, old_ref.shape[0] // abc_ref.shape[0], came, old_ref, table_ref, field_ref)
    mix(turned_ref, sides_ref, mixed_ref)
    spread_down(abc_ref, bac_ref, field_ref, out_ref, mixed_ref)


def arrive(depth, pairs, came, old_ref, table_ref, field_ref):
    arrived = choose(entry(table_ref, FROM_PARENT), loads(came))
    arrived = unfold(arrived, pairs)
    field_ref[...] = either(entry(table_ref, DEPTH) == depth, lambda: old_ref[...], lambda: arrived)


def mix(turned_ref, sides_ref, mixed_ref):
    extent = turned_ref.shape[1]
    rows_apply(turned_ref.at[0], split_terms(sides_ref[1], extent), mixed_ref.at[0], extent)
    rows_apply(turned_ref.at[1], split_terms(sides_ref[0], extent), mixed_ref.at[1], extent)


def spread_down(abc_ref, bac_ref, field_ref, out_ref, mixed_ref):
    extent = bac_ref.shape[0]
    diagonals = block_diagonals(split_terms(field_ref[...], extent), extent)
    out_ref[0] = contract(apply_lanes(tall(abc_ref), diagonals, extent), mixed_ref.at[0], extent)
    out_ref[1] = contract(apply_lanes(tall(bac_ref), diagonals, extent), mixed_ref.at[1], extent)


def weigh_kernel(pair, bac_ref, sides_ref, table_ref, out_ref, spread_ref):
    extent = bac_ref.shape[0]
    mine = slice(pair * extent, (pair + 1) * extent)
    rows_out = out_ref.shape[1]
    per = LANES // extent
    half = extent // per
    rows_spread(bac_ref, split_terms(sides_ref[1, mine], extent), spread_ref, extent)
    rows = lax.rem(iota((LANES, extent), 0), extent)
    lanes = iota((LANES, extent), 1)
    wanted = per * lax.rem(lanes, half) + lax.div(lanes, half)
    pick = jnp.where(rows == wanted, 1.0, 0.0).astype(jnp.bfloat16)
    group = lax.div(iota((half, LANES), 1), extent)
    for term, mat in enumerate(split_terms(sides_ref[0, mine], extent)):
        permuted = dot(mat, pick)
        kept = permuted[:rows_out]
        for g in range(1, extent // rows_out):
            kept = jnp.where(entry(table_ref, GROUP)[:, :extent] == g, permuted[g * rows_out : (g + 1) * rows_out], kept)
        kept = kept.astype(jnp.bfloat16)
        tiles = []
        for j in range(extent // per):
            given = [spread_ref[term, (per * j + q) * half : (per * j + q + 1) * half, :] for q in range(per)]
            stacked = []
            for p in range(per):
                row = None
                for q in range(per):
                    shift = (q - p) * extent % LANES
                    moved = pltpu.roll(given[q], shift, 1) if shift else given[q]
                    row = moved if row is None else jnp.where(group == q, moved, row)
                stacked.append(row)
            tiles.append(jnp.concatenate(stacked, axis=0).astype(jnp.bfloat16))
        for j in range(0, len(tiles), WIDE // LANES):
            wide = jnp.concatenate(tiles[j : j + WIDE // LANES], axis=1)
            out_ref[term, :, j * LANES : j * LANES + WIDE] = dot(kept, wide).astype(jnp.bfloat16)


def last_kernel(depth, pairs, *refs):
    came, (old_ref, table_ref, field_ref) = refs[:LOW], refs[LOW:]
    arrive(depth, pairs, came, old_ref, table_ref, field_ref)


def part_kernel(field_ref, *refs):
    out_ref = refs[-1]
    width = refs[0].shape[2]
    out_ref[...] = weighted_sum(refs[:-1], field_ref[...], math.isqrt(width)).astype(jnp.bfloat16)


def finish_kernel(groups, own_ref, *refs):
    table_ref, out_ref = refs[-2:]
    rows, width = out_ref.shape[1:]
    total = own_ref[...].astype(jnp.float32)
    fields, weighed = refs[: groups - 1], refs[groups - 1 : -2]
    for g, field_ref in enumerate(fields):
        pairs = len(weighed) // len(fields)
        part = weighted_sum(weighed[g * pairs : (g + 1) * pairs], field_ref[...], math.isqrt(width))
        total = total + part.astype(jnp.bfloat16).astype(jnp.float32)
    real = jnp.concatenate([entry(table_ref, DEPTH)] * (WIDE // LANES), axis=1) >= 0
    total = jnp.where(real, total, 0.0).astype(jnp.bfloat16)
    for j in range(width // WIDE):
        out_ref[0, :, j * WIDE : (j + 1) * WIDE] = total[j * rows : (j + 1) * rows]


def weighted_sum(weighed_refs, field, extent):
    per, _, width = weighed_refs[0].shape
    quads = WIDE // extent
    copies = pick_rows(LANES, WIDE, extent)
    spread = dot(jnp.concatenate(split_terms(field, extent), axis=0), copies)
    same = lax.div(iota((WIDE, WIDE), 0), extent) == lax.div(iota((WIDE, WIDE), 1), extent)
    total = None
    for term in range(per * len(weighed_refs)):
        weighed_ref = weighed_refs[term // per]
        block = spread[term * extent : (term + 1) * extent]
        diagonal = jnp.where(same, jnp.concatenate([block] * quads, axis=0), 0.0).astype(jnp.bfloat16)
        pieces = [weighed_ref[term % per, :, j : j + WIDE] for j in range(0, width, WIDE)]
        part = dot(jnp.concatenate(pieces, axis=0), diagonal)
        total = part if total is None else total + part
    return total


def pick_rows(rows, lanes, extent):
    same = lax.rem(iota((rows, lanes), 0), extent) == lax.rem(iota((rows, lanes), 1), extent)
    return jnp.where(same, 1.0, 0.0).astype(jnp.bfloat16)


VMEM = pl.BlockSpec(memory_space=pltpu.VMEM)
SMEM = pl.BlockSpec(memory_space=pltpu.SMEM)
HBM = pl.BlockSpec(memory_space=pltpu.HBM)


def call(kernel, out_shape, *operands, scratch=(), smem_out=(), in_hbm=(), kept=True, beside=()):
    shapes = out_shape if isinstance(out_shape, list) else [out_shape]
    specs = [SMEM if i in smem_out else VMEM for i in range(len(shapes))]
    taken = [VMEM] * len(operands)
    operands = list(operands)
    for i, operand in enumerate(operands):
        if i in in_hbm:
            taken[i] = HBM
            operands[i] = pltpu.with_memory_space_constraint(operand, pltpu.HBM)
        elif operand.size >= KEPT:
            operands[i] = pltpu.with_memory_space_constraint(operand, pltpu.VMEM)
    shapes = [pltpu.VMEM(x.shape, x.dtype) if kept and x.size >= KEPT else x for x in shapes]
    given = len(operands)
    operands += [pltpu.with_memory_space_constraint(x, pltpu.VMEM) for x in beside]

    def without(*refs):
        kernel(*refs[:given], *refs[len(operands) :])

    return pl.pallas_call(
        without,
        out_shape=shapes if isinstance(out_shape, list) else shapes[0],
        in_specs=taken + [VMEM] * len(beside),
        out_specs=specs if isinstance(out_shape, list) else specs[0],
        scratch_shapes=list(scratch),
        compiler_params=pltpu.CompilerParams(vmem_limit_bytes=16 * 2**20),
    )(*operands)


def exchange(value, mask, nodes):
    return lax.ppermute(value, "node", [(i, i ^ mask) for i in range(nodes)])


def high_exchange(value, nodes):
    return [value] + [exchange(value, high * LOW, nodes) for high in range(1, nodes // LOW)]


def low_exchange(values, nodes):
    return [values[0]] + [exchange(values[j], j, nodes) for j in range(1, LOW)]


def per_device(node_tensors, prim_ops, active, top_field, node_map):
    nodes = lax.axis_size("node")
    groups = lax.axis_size("term")
    depths = nodes.bit_length() - 1
    turned_active = jnp.swapaxes(active, 1, 2)

    extent = node_tensors.shape[1]
    terms = prim_ops.shape[1]
    pairs = terms * extent // LANES
    flat = jax.ShapeDtypeStruct((extent, extent * extent), jnp.bfloat16)
    mats = jax.ShapeDtypeStruct((pairs * extent, LANES), jnp.bfloat16)
    two = jax.ShapeDtypeStruct((2,) + mats.shape, jnp.bfloat16)
    message = jax.ShapeDtypeStruct((-(-pairs // 2) * (extent + PAD), LANES), jnp.bfloat16)
    messages = jax.ShapeDtypeStruct((2,) + message.shape, jnp.bfloat16)
    table_shape = jax.ShapeDtypeStruct((TABLE, LANES), jnp.int32)
    spread = jax.ShapeDtypeStruct((terms, extent * extent * extent // LANES, LANES), jnp.bfloat16)
    part = jax.ShapeDtypeStruct((LANES // extent, extent // groups, extent * extent), jnp.bfloat16)
    space = pltpu.VMEM((LANES // extent,) + spread.shape[1:], jnp.float32)
    both = [pltpu.VMEM((2,) + spread.shape, jnp.bfloat16)]
    mixed_space = pltpu.VMEM(spread.shape, jnp.bfloat16)
    turn_space = pltpu.VMEM(spread.shape[1:], jnp.float32)

    def others(value):
        return [
            lax.ppermute(value, "term", [(i, (i + shift) % groups) for i in range(groups)]) for shift in range(1, groups)
        ]

    def weigh_beside(count, values):
        for sides, pair in to_weigh[len(weighed) : len(weighed) + count]:
            weighed.append(call(functools.partial(weigh_kernel, pair), part, bac, sides, table, scratch=[space]))
        return lax.optimization_barrier((values, weighed[-count:]))

    def with_top(first, second):
        def branch(mask):
            return lambda first, second: (exchange(first, nodes // 2, nodes), exchange(second, mask, nodes))

        return lax.switch(apart[0], [branch(mask) for mask in range(1, nodes)], first, second)

    abc, bac, cba, left, right, field, mine, table = call(
        start_kernel,
        [flat, flat, flat, mats, mats, mats, message, table_shape],
        node_tensors,
        prim_ops,
        turned_active,
        top_field,
        node_map,
        scratch=[
            pltpu.VMEM(prim_ops.shape, jnp.bfloat16),
            pltpu.SMEM(turned_active.shape, jnp.int32),
            pltpu.VMEM(top_field.shape, jnp.bfloat16),
            pltpu.SMEM(node_map.shape, jnp.int32),
            mixed_space,
            turn_space,
            pltpu.SMEM((nodes,), jnp.int32),
            pltpu.SemaphoreType.DMA((5,)),
        ],
        in_hbm=(0, 1, 2, 3, 4),
    )
    for depth in range(depths - 2, 0, -1):
        parts = high_exchange(mine, nodes)
        came = low_exchange(call(relay_up_kernel, [messages] * LOW, *parts, table), nodes)
        if depth == depths - 2:
            turned, apart = call(
                turn_kernel,
                [jax.ShapeDtypeStruct((2,) + flat.shape, flat.dtype), jax.ShapeDtypeStruct((1,), jnp.int32)],
                bac,
                cba,
                table,
                scratch=[turn_space],
                smem_out=(1,),
            )
            came, turned, apart = lax.optimization_barrier((came, turned, apart))
        left, right, mine = call(
            functools.partial(up_kernel, depth),
            [mats, mats, message],
            *came,
            bac,
            cba,
            left,
            right,
            table,
            scratch=[mixed_space],
        )

    came_left, came_right = with_top(mine, mine)
    landing = both + [pltpu.VMEM(message.shape, jnp.bfloat16)] * 2 + [pltpu.SemaphoreType.DMA((2,))]
    sides, fields = call(
        top_kernel,
        [two, messages],
        came_left,
        came_right,
        abc,
        bac,
        turned,
        field,
        left,
        right,
        table,
        scratch=landing,
        in_hbm=(0, 1),
    )
    came_left, came_right = with_top(fields[0], fields[1])
    to_weigh = [(each, pair) for each in [sides] + others(sides) for pair in range(pairs)]
    share = -(-len(to_weigh) // (2 * (depths - 2)))
    field, fields = call(
        below_top_kernel,
        [mats, messages],
        came_left,
        came_right,
        abc,
        bac,
        turned,
        field,
        sides,
        table,
        scratch=both,
    )
    weighed = []
    for depth in range(2, depths):
        parts = high_exchange(fields, nodes)
        parts, weighed[-share:] = weigh_beside(share, parts)
        came = low_exchange(call(relay_down_kernel, [message] * LOW, *parts, table), nodes)
        came, weighed[-share:] = weigh_beside(share, came)
        if depth < depths - 1:
            field, fields = call(
                functools.partial(down_kernel, depth),
                [mats, messages],
                *came,
                abc,
                bac,
                turned,
                field,
                sides,
                table,
                scratch=both,
            )
    field = call(functools.partial(last_kernel, depths - 1, pairs), mats, *came, field, table)
    out = jax.ShapeDtypeStruct((1, extent // groups, extent * extent), jnp.bfloat16)
    tall_part = jax.ShapeDtypeStruct((extent * extent * extent // groups // WIDE, WIDE), jnp.bfloat16)
    fields = others(field)
    own = call(part_kernel, tall_part, field, *weighed[:pairs], kept=False)
    own, fields = lax.optimization_barrier((own, fields))
    rest = weighed[pairs:]
    return call(functools.partial(finish_kernel, groups), out, own, *fields, *rest, table, kept=False)


def solution(mesh):
    placed = (
        P("node", None, None),
        P("node", "term", None, None, None),
        P("node", "term", None),
        P("term", None, None),
        P(),
    )
    return jax.shard_map(
        per_device, mesh=mesh, in_specs=placed, out_specs=P("node", "term", None), check_vma=False
    )
```

profile of v0, /device:TPU:0, one launch (start us, length us, event | category | flops | bytes accessed | tf_op | source)
XLA Modules:
  0.0 92.3 jit_solution(9626490264800891673)
XLA Ops:
  0.0 4.3 %shard_map.55 = (bf16[64,4096]{1,0:T(8,128)(2,1)S(1)}, bf16[64,4096]{1,0:T(8,128)(2,1)S(1)}, bf16[64,4096]{1,0:T(8,128)(2,1)S(1)}, bf16[128,128]{1,0:T(8,128)(2,...) custom-call(bf16[1,64,4096]{2,1,0:T(8,128)(2,1)} %refs_0_.1, ...), custom_call_target="tpu_custom_call" | custom-call | tf_op jit(solution)/shard_map/pallas_call | solution.py:521
  4.3 3.1 %collective-permute-start.59 = (bf16[80,128]{1,0:T(8,128)(2,1)S(1)}, bf16[80,128]{1,0:T(8,128)(2,1)S(1)}, u32[]{:S(2)}, u32[]{:S(2)}) collective-permute-start(bf16[80,128]{1,0:T(8,128)(2,1)S(1)} %get-tuple-element.180.refs_0_), channel_id=1, source_target_pairs={{0,8},{2,10},{4,12},{6,14},{8,0},{10,2},{12,4},{14,6},{16,24},{18,... | collective-permute-start | bytes 61448 | tf_op jit(solution)/shard_map/ppermute | solution.py:532
  7.4 2.6 %collective-permute-start.60 = (bf16[80,128]{1,0:T(8,128)(2,1)S(1)}, bf16[80,128]{1,0:T(8,128)(2,1)S(1)}, u32[]{:S(2)}, u32[]{:S(2)}) collective-permute-start(bf16[80,128]{1,0:T(8,128)(2,1)S(1)} %get-tuple-element.180.refs_0_), channel_id=1, source_target_pairs={{0,16},{2,18},{4,20},{6,22},{8,24},{10,26},{12,28},{14,30},{16,0},... | collective-permute-start | bytes 61448 | tf_op jit(solution)/shard_map/ppermute | solution.py:532
  10.0 2.3 %collective-permute-done.60.refs_2_ = bf16[80,128]{1,0:T(8,128)(2,1)S(1)} collective-permute-done((bf16[80,128]{1,0:T(8,128)(2,1)S(1)}, bf16[80,128]{1,0:T(8,128)(2,1)S(1)}, u32[]{:S(2)}, u32[]{:S(2)}) %collective-permute-start.60) | collective-permute-done | bytes 20512 | tf_op jit(solution)/shard_map/ppermute | solution.py:532
  12.3 3.3 %collective-permute-done.61.refs_3_ = bf16[80,128]{1,0:T(8,128)(2,1)S(1)} collective-permute-done((bf16[80,128]{1,0:T(8,128)(2,1)S(1)}, bf16[80,128]{1,0:T(8,128)(2,1)S(1)}, u32[]{:S(2)}, u32[]{:S(2)}) %collective-permute-start.61) | collective-permute-done | bytes 20512 | tf_op jit(solution)/shard_map/ppermute | solution.py:532
  17.6 2.3 %shard_map.57 = (bf16[2,64,4096]{2,1,0:T(8,128)(2,1)S(1)}, s32[1]{0:T(128)}) custom-call(bf16[64,4096]{1,0:T(8,128)(2,1)S(1)} %get-tuple-element.186.refs_0_.refs_4_.refs_3_.refs_5_, bf16[64,4096]{1,0:T(8,128)(2,1)S(1)} %get-tuple-element.187.refs_1_.refs_5_, s32[24,128]{1,0:T(8,128)S(1)} %get-tuple-element.181.refs_4_.refs_2_.refs_8_.refs_7_.refs_9_.refs_5_), custom_call_target="tpu_custom_call" | custom-call | tf_op jit(solution)/shard_map/pallas_call | solution.py:521
  20.8 2.2 %shard_map.58 = (bf16[128,128]{1,0:T(8,128)(2,1)S(1)}, bf16[128,128]{1,0:T(8,128)(2,1)S(1)}, bf16[80,128]{1,0:T(8,128)(2,1)S(1)}) custom-call(bf16[2,80,128]{2,1,0:T(8,128)(2,1)S(1)} %get-tuple-element.191.refs_0_, bf16[2,80,128]{2,1,0:T(8,128)(2,1)S(1)} %collective-permute-done.62.refs_1_, bf16[2,80,128]{2,1,0:T(8,128)(2,1)S(1)} %collective-permute-done.63.refs_2_, ...), custom_call_target="tpu_custom_call" | custom-call | tf_op jit(solution)/shard_map/pallas_call | solution.py:521
  23.8 3.6 %collective-permute-start.67 = (bf16[80,128]{1,0:T(8,128)(2,1)S(1)}, bf16[80,128]{1,0:T(8,128)(2,1)S(1)}, u32[]{:S(2)}, u32[]{:S(2)}) collective-permute-start(bf16[80,128]{1,0:T(8,128)(2,1)S(1)} %get-tuple-element.197.refs_0_), channel_id=1, source_target_pairs={{0,24},{2,26},{4,28},{6,30},{8,16},{10,18},{12,20},{14,22},{16,8},... | collective-permute-start | bytes 61448 | tf_op jit(solution)/shard_map/ppermute | solution.py:532
  34.3 2.2 %shard_map.60 = (bf16[128,128]{1,0:T(8,128)(2,1)S(1)}, bf16[128,128]{1,0:T(8,128)(2,1)S(1)}, bf16[80,128]{1,0:T(8,128)(2,1)S(1)}) custom-call(bf16[2,80,128]{2,1,0:T(8,128)(2,1)S(1)} %get-tuple-element.198.refs_0_, bf16[2,80,128]{2,1,0:T(8,128)(2,1)S(1)} %collective-permute-done.68.refs_1_, bf16[2,80,128]{2,1,0:T(8,128)(2,1)S(1)} %collective-permute-done.69.refs_2_, ...), custom_call_target="tpu_custom_call" | custom-call | tf_op jit(solution)/shard_map/pallas_call | solution.py:521
  36.5 5.1 %conditional.2 = (bf16[80,128]{1,0:T(8,128)(2,1)}, bf16[80,128]{1,0:T(8,128)(2,1)}) conditional(s32[]{:T(128)} %bitcast.1, bf16[80,128]{1,0:T(8,128)(2,1)S(1)} %get-tuple-element.204, bf16[80,128]{1,0:T(8,128)(2,1)S(1)} %get-tuple-element.204, bf16[80,128]{1,0:T(8,128)(2,1)S(1)} %get-tuple-element.204, ...), branch_computations={%region_0.0_spmd, %region_1.0_spmd, %region_2.0_spmd, %region_3.0_... | conditional | bytes 163936 | solution.py:579
  37.9 3.7 %collective-permute-done.2 = bf16[80,128]{1,0:T(8,128)(2,1)} collective-permute-done((bf16[80,128]{1,0:T(8,128)(2,1)S(1)}, bf16[80,128]{1,0:T(8,128)(2,1)}, u32[]{:S(2)}, u32[]{:S(2)}) %collective-permute-start.2) | collective-permute-done | bytes 20512 | tf_op jit(solution)/shard_map/cond/branch_1_fun/ppermute | solution.py:532
  41.6 4.3 %shard_map.61 = (bf16[2,128,128]{2,1,0:T(8,128)(2,1)S(1)}, bf16[2,80,128]{2,1,0:T(8,128)(2,1)S(1)}) custom-call(bf16[80,128]{1,0:T(8,128)(2,1)} %get-tuple-element.205.refs_0_, bf16[80,128]{1,0:T(8,128)(2,1)} %get-tuple-element.206.refs_1_, bf16[64,4096]{1,0:T(8,128)(2,1)S(1)} %get-tuple-element.207.refs_2_.refs_4_, ...), custom_call_target="tpu_custom_call" | custom-call | tf_op jit(solution)/shard_map/pallas_call | solution.py:521
  45.9 5.8 %conditional.3 = (bf16[80,128]{1,0:T(8,128)(2,1)}, bf16[80,128]{1,0:T(8,128)(2,1)}) conditional(s32[]{:T(128)} %bitcast.1, (bf16[80,128]{1,0:T(8,128)(2,1)S(1)}, bf16[80,128]{1,0:T(8,128)(2,1)S(1)}) %tuple.132, (bf16[80,128]{1,0:T(8,128)(2,1)S(1)}, bf16[80,128]{1,0:T(8,128)(2,1)S(1)}) %tuple.132, ...), branch_computations={%region_15.0_spmd, %region_16.0_spmd, %region_17.0_spmd, %region_1... | conditional | bytes 163936 | solution.py:579
  48.7 2.1 %collective-permute-done.31 = bf16[80,128]{1,0:T(8,128)(2,1)} collective-permute-done((bf16[80,128]{1,0:T(8,128)(2,1)S(1)}, bf16[80,128]{1,0:T(8,128)(2,1)}, u32[]{:S(2)}, u32[]{:S(2)}) %collective-permute-start.31) | collective-permute-done | bytes 20512 | tf_op jit(solution)/shard_map/cond/branch_1_fun/ppermute | solution.py:532
  51.7 4.4 %shard_map.62 = (bf16[128,128]{1,0:T(8,128)(2,1)S(1)}, bf16[2,80,128]{2,1,0:T(8,128)(2,1)S(1)}) custom-call(bf16[80,128]{1,0:T(8,128)(2,1)} %get-tuple-element.213.refs_0_, bf16[80,128]{1,0:T(8,128)(2,1)} %get-tuple-element.214.refs_1_, bf16[64,4096]{1,0:T(8,128)(2,1)S(1)} %get-tuple-element.207.refs_2_.refs_4_, ...), custom_call_target="tpu_custom_call" | custom-call | tf_op jit(solution)/shard_map/pallas_call | solution.py:521
  56.1 2.2 %collective-permute-start.71 = (bf16[2,80,128]{2,1,0:T(8,128)(2,1)S(1)}, bf16[2,80,128]{2,1,0:T(8,128)(2,1)S(1)}, u32[]{:S(2)}, u32[]{:S(2)}) collective-permute-start(bf16[2,80,128]{2,1,0:T(8,128)(2,1)S(1)} %get-tuple-element.217.refs_0_), channel_id=1, source_target_pairs={{0,8},{2,10},{4,12},{6,14},{8,0},{10,2},{12,4},{14,6},{16,24},{18,... | collective-permute-start | bytes 122888 | tf_op jit(solution)/shard_map/ppermute | solution.py:532
  58.3 2.0 %collective-permute-start.72 = (bf16[2,80,128]{2,1,0:T(8,128)(2,1)S(1)}, bf16[2,80,128]{2,1,0:T(8,128)(2,1)S(1)}, u32[]{:S(2)}, u32[]{:S(2)}) collective-permute-start(bf16[2,80,128]{2,1,0:T(8,128)(2,1)S(1)} %get-tuple-element.217.refs_0_), channel_id=1, source_target_pairs={{0,16},{2,18},{4,20},{6,22},{8,24},{10,26},{12,28},{14,30},{16,0},... | collective-permute-start | bytes 122888 | tf_op jit(solution)/shard_map/ppermute | solution.py:532
  62.3 2.0 %shard_map.63.refs_1_ = bf16[2,32,4096]{2,1,0:T(8,128)(2,1)S(1)} custom-call(bf16[64,4096]{1,0:T(8,128)(2,1)S(1)} %get-tuple-element.186.refs_0_.refs_4_.refs_3_.refs_5_, bf16[2,128,128]{2,1,0:T(8,128)(2,1)S(1)} %get-tuple-element.215.refs_6_.refs_1_.refs_8_, s32[24,128]{1,0:T(8,128)S(1)} %get-tuple-element.181.refs_4_.refs_2_.refs_8_.refs_7_.refs_9_.refs_5_), custom_call_target="tpu_custom_call" | custom-call | tf_op jit(solution)/shard_map/pallas_call | solution.py:521
  70.5 3.7 %shard_map.66 = (bf16[128,128]{1,0:T(8,128)(2,1)S(1)}, bf16[2,80,128]{2,1,0:T(8,128)(2,1)S(1)}) custom-call(bf16[80,128]{1,0:T(8,128)(2,1)S(1)} %get-tuple-element.225.refs_0_, bf16[80,128]{1,0:T(8,128)(2,1)S(1)} %collective-permute-done.74.refs_1_, bf16[80,128]{1,0:T(8,128)(2,1)S(1)} %collective-permute-done.75.refs_2_, ...), custom_call_target="tpu_custom_call" | custom-call | tf_op jit(solution)/shard_map/pallas_call | solution.py:521
  74.3 2.1 %collective-permute-start.78 = (bf16[2,80,128]{2,1,0:T(8,128)(2,1)S(1)}, bf16[2,80,128]{2,1,0:T(8,128)(2,1)S(1)}, u32[]{:S(2)}, u32[]{:S(2)}) collective-permute-start(bf16[2,80,128]{2,1,0:T(8,128)(2,1)S(1)} %get-tuple-element.231.refs_0_), channel_id=1, source_target_pairs={{0,16},{2,18},{4,20},{6,22},{8,24},{10,26},{12,28},{14,30},{16,0},... | collective-permute-start | bytes 122888 | tf_op jit(solution)/shard_map/ppermute | solution.py:532
  76.4 2.2 %collective-permute-start.79 = (bf16[2,80,128]{2,1,0:T(8,128)(2,1)S(1)}, bf16[2,80,128]{2,1,0:T(8,128)(2,1)S(1)}, u32[]{:S(2)}, u32[]{:S(2)}) collective-permute-start(bf16[2,80,128]{2,1,0:T(8,128)(2,1)S(1)} %get-tuple-element.231.refs_0_), channel_id=1, source_target_pairs={{0,24},{2,26},{4,28},{6,30},{8,16},{10,18},{12,20},{14,22},{16,8},... | collective-permute-start | bytes 122888 | tf_op jit(solution)/shard_map/ppermute | solution.py:532
  78.6 2.3 %shard_map.67.refs_2_ = bf16[2,32,4096]{2,1,0:T(8,128)(2,1)S(1)} custom-call(bf16[64,4096]{1,0:T(8,128)(2,1)S(1)} %get-tuple-element.186.refs_0_.refs_4_.refs_3_.refs_5_, bf16[2,128,128]{2,1,0:T(8,128)(2,1)S(1)} %collective-permute-done.80.refs_1_, s32[24,128]{1,0:T(8,128)S(1)} %get-tuple-element.181.refs_4_.refs_2_.refs_8_.refs_7_.refs_9_.refs_5_), custom_call_target="tpu_custom_call" | custom-call | tf_op jit(solution)/shard_map/pallas_call | solution.py:521
  84.2 2.0 %shard_map.69.refs_3_ = bf16[2,32,4096]{2,1,0:T(8,128)(2,1)S(1)} custom-call(bf16[64,4096]{1,0:T(8,128)(2,1)S(1)} %get-tuple-element.186.refs_0_.refs_4_.refs_3_.refs_5_, bf16[2,128,128]{2,1,0:T(8,128)(2,1)S(1)} %collective-permute-done.80.refs_1_, s32[24,128]{1,0:T(8,128)S(1)} %get-tuple-element.181.refs_4_.refs_2_.refs_8_.refs_7_.refs_9_.refs_5_), custom_call_target="tpu_custom_call" | custom-call | tf_op jit(solution)/shard_map/pallas_call | solution.py:521
  88.2 2.7 %collective-permute-done.84.refs_1_ = bf16[128,128]{1,0:T(8,128)(2,1)S(1)} collective-permute-done((bf16[128,128]{1,0:T(8,128)(2,1)S(1)}, bf16[128,128]{1,0:T(8,128)(2,1)S(1)}, u32[]{:S(2)}, u32[]{:S(2)}) %collective-permute-start.84) | collective-permute-done | bytes 32800 | tf_op jit(solution)/shard_map/ppermute | solution.py:567
  (57 shorter events, 29.6 us)
Async XLA Ops:
  4.3 5.7 %collective-permute-start.59 = (bf16[80,128]{1,0:T(8,128)(2,1)S(1)}, bf16[80,128]{1,0:T(8,128)(2,1)S(1)}, u32[]{:S(2)}, u32[]{:S(2)}) collective-permute-start(bf16[80,128]{1,0:T(8,128)(2,1)S(1)} %get-tuple-element.180.refs_0_), channel_id=1, source_target_pairs={{0,8},{2,10},{4,12},{6,14},{8,0},{10,2},{12,4},{14,6},{16,24},{18,... | collective-permute-start | bytes 61448 | tf_op jit(solution)/shard_map/ppermute | solution.py:532
  7.4 4.9 %collective-permute-start.60 = (bf16[80,128]{1,0:T(8,128)(2,1)S(1)}, bf16[80,128]{1,0:T(8,128)(2,1)S(1)}, u32[]{:S(2)}, u32[]{:S(2)}) collective-permute-start(bf16[80,128]{1,0:T(8,128)(2,1)S(1)} %get-tuple-element.180.refs_0_), channel_id=1, source_target_pairs={{0,16},{2,18},{4,20},{6,22},{8,24},{10,26},{12,28},{14,30},{16,0},... | collective-permute-start | bytes 61448 | tf_op jit(solution)/shard_map/ppermute | solution.py:532
  10.0 5.6 %collective-permute-start.61 = (bf16[80,128]{1,0:T(8,128)(2,1)S(1)}, bf16[80,128]{1,0:T(8,128)(2,1)S(1)}, u32[]{:S(2)}, u32[]{:S(2)}) collective-permute-start(bf16[80,128]{1,0:T(8,128)(2,1)S(1)} %get-tuple-element.180.refs_0_), channel_id=1, source_target_pairs={{0,24},{2,26},{4,28},{6,30},{8,16},{10,18},{12,20},{14,22},{16,8},... | collective-permute-start | bytes 61448 | tf_op jit(solution)/shard_map/ppermute | solution.py:532
  15.6 4.3 %collective-permute-start.62 = (bf16[2,80,128]{2,1,0:T(8,128)(2,1)S(1)}, bf16[2,80,128]{2,1,0:T(8,128)(2,1)S(1)}, u32[]{:S(2)}, u32[]{:S(2)}) collective-permute-start(bf16[2,80,128]{2,1,0:T(8,128)(2,1)S(1)} %get-tuple-element.183), channel_id=1, source_target_pairs={{0,2},{2,0},{4,6},{6,4},{8,10},{10,8},{12,14},{14,12},{16,18},{18,... | collective-permute-start | bytes 122888 | tf_op jit(solution)/shard_map/ppermute | solution.py:532
  15.7 4.2 %collective-permute-start.63 = (bf16[2,80,128]{2,1,0:T(8,128)(2,1)S(1)}, bf16[2,80,128]{2,1,0:T(8,128)(2,1)S(1)}, u32[]{:S(2)}, u32[]{:S(2)}) collective-permute-start(bf16[2,80,128]{2,1,0:T(8,128)(2,1)S(1)} %get-tuple-element.184), channel_id=1, source_target_pairs={{0,4},{2,6},{4,0},{6,2},{8,12},{10,14},{12,8},{14,10},{16,20},{18,... | collective-permute-start | bytes 122888 | tf_op jit(solution)/shard_map/ppermute | solution.py:532
  23.0 4.5 %collective-permute-start.65 = (bf16[80,128]{1,0:T(8,128)(2,1)S(1)}, bf16[80,128]{1,0:T(8,128)(2,1)S(1)}, u32[]{:S(2)}, u32[]{:S(2)}) collective-permute-start(bf16[80,128]{1,0:T(8,128)(2,1)S(1)} %get-tuple-element.197.refs_0_), channel_id=1, source_target_pairs={{0,8},{2,10},{4,12},{6,14},{8,0},{10,2},{12,4},{14,6},{16,24},{18,... | collective-permute-start | bytes 61448 | tf_op jit(solution)/shard_map/ppermute | solution.py:532
  23.0 4.7 %collective-permute-start.66 = (bf16[80,128]{1,0:T(8,128)(2,1)S(1)}, bf16[80,128]{1,0:T(8,128)(2,1)S(1)}, u32[]{:S(2)}, u32[]{:S(2)}) collective-permute-start(bf16[80,128]{1,0:T(8,128)(2,1)S(1)} %get-tuple-element.197.refs_0_), channel_id=1, source_target_pairs={{0,16},{2,18},{4,20},{6,22},{8,24},{10,26},{12,28},{14,30},{16,0},... | collective-permute-start | bytes 61448 | tf_op jit(solution)/shard_map/ppermute | solution.py:532
  23.8 5.6 %collective-permute-start.67 = (bf16[80,128]{1,0:T(8,128)(2,1)S(1)}, bf16[80,128]{1,0:T(8,128)(2,1)S(1)}, u32[]{:S(2)}, u32[]{:S(2)}) collective-permute-start(bf16[80,128]{1,0:T(8,128)(2,1)S(1)} %get-tuple-element.197.refs_0_), channel_id=1, source_target_pairs={{0,24},{2,26},{4,28},{6,30},{8,16},{10,18},{12,20},{14,22},{16,8},... | collective-permute-start | bytes 61448 | tf_op jit(solution)/shard_map/ppermute | solution.py:532
  29.6 4.2 %collective-permute-start.69 = (bf16[2,80,128]{2,1,0:T(8,128)(2,1)S(1)}, bf16[2,80,128]{2,1,0:T(8,128)(2,1)S(1)}, u32[]{:S(2)}, u32[]{:S(2)}) collective-permute-start(bf16[2,80,128]{2,1,0:T(8,128)(2,1)S(1)} %get-tuple-element.200), channel_id=1, source_target_pairs={{0,4},{2,6},{4,0},{6,2},{8,12},{10,14},{12,8},{14,10},{16,20},{18,... | collective-permute-start | bytes 122888 | tf_op jit(solution)/shard_map/ppermute | solution.py:532
  36.5 5.1 %collective-permute-start.2 = (bf16[80,128]{1,0:T(8,128)(2,1)S(1)}, bf16[80,128]{1,0:T(8,128)(2,1)}, u32[]{:S(2)}, u32[]{:S(2)}) collective-permute-start(bf16[80,128]{1,0:T(8,128)(2,1)S(1)} %param.1), channel_id=1, source_target_pairs={{0,16},{2,18},{4,20},{6,22},{8,24},{10,26},{12,28},{14,30},{16,0},... | collective-permute-start | bytes 61448 | tf_op jit(solution)/shard_map/cond/branch_1_fun/ppermute | solution.py:532
  37.0 4.6 %collective-permute-start.3 = (bf16[80,128]{1,0:T(8,128)(2,1)S(1)}, bf16[80,128]{1,0:T(8,128)(2,1)}, u32[]{:S(2)}, u32[]{:S(2)}) collective-permute-start(bf16[80,128]{1,0:T(8,128)(2,1)S(1)} %param.1), channel_id=1, source_target_pairs={{0,4},{2,6},{4,0},{6,2},{8,12},{10,14},{12,8},{14,10},{16,20},{18,... | collective-permute-start | bytes 61448 | tf_op jit(solution)/shard_map/cond/branch_1_fun/ppermute | solution.py:532
  46.0 4.9 %collective-permute-start.31 = (bf16[80,128]{1,0:T(8,128)(2,1)S(1)}, bf16[80,128]{1,0:T(8,128)(2,1)}, u32[]{:S(2)}, u32[]{:S(2)}) collective-permute-start(bf16[80,128]{1,0:T(8,128)(2,1)S(1)} %get-tuple-element.82), channel_id=1, source_target_pairs={{0,16},{2,18},{4,20},{6,22},{8,24},{10,26},{12,28},{14,30},{16,0},... | collective-permute-start | bytes 61448 | tf_op jit(solution)/shard_map/cond/branch_1_fun/ppermute | solution.py:532
  56.1 8.2 %collective-permute-start.71 = (bf16[2,80,128]{2,1,0:T(8,128)(2,1)S(1)}, bf16[2,80,128]{2,1,0:T(8,128)(2,1)S(1)}, u32[]{:S(2)}, u32[]{:S(2)}) collective-permute-start(bf16[2,80,128]{2,1,0:T(8,128)(2,1)S(1)} %get-tuple-element.217.refs_0_), channel_id=1, source_target_pairs={{0,8},{2,10},{4,12},{6,14},{8,0},{10,2},{12,4},{14,6},{16,24},{18,... | collective-permute-start | bytes 122888 | tf_op jit(solution)/shard_map/ppermute | solution.py:532
  58.3 6.0 %collective-permute-start.72 = (bf16[2,80,128]{2,1,0:T(8,128)(2,1)S(1)}, bf16[2,80,128]{2,1,0:T(8,128)(2,1)S(1)}, u32[]{:S(2)}, u32[]{:S(2)}) collective-permute-start(bf16[2,80,128]{2,1,0:T(8,128)(2,1)S(1)} %get-tuple-element.217.refs_0_), channel_id=1, source_target_pairs={{0,16},{2,18},{4,20},{6,22},{8,24},{10,26},{12,28},{14,30},{16,0},... | collective-permute-start | bytes 122888 | tf_op jit(solution)/shard_map/ppermute | solution.py:532
  60.4 5.8 %collective-permute-start.73 = (bf16[2,80,128]{2,1,0:T(8,128)(2,1)S(1)}, bf16[2,80,128]{2,1,0:T(8,128)(2,1)S(1)}, u32[]{:S(2)}, u32[]{:S(2)}) collective-permute-start(bf16[2,80,128]{2,1,0:T(8,128)(2,1)S(1)} %get-tuple-element.217.refs_0_), channel_id=1, source_target_pairs={{0,24},{2,26},{4,28},{6,30},{8,16},{10,18},{12,20},{14,22},{16,8},... | collective-permute-start | bytes 122888 | tf_op jit(solution)/shard_map/ppermute | solution.py:532
  60.8 17.9 %collective-permute-start.80 = (bf16[2,128,128]{2,1,0:T(8,128)(2,1)S(1)}, bf16[2,128,128]{2,1,0:T(8,128)(2,1)S(1)}, u32[]{:S(2)}, u32[]{:S(2)}) collective-permute-start(bf16[2,128,128]{2,1,0:T(8,128)(2,1)S(1)} %get-tuple-element.215.refs_6_.refs_1_.refs_8_), channel_id=1, source_target_pairs={{0,1},{1,0},{2,3},{3,2},{4,5},{5,4},{6,7},{7,6},{8,9},{9,8},{10,11... | collective-permute-start | bytes 196616 | tf_op jit(solution)/shard_map/ppermute | solution.py:567
  66.3 4.0 %collective-permute-start.74 = (bf16[80,128]{1,0:T(8,128)(2,1)S(1)}, bf16[80,128]{1,0:T(8,128)(2,1)S(1)}, u32[]{:S(2)}, u32[]{:S(2)}) collective-permute-start(bf16[80,128]{1,0:T(8,128)(2,1)S(1)} %get-tuple-element.222), channel_id=1, source_target_pairs={{0,2},{2,0},{4,6},{6,4},{8,10},{10,8},{12,14},{14,12},{16,18},{18,... | collective-permute-start | bytes 61448 | tf_op jit(solution)/shard_map/ppermute | solution.py:532
  66.3 3.9 %collective-permute-start.75 = (bf16[80,128]{1,0:T(8,128)(2,1)S(1)}, bf16[80,128]{1,0:T(8,128)(2,1)S(1)}, u32[]{:S(2)}, u32[]{:S(2)}) collective-permute-start(bf16[80,128]{1,0:T(8,128)(2,1)S(1)} %get-tuple-element.223), channel_id=1, source_target_pairs={{0,4},{2,6},{4,0},{6,2},{8,12},{10,14},{12,8},{14,10},{16,20},{18,... | collective-permute-start | bytes 61448 | tf_op jit(solution)/shard_map/ppermute | solution.py:532
  74.2 6.7 %collective-permute-start.77 = (bf16[2,80,128]{2,1,0:T(8,128)(2,1)S(1)}, bf16[2,80,128]{2,1,0:T(8,128)(2,1)S(1)}, u32[]{:S(2)}, u32[]{:S(2)}) collective-permute-start(bf16[2,80,128]{2,1,0:T(8,128)(2,1)S(1)} %get-tuple-element.231.refs_0_), channel_id=1, source_target_pairs={{0,8},{2,10},{4,12},{6,14},{8,0},{10,2},{12,4},{14,6},{16,24},{18,... | collective-permute-start | bytes 122888 | tf_op jit(solution)/shard_map/ppermute | solution.py:532
  74.3 6.7 %collective-permute-start.78 = (bf16[2,80,128]{2,1,0:T(8,128)(2,1)S(1)}, bf16[2,80,128]{2,1,0:T(8,128)(2,1)S(1)}, u32[]{:S(2)}, u32[]{:S(2)}) collective-permute-start(bf16[2,80,128]{2,1,0:T(8,128)(2,1)S(1)} %get-tuple-element.231.refs_0_), channel_id=1, source_target_pairs={{0,16},{2,18},{4,20},{6,22},{8,24},{10,26},{12,28},{14,30},{16,0},... | collective-permute-start | bytes 122888 | tf_op jit(solution)/shard_map/ppermute | solution.py:532
  76.4 5.8 %collective-permute-start.79 = (bf16[2,80,128]{2,1,0:T(8,128)(2,1)S(1)}, bf16[2,80,128]{2,1,0:T(8,128)(2,1)S(1)}, u32[]{:S(2)}, u32[]{:S(2)}) collective-permute-start(bf16[2,80,128]{2,1,0:T(8,128)(2,1)S(1)} %get-tuple-element.231.refs_0_), channel_id=1, source_target_pairs={{0,24},{2,26},{4,28},{6,30},{8,16},{10,18},{12,20},{14,22},{16,8},... | collective-permute-start | bytes 122888 | tf_op jit(solution)/shard_map/ppermute | solution.py:532
  82.3 4.0 %collective-permute-start.81 = (bf16[80,128]{1,0:T(8,128)(2,1)S(1)}, bf16[80,128]{1,0:T(8,128)(2,1)S(1)}, u32[]{:S(2)}, u32[]{:S(2)}) collective-permute-start(bf16[80,128]{1,0:T(8,128)(2,1)S(1)} %get-tuple-element.236), channel_id=1, source_target_pairs={{0,2},{2,0},{4,6},{6,4},{8,10},{10,8},{12,14},{14,12},{16,18},{18,... | collective-permute-start | bytes 61448 | tf_op jit(solution)/shard_map/ppermute | solution.py:532
  82.4 3.9 %collective-permute-start.82 = (bf16[80,128]{1,0:T(8,128)(2,1)S(1)}, bf16[80,128]{1,0:T(8,128)(2,1)S(1)}, u32[]{:S(2)}, u32[]{:S(2)}) collective-permute-start(bf16[80,128]{1,0:T(8,128)(2,1)S(1)} %get-tuple-element.237), channel_id=1, source_target_pairs={{0,4},{2,6},{4,0},{6,2},{8,12},{10,14},{12,8},{14,10},{16,20},{18,... | collective-permute-start | bytes 61448 | tf_op jit(solution)/shard_map/ppermute | solution.py:532
  87.0 4.0 %collective-permute-start.84 = (bf16[128,128]{1,0:T(8,128)(2,1)S(1)}, bf16[128,128]{1,0:T(8,128)(2,1)S(1)}, u32[]{:S(2)}, u32[]{:S(2)}) collective-permute-start(bf16[128,128]{1,0:T(8,128)(2,1)S(1)} %shard_map.70.refs_0_), channel_id=1, source_target_pairs={{0,1},{1,0},{2,3},{3,2},{4,5},{5,4},{6,7},{7,6},{8,9},{9,8},{10,11... | collective-permute-start | bytes 98312 | tf_op jit(solution)/shard_map/ppermute | solution.py:567
  (6 other events, 20.2 us)
where the time goes:
time: 93 us; the launch traced here: 92.3 us
  Pallas kernels  34.1 us (37%)
  starting transfers between devices  33.2 us (36%)
  waiting for transfers between devices  23.9 us (26%)
    pallas_call x18, Pallas kernels, call(): pl.pallas_call(without, out_shape=shapes if isinstance(out_shape, list) e...  34.1 us
    ppermute x28, starting transfers between devices, exchange(): return lax.ppermute(value, 'node', [(i, i ^ mask) for i in range(nodes)])  31.1 us
    ppermute x28, waiting for transfers between devices, exchange(): return lax.ppermute(value, 'node', [(i, i ^ mask) for i in range(nodes)])  21.2 us
    ppermute x2, waiting for transfers between devices, others(): lax.ppermute(value, 'term', [(i, (i + shift) % groups) for i in range(gro...  2.75 us
    ppermute x2, starting transfers between devices, others(): lax.ppermute(value, 'term', [(i, (i + shift) % groups) for i in range(gro...  2.15 us
  transfers between devices with their start and end apart: 30, of which 15 were waited for; matrix products, arithmetic and copies ran while one was open for 0% of the time, Pallas kernels for 16%

commit v1 on v0

--- a/solution.py
+++ b/solution.py
@@ -318,6 +318,11 @@
     swap(flip(bac_ref[...], extent), turn_ref, turned_ref.at[1], extent)
 
 
+def both_kernel(first_ref, second_ref, out_ref):
+    out_ref[0] = first_ref[...]
+    out_ref[1] = second_ref[...]
+
+
 def relay_up_kernel(*refs):
     parts, table_ref, outs = refs[:-5], refs[-5], refs[-4:]
     for j, out in enumerate(outs):
@@ -347,38 +352,28 @@
     out_ref[...] = contract(apply_lanes(tall(cba_ref), diagonals, extent), mixed_ref, extent)
 
 
-def fetch(came, held, sems):
-    copies = [pltpu.make_async_copy(*pair, sems.at[k]) for k, pair in enumerate(zip(came, held))]
-    for copy in copies:
-        copy.start()
-    return copies
-
-
 def top_kernel(
-    came_left_hbm, came_right_hbm, abc_ref, bac_ref, turned_ref, field_ref, old_left_ref, old_right_ref, table_ref,
-    sides_ref, out_ref, mixed_ref, came_left_ref, came_right_ref, sems,
+    came_ref, abc_ref, bac_ref, turned_ref, field_ref, old_left_ref, old_right_ref, table_ref,
+    sides_ref, out_ref, mixed_ref,
 ):
-    copies = fetch((came_left_hbm, came_right_hbm), (came_left_ref, came_right_ref), sems)
     extent = bac_ref.shape[0]
     now = entry(table_ref, DEPTH) == 0
     diagonals = block_diagonals(split_terms(field_ref[...], extent), extent)
     left_lanes = apply_lanes(tall(abc_ref), diagonals, extent)
-    for copy in copies:
-        copy.wait()
     pairs = old_left_ref.shape[0] // extent
-    sides_ref[0] = either(now, lambda: old_left_ref[...], lambda: unfold(came_left_ref[...], pairs))
-    sides_ref[1] = either(now, lambda: old_right_ref[...], lambda: unfold(came_right_ref[...], pairs))
+    sides_ref[0] = either(now, lambda: old_left_ref[...], lambda: unfold(came_ref[0], pairs))
+    sides_ref[1] = either(now, lambda: old_right_ref[...], lambda: unfold(came_ref[1], pairs))
     mix(turned_ref, sides_ref, mixed_ref)
     out_ref[0] = contract(left_lanes, mixed_ref.at[0], extent)
     out_ref[1] = contract(apply_lanes(tall(bac_ref), diagonals, extent), mixed_ref.at[1], extent)
 
 
 def below_top_kernel(
-    came_left_ref, came_right_ref, abc_ref, bac_ref, turned_ref, old_ref, sides_ref, table_ref,
+    came_ref, abc_ref, bac_ref, turned_ref, old_ref, sides_ref, table_ref,
     field_ref, out_ref, mixed_ref,
 ):
     position = entry(table_ref, POSITION)
-    came = unfold(either(position == 2, *loads([came_left_ref, came_right_ref])), old_ref.shape[0] // abc_ref.shape[0])
+    came = unfold(either(position == 2, *[f for side in range(2) for f in loads([came_ref], side)]), old_ref.shape[0] // abc_ref.shape[0])
     now = jnp.logical_or(position == 1, position == 2)
     field_ref[...] = either(now, lambda: old_ref[...], lambda: came)
     mix(turned_ref, sides_ref, mixed_ref)
@@ -386,10 +381,9 @@
 
 
 def down_kernel(depth, *refs):
-    came, (abc_ref, bac_ref, turned_ref, old_ref, sides_ref, table_ref) = refs[:LOW], refs[LOW : LOW + 6]
-    field_ref, out_ref, mixed_ref = refs[LOW + 6 :]
+    came, (abc_ref, bac_ref, old_ref, mixed_ref, table_ref) = refs[:LOW], refs[LOW : LOW + 5]
+    field_ref, out_ref = refs[LOW + 5 :]
     arrive(depth, old_ref.shape[0] // abc_ref.shape[0], came, old_ref, table_ref, field_ref)
-    mix(turned_ref, sides_ref, mixed_ref)
     spread_down(abc_ref, bac_ref, field_ref, out_ref, mixed_ref)
 
 
@@ -500,7 +494,7 @@
 HBM = pl.BlockSpec(memory_space=pltpu.HBM)
 
 
-def call(kernel, out_shape, *operands, scratch=(), smem_out=(), in_hbm=(), kept=True, beside=()):
+def call(kernel, out_shape, *operands, scratch=(), smem_out=(), in_hbm=(), kept=True, in_vmem=False, beside=()):
     shapes = out_shape if isinstance(out_shape, list) else [out_shape]
     specs = [SMEM if i in smem_out else VMEM for i in range(len(shapes))]
     taken = [VMEM] * len(operands)
@@ -511,7 +505,7 @@
             operands[i] = pltpu.with_memory_space_constraint(operand, pltpu.HBM)
         elif operand.size >= KEPT:
             operands[i] = pltpu.with_memory_space_constraint(operand, pltpu.VMEM)
-    shapes = [pltpu.VMEM(x.shape, x.dtype) if kept and x.size >= KEPT else x for x in shapes]
+    shapes = [pltpu.VMEM(x.shape, x.dtype) if in_vmem or (kept and x.size >= KEPT) else x for x in shapes]
     given = len(operands)
     operands += [pltpu.with_memory_space_constraint(x, pltpu.VMEM) for x in beside]
 
@@ -568,13 +562,19 @@
         ]
 
     def weigh_beside(count, values):
-        for sides, pair in to_weigh[len(weighed) : len(weighed) + count]:
+        first = len(weighed)
+        for sides, pair in to_weigh[first : first + count]:
             weighed.append(call(functools.partial(weigh_kernel, pair), part, bac, sides, table, scratch=[space]))
-        return lax.optimization_barrier((values, weighed[-count:]))
+        values, weighed[first:] = lax.optimization_barrier((values, weighed[first:]))
+        return values
 
     def with_top(first, second):
         def branch(mask):
-            return lambda first, second: (exchange(first, nodes // 2, nodes), exchange(second, mask, nodes))
+            def go(first, second):
+                came = exchange(first, nodes // 2, nodes), exchange(second, mask, nodes)
+                return call(both_kernel, messages, *came, in_vmem=True)
+
+            return go
 
         return lax.switch(apart[0], [branch(mask) for mask in range(1, nodes)], first, second)
 
@@ -624,13 +624,11 @@
             scratch=[mixed_space],
         )
 
-    came_left, came_right = with_top(mine, mine)
-    landing = both + [pltpu.VMEM(message.shape, jnp.bfloat16)] * 2 + [pltpu.SemaphoreType.DMA((2,))]
+    came = pltpu.with_memory_space_constraint(with_top(mine, mine), pltpu.VMEM)
     sides, fields = call(
         top_kernel,
         [two, messages],
-        came_left,
-        came_right,
+        came,
         abc,
         bac,
         turned,
@@ -638,17 +636,15 @@
         left,
         right,
         table,
-        scratch=landing,
-        in_hbm=(0, 1),
+        scratch=both,
     )
-    came_left, came_right = with_top(fields[0], fields[1])
+    came = pltpu.with_memory_space_constraint(with_top(fields[0], fields[1]), pltpu.VMEM)
     to_weigh = [(each, pair) for each in [sides] + others(sides) for pair in range(pairs)]
-    share = -(-len(to_weigh) // (2 * (depths - 2)))
+    share = -(-len(to_weigh) // (1 + 3 * (depths - 3)))
     field, fields = call(
         below_top_kernel,
         [mats, messages],
-        came_left,
-        came_right,
+        came,
         abc,
         bac,
         turned,
@@ -660,9 +656,13 @@
     weighed = []
     for depth in range(2, depths):
         parts = high_exchange(fields, nodes)
-        parts, weighed[-share:] = weigh_beside(share, parts)
+        if depth == 2:
+            ahead = jax.ShapeDtypeStruct((2,) + spread.shape, spread.dtype)
+            parts, mixed = lax.optimization_barrier((parts, call(mix, ahead, turned, sides)))
+        else:
+            parts = weigh_beside(2 * share, parts)
         came = low_exchange(call(relay_down_kernel, [message] * LOW, *parts, table), nodes)
-        came, weighed[-share:] = weigh_beside(share, came)
+        came = weigh_beside(share, came)
         if depth < depths - 1:
             field, fields = call(
                 functools.partial(down_kernel, depth),
@@ -670,11 +670,9 @@
                 *came,
                 abc,
                 bac,
-                turned,
                 field,
-                sides,
+                mixed,
                 table,
-                scratch=both,
             )
     field = call(functools.partial(last_kernel, depths - 1, pairs), mats, *came, field, table)
     out = jax.ShapeDtypeStruct((1, extent // groups, extent * extent), jnp.bfloat16)

time: 93 us -> 90 us (0.968)
  waiting for transfers between devices: 23.9 us -> 19.5 us
  starting transfers between devices: 33.2 us -> 36.3 us
  Pallas kernels: 34.1 us -> 33.1 us
    ppermute x28, waiting for transfers between devices: 21.2 us -> 17.7 us  [exchange(): return lax.ppermute(value, 'node', [(i, i ^ mask) for i in range(nodes)])]
    ppermute x28, starting transfers between devices: 31.1 us -> 33.1 us  [exchange(): return lax.ppermute(value, 'node', [(i, i ^ mask) for i in range(nodes)])]
    pallas_call x18 -> x21, Pallas kernels: 34.1 us -> 33.1 us  [call(): pl.pallas_call(without, out_shape=shapes if isinstance(out_shape, list) e...]
    ppermute x2, starting transfers between devices: 2.15 us -> 3.13 us  [others(): lax.ppermute(value, 'term', [(i, (i + shift) % groups) for i in range(gro...]
    ppermute x2, waiting for transfers between devices: 2.75 us -> 1.78 us  [others(): lax.ppermute(value, 'term', [(i, (i + shift) % groups) for i in range(gro...]
  transfers between devices with their start and end apart: 30 -> 30, of which waited for: 15 -> 15; matrix products, arithmetic and copies ran while one was open for 0% -> 0% of each run, Pallas kernels for 16% -> 17%
where the time goes in v1:
time: 90 us; the launch traced here: 89.9 us
  starting transfers between devices  36.3 us (40%)
  Pallas kernels  33.1 us (37%)
  waiting for transfers between devices  19.5 us (22%)
  between operations  0.94 us (1%)
    ppermute x28, starting transfers between devices, exchange(): return lax.ppermute(value, 'node', [(i, i ^ mask) for i in range(nodes)])  33.1 us
    pallas_call x21, Pallas kernels, call(): pl.pallas_call(without, out_shape=shapes if isinstance(out_shape, list) e...  33.1 us
    ppermute x28, waiting for transfers between devices, exchange(): return lax.ppermute(value, 'node', [(i, i ^ mask) for i in range(nodes)])  17.7 us
    ppermute x2, starting transfers between devices, others(): lax.ppermute(value, 'term', [(i, (i + shift) % groups) for i in range(gro...  3.13 us
  transfers between devices with their start and end apart: 30, of which 15 were waited for; matrix products, arithmetic and copies ran while one was open for 0% of the time, Pallas kernels for 17%

profile of v1, /device:TPU:0, one launch (start us, length us, event | category | flops | bytes accessed | tf_op | source)
XLA Modules:
  0.0 89.9 jit_solution(2152211171767101673)
XLA Ops:
  0.0 4.3 %shard_map.55 = (bf16[64,4096]{1,0:T(8,128)(2,1)S(1)}, bf16[64,4096]{1,0:T(8,128)(2,1)S(1)}, bf16[64,4096]{1,0:T(8,128)(2,1)S(1)}, bf16[128,128]{1,0:T(8,128)(2,...) custom-call(bf16[1,64,4096]{2,1,0:T(8,128)(2,1)} %refs_0_.1, ...), custom_call_target="tpu_custom_call" | custom-call | tf_op jit(solution)/shard_map/pallas_call | solution.py:515
  4.3 3.1 %collective-permute-start.59 = (bf16[80,128]{1,0:T(8,128)(2,1)S(1)}, bf16[80,128]{1,0:T(8,128)(2,1)S(1)}, u32[]{:S(2)}, u32[]{:S(2)}) collective-permute-start(bf16[80,128]{1,0:T(8,128)(2,1)S(1)} %get-tuple-element.209.refs_0_), channel_id=1, source_target_pairs={{0,8},{2,10},{4,12},{6,14},{8,0},{10,2},{12,4},{14,6},{16,24},{18,... | collective-permute-start | bytes 61448 | tf_op jit(solution)/shard_map/ppermute | solution.py:526
  7.4 2.6 %collective-permute-start.60 = (bf16[80,128]{1,0:T(8,128)(2,1)S(1)}, bf16[80,128]{1,0:T(8,128)(2,1)S(1)}, u32[]{:S(2)}, u32[]{:S(2)}) collective-permute-start(bf16[80,128]{1,0:T(8,128)(2,1)S(1)} %get-tuple-element.209.refs_0_), channel_id=1, source_target_pairs={{0,16},{2,18},{4,20},{6,22},{8,24},{10,26},{12,28},{14,30},{16,0},... | collective-permute-start | bytes 61448 | tf_op jit(solution)/shard_map/ppermute | solution.py:526
  10.0 2.3 %collective-permute-done.60.refs_2_ = bf16[80,128]{1,0:T(8,128)(2,1)S(1)} collective-permute-done((bf16[80,128]{1,0:T(8,128)(2,1)S(1)}, bf16[80,128]{1,0:T(8,128)(2,1)S(1)}, u32[]{:S(2)}, u32[]{:S(2)}) %collective-permute-start.60) | collective-permute-done | bytes 20512 | tf_op jit(solution)/shard_map/ppermute | solution.py:526
  12.3 3.3 %collective-permute-done.61.refs_3_ = bf16[80,128]{1,0:T(8,128)(2,1)S(1)} collective-permute-done((bf16[80,128]{1,0:T(8,128)(2,1)S(1)}, bf16[80,128]{1,0:T(8,128)(2,1)S(1)}, u32[]{:S(2)}, u32[]{:S(2)}) %collective-permute-start.61) | collective-permute-done | bytes 20512 | tf_op jit(solution)/shard_map/ppermute | solution.py:526
  17.6 2.3 %shard_map.57 = (bf16[2,64,4096]{2,1,0:T(8,128)(2,1)S(1)}, s32[1]{0:T(128)}) custom-call(bf16[64,4096]{1,0:T(8,128)(2,1)S(1)} %get-tuple-element.215.refs_0_.refs_4_.refs_2_.refs_5_, bf16[64,4096]{1,0:T(8,128)(2,1)S(1)} %get-tuple-element.216.refs_1_.refs_5_, s32[24,128]{1,0:T(8,128)S(1)} %get-tuple-element.210.refs_4_.refs_2_.refs_8_.refs_7_.refs_6_.refs_5_), custom_call_target="tpu_custom_call" | custom-call | tf_op jit(solution)/shard_map/pallas_call | solution.py:515
  20.8 2.2 %shard_map.58 = (bf16[128,128]{1,0:T(8,128)(2,1)S(1)}, bf16[128,128]{1,0:T(8,128)(2,1)S(1)}, bf16[80,128]{1,0:T(8,128)(2,1)S(1)}) custom-call(bf16[2,80,128]{2,1,0:T(8,128)(2,1)S(1)} %get-tuple-element.220.refs_0_, bf16[2,80,128]{2,1,0:T(8,128)(2,1)S(1)} %collective-permute-done.62.refs_1_, bf16[2,80,128]{2,1,0:T(8,128)(2,1)S(1)} %collective-permute-done.63.refs_2_, ...), custom_call_target="tpu_custom_call" | custom-call | tf_op jit(solution)/shard_map/pallas_call | solution.py:515
  23.8 3.6 %collective-permute-start.67 = (bf16[80,128]{1,0:T(8,128)(2,1)S(1)}, bf16[80,128]{1,0:T(8,128)(2,1)S(1)}, u32[]{:S(2)}, u32[]{:S(2)}) collective-permute-start(bf16[80,128]{1,0:T(8,128)(2,1)S(1)} %get-tuple-element.226.refs_0_), channel_id=1, source_target_pairs={{0,24},{2,26},{4,28},{6,30},{8,16},{10,18},{12,20},{14,22},{16,8},... | collective-permute-start | bytes 61448 | tf_op jit(solution)/shard_map/ppermute | solution.py:526
  34.3 2.2 %shard_map.60 = (bf16[128,128]{1,0:T(8,128)(2,1)S(1)}, bf16[128,128]{1,0:T(8,128)(2,1)S(1)}, bf16[80,128]{1,0:T(8,128)(2,1)S(1)}) custom-call(bf16[2,80,128]{2,1,0:T(8,128)(2,1)S(1)} %get-tuple-element.227.refs_0_, bf16[2,80,128]{2,1,0:T(8,128)(2,1)S(1)} %collective-permute-done.68.refs_1_, bf16[2,80,128]{2,1,0:T(8,128)(2,1)S(1)} %collective-permute-done.69.refs_2_, ...), custom_call_target="tpu_custom_call" | custom-call | tf_op jit(solution)/shard_map/pallas_call | solution.py:515
  36.5 5.2 %conditional.2 = (bf16[2,80,128]{2,1,0:T(8,128)(2,1)S(1)}) conditional(s32[]{:T(128)} %bitcast.1, bf16[80,128]{1,0:T(8,128)(2,1)S(1)} %get-tuple-element.233, bf16[80,128]{1,0:T(8,128)(2,1)S(1)} %get-tuple-element.233, bf16[80,128]{1,0:T(8,128)(2,1)S(1)} %get-tuple-element.233, ...), branch_computations={%region_0.0_spmd, %region_1.0_spmd, %region_2.0_spmd, %region_3.0_... | conditional | bytes 163928 | solution.py:579
  37.0 3.2 %collective-permute-start.9 = (bf16[80,128]{1,0:T(8,128)(2,1)S(1)}, bf16[80,128]{1,0:T(8,128)(2,1)S(1)}, u32[]{:S(2)}, u32[]{:S(2)}) collective-permute-start(bf16[80,128]{1,0:T(8,128)(2,1)S(1)} %param.4), channel_id=1, source_target_pairs={{0,10},{2,8},{4,14},{6,12},{8,2},{10,0},{12,6},{14,4},{16,26},{18,... | collective-permute-start | bytes 61448 | tf_op jit(solution)/shard_map/cond/branch_4_fun/ppermute | solution.py:526
  41.7 3.7 %shard_map.61 = (bf16[2,128,128]{2,1,0:T(8,128)(2,1)S(1)}, bf16[2,80,128]{2,1,0:T(8,128)(2,1)S(1)}) custom-call(bf16[2,80,128]{2,1,0:T(8,128)(2,1)S(1)} %get-tuple-element.278.refs_0_, bf16[64,4096]{1,0:T(8,128)(2,1)S(1)} %get-tuple-element.234.refs_1_.refs_4_, bf16[64,4096]{1,0:T(8,128)(2,1)S(1)} %get-tuple-element.215.refs_0_.refs_4_.refs_2_.refs_5_, ...), custom_call_target="tpu_custom_call" | custom-call | tf_op jit(solution)/shard_map/pallas_call | solution.py:515
  45.4 4.9 %conditional.3 = (bf16[2,80,128]{2,1,0:T(8,128)(2,1)S(1)}) conditional(s32[]{:T(128)} %bitcast.1, (bf16[80,128]{1,0:T(8,128)(2,1)S(1)}, bf16[80,128]{1,0:T(8,128)(2,1)S(1)}) %tuple.102, (bf16[80,128]{1,0:T(8,128)(2,1)S(1)}, bf16[80,128]{1,0:T(8,128)(2,1)S(1)}) %tuple.102, (bf16[80,128]{1,0:T(8,128)(2,1)S(1)}, ...), branch_computations={%region_15.0_spmd, %region_16.0_spmd, %region_17.0_spmd, %region_1... | conditional | bytes 163928 | solution.py:579
  47.8 2.5 %collective-permute-done.37.refs_0_ = bf16[80,128]{1,0:T(8,128)(2,1)S(1)} collective-permute-done((bf16[80,128]{1,0:T(8,128)(2,1)S(1)}, bf16[80,128]{1,0:T(8,128)(2,1)S(1)}, u32[]{:S(2)}, u32[]{:S(2)}) %collective-permute-start.37) | collective-permute-done | bytes 20512 | tf_op jit(solution)/shard_map/cond/branch_4_fun/ppermute | solution.py:526
  50.3 3.7 %shard_map.62 = (bf16[128,128]{1,0:T(8,128)(2,1)S(1)}, bf16[2,80,128]{2,1,0:T(8,128)(2,1)S(1)}) custom-call(bf16[2,80,128]{2,1,0:T(8,128)(2,1)S(1)} %get-tuple-element.279.refs_0_, bf16[64,4096]{1,0:T(8,128)(2,1)S(1)} %get-tuple-element.234.refs_1_.refs_4_, bf16[64,4096]{1,0:T(8,128)(2,1)S(1)} %get-tuple-element.215.refs_0_.refs_4_.refs_2_.refs_5_, ...), custom_call_target="tpu_custom_call" | custom-call | tf_op jit(solution)/shard_map/pallas_call | solution.py:515
  54.0 2.4 %collective-permute-start.71 = (bf16[2,80,128]{2,1,0:T(8,128)(2,1)S(1)}, bf16[2,80,128]{2,1,0:T(8,128)(2,1)S(1)}, u32[]{:S(2)}, u32[]{:S(2)}) collective-permute-start(bf16[2,80,128]{2,1,0:T(8,128)(2,1)S(1)} %get-tuple-element.242.refs_0_), channel_id=1, source_target_pairs={{0,8},{2,10},{4,12},{6,14},{8,0},{10,2},{12,4},{14,6},{16,24},{18,... | collective-permute-start | bytes 122888 | tf_op jit(solution)/shard_map/ppermute | solution.py:526
  61.6 2.3 %collective-permute-done.73.refs_3_ = bf16[2,80,128]{2,1,0:T(8,128)(2,1)S(1)} collective-permute-done((bf16[2,80,128]{2,1,0:T(8,128)(2,1)S(1)}, bf16[2,80,128]{2,1,0:T(8,128)(2,1)S(1)}, u32[]{:S(2)}, u32[]{:S(2)}) %collective-permute-start.73) | collective-permute-done | bytes 40992 | tf_op jit(solution)/shard_map/ppermute | solution.py:526
  65.9 2.0 %shard_map.65.refs_1_ = bf16[2,32,4096]{2,1,0:T(8,128)(2,1)S(1)} custom-call(bf16[64,4096]{1,0:T(8,128)(2,1)S(1)} %get-tuple-element.215.refs_0_.refs_4_.refs_2_.refs_5_, bf16[2,128,128]{2,1,0:T(8,128)(2,1)S(1)} %get-tuple-element.240.refs_5_.refs_1_, s32[24,128]{1,0:T(8,128)S(1)} %get-tuple-element.210.refs_4_.refs_2_.refs_8_.refs_7_.refs_6_.refs_5_), custom_call_target="tpu_custom_call" | custom-call | tf_op jit(solution)/shard_map/pallas_call | solution.py:515
  68.3 2.8 %shard_map.66 = (bf16[128,128]{1,0:T(8,128)(2,1)S(1)}, bf16[2,80,128]{2,1,0:T(8,128)(2,1)S(1)}) custom-call(bf16[80,128]{1,0:T(8,128)(2,1)S(1)} %get-tuple-element.250.refs_0_, bf16[80,128]{1,0:T(8,128)(2,1)S(1)} %collective-permute-done.74.refs_1_, bf16[80,128]{1,0:T(8,128)(2,1)S(1)} %collective-permute-done.75.refs_2_, ...), custom_call_target="tpu_custom_call" | custom-call | tf_op jit(solution)/shard_map/pallas_call | solution.py:515
  72.5 3.0 %collective-permute-start.79 = (bf16[2,80,128]{2,1,0:T(8,128)(2,1)S(1)}, bf16[2,80,128]{2,1,0:T(8,128)(2,1)S(1)}, u32[]{:S(2)}, u32[]{:S(2)}) collective-permute-start(bf16[2,80,128]{2,1,0:T(8,128)(2,1)S(1)} %get-tuple-element.257.refs_0_), channel_id=1, source_target_pairs={{0,24},{2,26},{4,28},{6,30},{8,16},{10,18},{12,20},{14,22},{16,8},... | collective-permute-start | bytes 122888 | tf_op jit(solution)/shard_map/ppermute | solution.py:526
  75.5 2.0 %shard_map.67.refs_2_ = bf16[2,32,4096]{2,1,0:T(8,128)(2,1)S(1)} custom-call(bf16[64,4096]{1,0:T(8,128)(2,1)S(1)} %get-tuple-element.215.refs_0_.refs_4_.refs_2_.refs_5_, bf16[2,128,128]{2,1,0:T(8,128)(2,1)S(1)} %get-tuple-element.240.refs_5_.refs_1_, s32[24,128]{1,0:T(8,128)S(1)} %get-tuple-element.210.refs_4_.refs_2_.refs_8_.refs_7_.refs_6_.refs_5_), custom_call_target="tpu_custom_call" | custom-call | tf_op jit(solution)/shard_map/pallas_call | solution.py:515
  77.5 2.3 %shard_map.68.refs_2_ = bf16[2,32,4096]{2,1,0:T(8,128)(2,1)S(1)} custom-call(bf16[64,4096]{1,0:T(8,128)(2,1)S(1)} %get-tuple-element.215.refs_0_.refs_4_.refs_2_.refs_5_, bf16[2,128,128]{2,1,0:T(8,128)(2,1)S(1)} %collective-permute-done.80.refs_1_, s32[24,128]{1,0:T(8,128)S(1)} %get-tuple-element.210.refs_4_.refs_2_.refs_8_.refs_7_.refs_6_.refs_5_), custom_call_target="tpu_custom_call" | custom-call | tf_op jit(solution)/shard_map/pallas_call | solution.py:515
  81.9 2.0 %shard_map.70.refs_3_ = bf16[2,32,4096]{2,1,0:T(8,128)(2,1)S(1)} custom-call(bf16[64,4096]{1,0:T(8,128)(2,1)S(1)} %get-tuple-element.215.refs_0_.refs_4_.refs_2_.refs_5_, bf16[2,128,128]{2,1,0:T(8,128)(2,1)S(1)} %collective-permute-done.80.refs_1_, s32[24,128]{1,0:T(8,128)S(1)} %get-tuple-element.210.refs_4_.refs_2_.refs_8_.refs_7_.refs_6_.refs_5_), custom_call_target="tpu_custom_call" | custom-call | tf_op jit(solution)/shard_map/pallas_call | solution.py:515
  86.8 1.8 %collective-permute-done.84.refs_1_ = bf16[128,128]{1,0:T(8,128)(2,1)S(1)} collective-permute-done((bf16[128,128]{1,0:T(8,128)(2,1)S(1)}, bf16[128,128]{1,0:T(8,128)(2,1)S(1)}, u32[]{:S(2)}, u32[]{:S(2)}) %collective-permute-start.84) | collective-permute-done | bytes 32800 | tf_op jit(solution)/shard_map/ppermute | solution.py:561
  (60 shorter events, 29.5 us)
Async XLA Ops:
  4.3 5.7 %collective-permute-start.59 = (bf16[80,128]{1,0:T(8,128)(2,1)S(1)}, bf16[80,128]{1,0:T(8,128)(2,1)S(1)}, u32[]{:S(2)}, u32[]{:S(2)}) collective-permute-start(bf16[80,128]{1,0:T(8,128)(2,1)S(1)} %get-tuple-element.209.refs_0_), channel_id=1, source_target_pairs={{0,8},{2,10},{4,12},{6,14},{8,0},{10,2},{12,4},{14,6},{16,24},{18,... | collective-permute-start | bytes 61448 | tf_op jit(solution)/shard_map/ppermute | solution.py:526
  7.4 4.9 %collective-permute-start.60 = (bf16[80,128]{1,0:T(8,128)(2,1)S(1)}, bf16[80,128]{1,0:T(8,128)(2,1)S(1)}, u32[]{:S(2)}, u32[]{:S(2)}) collective-permute-start(bf16[80,128]{1,0:T(8,128)(2,1)S(1)} %get-tuple-element.209.refs_0_), channel_id=1, source_target_pairs={{0,16},{2,18},{4,20},{6,22},{8,24},{10,26},{12,28},{14,30},{16,0},... | collective-permute-start | bytes 61448 | tf_op jit(solution)/shard_map/ppermute | solution.py:526
  10.0 5.6 %collective-permute-start.61 = (bf16[80,128]{1,0:T(8,128)(2,1)S(1)}, bf16[80,128]{1,0:T(8,128)(2,1)S(1)}, u32[]{:S(2)}, u32[]{:S(2)}) collective-permute-start(bf16[80,128]{1,0:T(8,128)(2,1)S(1)} %get-tuple-element.209.refs_0_), channel_id=1, source_target_pairs={{0,24},{2,26},{4,28},{6,30},{8,16},{10,18},{12,20},{14,22},{16,8},... | collective-permute-start | bytes 61448 | tf_op jit(solution)/shard_map/ppermute | solution.py:526
  15.6 4.3 %collective-permute-start.62 = (bf16[2,80,128]{2,1,0:T(8,128)(2,1)S(1)}, bf16[2,80,128]{2,1,0:T(8,128)(2,1)S(1)}, u32[]{:S(2)}, u32[]{:S(2)}) collective-permute-start(bf16[2,80,128]{2,1,0:T(8,128)(2,1)S(1)} %get-tuple-element.212), channel_id=1, source_target_pairs={{0,2},{2,0},{4,6},{6,4},{8,10},{10,8},{12,14},{14,12},{16,18},{18,... | collective-permute-start | bytes 122888 | tf_op jit(solution)/shard_map/ppermute | solution.py:526
  15.7 4.2 %collective-permute-start.63 = (bf16[2,80,128]{2,1,0:T(8,128)(2,1)S(1)}, bf16[2,80,128]{2,1,0:T(8,128)(2,1)S(1)}, u32[]{:S(2)}, u32[]{:S(2)}) collective-permute-start(bf16[2,80,128]{2,1,0:T(8,128)(2,1)S(1)} %get-tuple-element.213), channel_id=1, source_target_pairs={{0,4},{2,6},{4,0},{6,2},{8,12},{10,14},{12,8},{14,10},{16,20},{18,... | collective-permute-start | bytes 122888 | tf_op jit(solution)/shard_map/ppermute | solution.py:526
  23.0 4.5 %collective-permute-start.65 = (bf16[80,128]{1,0:T(8,128)(2,1)S(1)}, bf16[80,128]{1,0:T(8,128)(2,1)S(1)}, u32[]{:S(2)}, u32[]{:S(2)}) collective-permute-start(bf16[80,128]{1,0:T(8,128)(2,1)S(1)} %get-tuple-element.226.refs_0_), channel_id=1, source_target_pairs={{0,8},{2,10},{4,12},{6,14},{8,0},{10,2},{12,4},{14,6},{16,24},{18,... | collective-permute-start | bytes 61448 | tf_op jit(solution)/shard_map/ppermute | solution.py:526
  23.0 4.7 %collective-permute-start.66 = (bf16[80,128]{1,0:T(8,128)(2,1)S(1)}, bf16[80,128]{1,0:T(8,128)(2,1)S(1)}, u32[]{:S(2)}, u32[]{:S(2)}) collective-permute-start(bf16[80,128]{1,0:T(8,128)(2,1)S(1)} %get-tuple-element.226.refs_0_), channel_id=1, source_target_pairs={{0,16},{2,18},{4,20},{6,22},{8,24},{10,26},{12,28},{14,30},{16,0},... | collective-permute-start | bytes 61448 | tf_op jit(solution)/shard_map/ppermute | solution.py:526
  23.8 5.6 %collective-permute-start.67 = (bf16[80,128]{1,0:T(8,128)(2,1)S(1)}, bf16[80,128]{1,0:T(8,128)(2,1)S(1)}, u32[]{:S(2)}, u32[]{:S(2)}) collective-permute-start(bf16[80,128]{1,0:T(8,128)(2,1)S(1)} %get-tuple-element.226.refs_0_), channel_id=1, source_target_pairs={{0,24},{2,26},{4,28},{6,30},{8,16},{10,18},{12,20},{14,22},{16,8},... | collective-permute-start | bytes 61448 | tf_op jit(solution)/shard_map/ppermute | solution.py:526
  29.6 4.2 %collective-permute-start.69 = (bf16[2,80,128]{2,1,0:T(8,128)(2,1)S(1)}, bf16[2,80,128]{2,1,0:T(8,128)(2,1)S(1)}, u32[]{:S(2)}, u32[]{:S(2)}) collective-permute-start(bf16[2,80,128]{2,1,0:T(8,128)(2,1)S(1)} %get-tuple-element.229), channel_id=1, source_target_pairs={{0,4},{2,6},{4,0},{6,2},{8,12},{10,14},{12,8},{14,10},{16,20},{18,... | collective-permute-start | bytes 122888 | tf_op jit(solution)/shard_map/ppermute | solution.py:526
  36.5 5.1 %collective-permute-start.8 = (bf16[80,128]{1,0:T(8,128)(2,1)S(1)}, bf16[80,128]{1,0:T(8,128)(2,1)S(1)}, u32[]{:S(2)}, u32[]{:S(2)}) collective-permute-start(bf16[80,128]{1,0:T(8,128)(2,1)S(1)} %param.4), channel_id=1, source_target_pairs={{0,16},{2,18},{4,20},{6,22},{8,24},{10,26},{12,28},{14,30},{16,0},... | collective-permute-start | bytes 61448 | tf_op jit(solution)/shard_map/cond/branch_4_fun/ppermute | solution.py:526
  37.0 4.7 %collective-permute-start.9 = (bf16[80,128]{1,0:T(8,128)(2,1)S(1)}, bf16[80,128]{1,0:T(8,128)(2,1)S(1)}, u32[]{:S(2)}, u32[]{:S(2)}) collective-permute-start(bf16[80,128]{1,0:T(8,128)(2,1)S(1)} %param.4), channel_id=1, source_target_pairs={{0,10},{2,8},{4,14},{6,12},{8,2},{10,0},{12,6},{14,4},{16,26},{18,... | collective-permute-start | bytes 61448 | tf_op jit(solution)/shard_map/cond/branch_4_fun/ppermute | solution.py:526
  45.4 4.8 %collective-permute-start.37 = (bf16[80,128]{1,0:T(8,128)(2,1)S(1)}, bf16[80,128]{1,0:T(8,128)(2,1)S(1)}, u32[]{:S(2)}, u32[]{:S(2)}) collective-permute-start(bf16[80,128]{1,0:T(8,128)(2,1)S(1)} %get-tuple-element.115), channel_id=1, source_target_pairs={{0,16},{2,18},{4,20},{6,22},{8,24},{10,26},{12,28},{14,30},{16,0},... | collective-permute-start | bytes 61448 | tf_op jit(solution)/shard_map/cond/branch_4_fun/ppermute | solution.py:526
  54.0 7.7 %collective-permute-start.71 = (bf16[2,80,128]{2,1,0:T(8,128)(2,1)S(1)}, bf16[2,80,128]{2,1,0:T(8,128)(2,1)S(1)}, u32[]{:S(2)}, u32[]{:S(2)}) collective-permute-start(bf16[2,80,128]{2,1,0:T(8,128)(2,1)S(1)} %get-tuple-element.242.refs_0_), channel_id=1, source_target_pairs={{0,8},{2,10},{4,12},{6,14},{8,0},{10,2},{12,4},{14,6},{16,24},{18,... | collective-permute-start | bytes 122888 | tf_op jit(solution)/shard_map/ppermute | solution.py:526
  56.4 5.2 %collective-permute-start.72 = (bf16[2,80,128]{2,1,0:T(8,128)(2,1)S(1)}, bf16[2,80,128]{2,1,0:T(8,128)(2,1)S(1)}, u32[]{:S(2)}, u32[]{:S(2)}) collective-permute-start(bf16[2,80,128]{2,1,0:T(8,128)(2,1)S(1)} %get-tuple-element.242.refs_0_), channel_id=1, source_target_pairs={{0,16},{2,18},{4,20},{6,22},{8,24},{10,26},{12,28},{14,30},{16,0},... | collective-permute-start | bytes 122888 | tf_op jit(solution)/shard_map/ppermute | solution.py:526
  58.1 5.8 %collective-permute-start.73 = (bf16[2,80,128]{2,1,0:T(8,128)(2,1)S(1)}, bf16[2,80,128]{2,1,0:T(8,128)(2,1)S(1)}, u32[]{:S(2)}, u32[]{:S(2)}) collective-permute-start(bf16[2,80,128]{2,1,0:T(8,128)(2,1)S(1)} %get-tuple-element.242.refs_0_), channel_id=1, source_target_pairs={{0,24},{2,26},{4,28},{6,30},{8,16},{10,18},{12,20},{14,22},{16,8},... | collective-permute-start | bytes 122888 | tf_op jit(solution)/shard_map/ppermute | solution.py:526
  58.8 18.7 %collective-permute-start.80 = (bf16[2,128,128]{2,1,0:T(8,128)(2,1)S(1)}, bf16[2,128,128]{2,1,0:T(8,128)(2,1)S(1)}, u32[]{:S(2)}, u32[]{:S(2)}) collective-permute-start(bf16[2,128,128]{2,1,0:T(8,128)(2,1)S(1)} %get-tuple-element.240.refs_5_.refs_1_), channel_id=1, source_target_pairs={{0,1},{1,0},{2,3},{3,2},{4,5},{5,4},{6,7},{7,6},{8,9},{9,8},{10,11... | collective-permute-start | bytes 196616 | tf_op jit(solution)/shard_map/ppermute | solution.py:561
  64.0 4.0 %collective-permute-start.74 = (bf16[80,128]{1,0:T(8,128)(2,1)S(1)}, bf16[80,128]{1,0:T(8,128)(2,1)S(1)}, u32[]{:S(2)}, u32[]{:S(2)}) collective-permute-start(bf16[80,128]{1,0:T(8,128)(2,1)S(1)} %get-tuple-element.247), channel_id=1, source_target_pairs={{0,2},{2,0},{4,6},{6,4},{8,10},{10,8},{12,14},{14,12},{16,18},{18,... | collective-permute-start | bytes 61448 | tf_op jit(solution)/shard_map/ppermute | solution.py:526
  64.1 3.9 %collective-permute-start.75 = (bf16[80,128]{1,0:T(8,128)(2,1)S(1)}, bf16[80,128]{1,0:T(8,128)(2,1)S(1)}, u32[]{:S(2)}, u32[]{:S(2)}) collective-permute-start(bf16[80,128]{1,0:T(8,128)(2,1)S(1)} %get-tuple-element.248), channel_id=1, source_target_pairs={{0,4},{2,6},{4,0},{6,2},{8,12},{10,14},{12,8},{14,10},{16,20},{18,... | collective-permute-start | bytes 61448 | tf_op jit(solution)/shard_map/ppermute | solution.py:526
  71.1 8.8 %collective-permute-start.77 = (bf16[2,80,128]{2,1,0:T(8,128)(2,1)S(1)}, bf16[2,80,128]{2,1,0:T(8,128)(2,1)S(1)}, u32[]{:S(2)}, u32[]{:S(2)}) collective-permute-start(bf16[2,80,128]{2,1,0:T(8,128)(2,1)S(1)} %get-tuple-element.257.refs_0_), channel_id=1, source_target_pairs={{0,8},{2,10},{4,12},{6,14},{8,0},{10,2},{12,4},{14,6},{16,24},{18,... | collective-permute-start | bytes 122888 | tf_op jit(solution)/shard_map/ppermute | solution.py:526
  71.1 8.7 %collective-permute-start.78 = (bf16[2,80,128]{2,1,0:T(8,128)(2,1)S(1)}, bf16[2,80,128]{2,1,0:T(8,128)(2,1)S(1)}, u32[]{:S(2)}, u32[]{:S(2)}) collective-permute-start(bf16[2,80,128]{2,1,0:T(8,128)(2,1)S(1)} %get-tuple-element.257.refs_0_), channel_id=1, source_target_pairs={{0,16},{2,18},{4,20},{6,22},{8,24},{10,26},{12,28},{14,30},{16,0},... | collective-permute-start | bytes 122888 | tf_op jit(solution)/shard_map/ppermute | solution.py:526
  72.5 7.3 %collective-permute-start.79 = (bf16[2,80,128]{2,1,0:T(8,128)(2,1)S(1)}, bf16[2,80,128]{2,1,0:T(8,128)(2,1)S(1)}, u32[]{:S(2)}, u32[]{:S(2)}) collective-permute-start(bf16[2,80,128]{2,1,0:T(8,128)(2,1)S(1)} %get-tuple-element.257.refs_0_), channel_id=1, source_target_pairs={{0,24},{2,26},{4,28},{6,30},{8,16},{10,18},{12,20},{14,22},{16,8},... | collective-permute-start | bytes 122888 | tf_op jit(solution)/shard_map/ppermute | solution.py:526
  79.9 4.0 %collective-permute-start.81 = (bf16[80,128]{1,0:T(8,128)(2,1)S(1)}, bf16[80,128]{1,0:T(8,128)(2,1)S(1)}, u32[]{:S(2)}, u32[]{:S(2)}) collective-permute-start(bf16[80,128]{1,0:T(8,128)(2,1)S(1)} %get-tuple-element.262), channel_id=1, source_target_pairs={{0,2},{2,0},{4,6},{6,4},{8,10},{10,8},{12,14},{14,12},{16,18},{18,... | collective-permute-start | bytes 61448 | tf_op jit(solution)/shard_map/ppermute | solution.py:526
  80.0 3.9 %collective-permute-start.82 = (bf16[80,128]{1,0:T(8,128)(2,1)S(1)}, bf16[80,128]{1,0:T(8,128)(2,1)S(1)}, u32[]{:S(2)}, u32[]{:S(2)}) collective-permute-start(bf16[80,128]{1,0:T(8,128)(2,1)S(1)} %get-tuple-element.263), channel_id=1, source_target_pairs={{0,4},{2,6},{4,0},{6,2},{8,12},{10,14},{12,8},{14,10},{16,20},{18,... | collective-permute-start | bytes 61448 | tf_op jit(solution)/shard_map/ppermute | solution.py:526
  84.6 4.0 %collective-permute-start.84 = (bf16[128,128]{1,0:T(8,128)(2,1)S(1)}, bf16[128,128]{1,0:T(8,128)(2,1)S(1)}, u32[]{:S(2)}, u32[]{:S(2)}) collective-permute-start(bf16[128,128]{1,0:T(8,128)(2,1)S(1)} %shard_map.71.refs_0_), channel_id=1, source_target_pairs={{0,1},{1,0},{2,3},{3,2},{4,5},{5,4},{6,7},{7,6},{8,9},{9,8},{10,11... | collective-permute-start | bytes 98312 | tf_op jit(solution)/shard_map/ppermute | solution.py:561
  (6 other events, 19.9 us)

commit v2 on v1

--- a/solution.py
+++ b/solution.py
@@ -12,6 +12,7 @@
 WIDE = 256
 BATCH = 2
 PAD = 16
+SKEW = 8
 KEPT = 2**18
 
 
@@ -44,7 +45,7 @@
         for part in range(WIDE // LANES):
             i = chunk * (WIDE // LANES) + part
             for term in range(len(mats)):
-                spread_ref[term, pl.ds(i, extent, stride=half), :] = result[
+                spread_ref[term, pl.ds(i, extent, stride=half + SKEW), :] = result[
                     term * extent : (term + 1) * extent, part * LANES : (part + 1) * LANES
                 ]
 
@@ -196,9 +197,9 @@
                 shift = (p - q) * extent % LANES
                 moved = pltpu.roll(given[p], shift, 1) if shift else given[p]
                 row = moved if row is None else jnp.where(group == p, moved, row)
-            turn_ref[pl.ds(per * j + q, half, stride=extent), :] = row
+            turn_ref[pl.ds(per * j + q, half, stride=extent + SKEW), :] = row
     for i in range(half):
-        out_ref[:, i * LANES : (i + 1) * LANES] = turn_ref[i * extent : (i + 1) * extent, :].astype(jnp.bfloat16)
+        out_ref[:, i * LANES : (i + 1) * LANES] = turn_ref[pl.ds(i * (extent + SKEW), extent), :].astype(jnp.bfloat16)
 
 
 def flip(value, extent):
@@ -426,7 +427,7 @@
         kept = kept.astype(jnp.bfloat16)
         tiles = []
         for j in range(extent // per):
-            given = [spread_ref[term, (per * j + q) * half : (per * j + q + 1) * half, :] for q in range(per)]
+            given = [spread_ref[term, pl.ds((per * j + q) * (half + SKEW), half), :] for q in range(per)]
             stacked = []
             for p in range(per):
                 row = None
@@ -551,10 +552,11 @@
     table_shape = jax.ShapeDtypeStruct((TABLE, LANES), jnp.int32)
     spread = jax.ShapeDtypeStruct((terms, extent * extent * extent // LANES, LANES), jnp.bfloat16)
     part = jax.ShapeDtypeStruct((LANES // extent, extent // groups, extent * extent), jnp.bfloat16)
-    space = pltpu.VMEM((LANES // extent,) + spread.shape[1:], jnp.float32)
+    per = LANES // extent
+    space = pltpu.VMEM((per, extent * (extent // per + SKEW), LANES), jnp.float32)
     both = [pltpu.VMEM((2,) + spread.shape, jnp.bfloat16)]
     mixed_space = pltpu.VMEM(spread.shape, jnp.bfloat16)
-    turn_space = pltpu.VMEM(spread.shape[1:], jnp.float32)
+    turn_space = pltpu.VMEM((extent // per * (extent + SKEW), LANES), jnp.float32)
 
     def others(value):
         return [

time: 90 us -> 89.7 us (level); the launches traced: 89.9 us -> 88.6 us
  Pallas kernels: 33.1 us -> 27.5 us
  waiting for transfers between devices: 19.5 us -> 23.3 us
    pallas_call x21, Pallas kernels: 33.1 us -> 27.5 us  [call(): pl.pallas_call(without, out_shape=shapes if isinstance(out_shape, list) e...]
    ppermute x28, waiting for transfers between devices: 17.7 us -> 21.3 us  [exchange(): return lax.ppermute(value, 'node', [(i, i ^ mask) for i in range(nodes)])]
  transfers between devices with their start and end apart: 30 -> 30, of which waited for: 15 -> 19; matrix products, arithmetic and copies ran while one was open for 0% -> 0% of each run, Pallas kernels for 17% -> 11%
where the time goes in v2:
time: 89.7 us; the launch traced here: 88.6 us
  starting transfers between devices  36.9 us (41%)
  Pallas kernels  27.5 us (31%)
  waiting for transfers between devices  23.3 us (26%)
  between operations  0.91 us (1%)
    ppermute x28, starting transfers between devices, exchange(): return lax.ppermute(value, 'node', [(i, i ^ mask) for i in range(nodes)])  34 us
    pallas_call x21, Pallas kernels, call(): pl.pallas_call(without, out_shape=shapes if isinstance(out_shape, list) e...  27.5 us
    ppermute x28, waiting for transfers between devices, exchange(): return lax.ppermute(value, 'node', [(i, i ^ mask) for i in range(nodes)])  21.3 us
    ppermute x2, starting transfers between devices, others(): lax.ppermute(value, 'term', [(i, (i + shift) % groups) for i in range(gro...  2.9 us
    ppermute x2, waiting for transfers between devices, others(): lax.ppermute(value, 'term', [(i, (i + shift) % groups) for i in range(gro...  2.01 us
  transfers between devices with their start and end apart: 30, of which 19 were waited for; matrix products, arithmetic and copies ran while one was open for 0% of the time, Pallas kernels for 11%

profile of v2, /device:TPU:0, one launch (start us, length us, event | category | flops | bytes accessed | tf_op | source)
XLA Modules:
  0.0 88.6 jit_solution(14923655954878079134)
XLA Ops:
  0.0 3.9 %shard_map.55 = (bf16[64,4096]{1,0:T(8,128)(2,1)S(1)}, bf16[64,4096]{1,0:T(8,128)(2,1)S(1)}, bf16[64,4096]{1,0:T(8,128)(2,1)S(1)}, bf16[128,128]{1,0:T(8,128)(2,...) custom-call(bf16[1,64,4096]{2,1,0:T(8,128)(2,1)} %refs_0_.1, ...), custom_call_target="tpu_custom_call" | custom-call | tf_op jit(solution)/shard_map/pallas_call | solution.py:516
  3.9 3.1 %collective-permute-start.59 = (bf16[80,128]{1,0:T(8,128)(2,1)S(1)}, bf16[80,128]{1,0:T(8,128)(2,1)S(1)}, u32[]{:S(2)}, u32[]{:S(2)}) collective-permute-start(bf16[80,128]{1,0:T(8,128)(2,1)S(1)} %get-tuple-element.209.refs_0_), channel_id=1, source_target_pairs={{0,8},{2,10},{4,12},{6,14},{8,0},{10,2},{12,4},{14,6},{16,24},{18,... | collective-permute-start | bytes 61448 | tf_op jit(solution)/shard_map/ppermute | solution.py:527
  7.0 2.6 %collective-permute-start.60 = (bf16[80,128]{1,0:T(8,128)(2,1)S(1)}, bf16[80,128]{1,0:T(8,128)(2,1)S(1)}, u32[]{:S(2)}, u32[]{:S(2)}) collective-permute-start(bf16[80,128]{1,0:T(8,128)(2,1)S(1)} %get-tuple-element.209.refs_0_), channel_id=1, source_target_pairs={{0,16},{2,18},{4,20},{6,22},{8,24},{10,26},{12,28},{14,30},{16,0},... | collective-permute-start | bytes 61448 | tf_op jit(solution)/shard_map/ppermute | solution.py:527
  9.6 2.3 %collective-permute-done.60.refs_2_ = bf16[80,128]{1,0:T(8,128)(2,1)S(1)} collective-permute-done((bf16[80,128]{1,0:T(8,128)(2,1)S(1)}, bf16[80,128]{1,0:T(8,128)(2,1)S(1)}, u32[]{:S(2)}, u32[]{:S(2)}) %collective-permute-start.60) | collective-permute-done | bytes 20512 | tf_op jit(solution)/shard_map/ppermute | solution.py:527
  11.8 3.3 %collective-permute-done.61.refs_3_ = bf16[80,128]{1,0:T(8,128)(2,1)S(1)} collective-permute-done((bf16[80,128]{1,0:T(8,128)(2,1)S(1)}, bf16[80,128]{1,0:T(8,128)(2,1)S(1)}, u32[]{:S(2)}, u32[]{:S(2)}) %collective-permute-start.61) | collective-permute-done | bytes 20512 | tf_op jit(solution)/shard_map/ppermute | solution.py:527
  15.3 1.5 %collective-permute-start.63 = (bf16[2,80,128]{2,1,0:T(8,128)(2,1)S(1)}, bf16[2,80,128]{2,1,0:T(8,128)(2,1)S(1)}, u32[]{:S(2)}, u32[]{:S(2)}) collective-permute-start(bf16[2,80,128]{2,1,0:T(8,128)(2,1)S(1)} %get-tuple-element.213), channel_id=1, source_target_pairs={{0,4},{2,6},{4,0},{6,2},{8,12},{10,14},{12,8},{14,10},{16,20},{18,... | collective-permute-start | bytes 122888 | tf_op jit(solution)/shard_map/ppermute | solution.py:527
  20.3 2.2 %shard_map.58 = (bf16[128,128]{1,0:T(8,128)(2,1)S(1)}, bf16[128,128]{1,0:T(8,128)(2,1)S(1)}, bf16[80,128]{1,0:T(8,128)(2,1)S(1)}) custom-call(bf16[2,80,128]{2,1,0:T(8,128)(2,1)S(1)} %get-tuple-element.220.refs_0_, bf16[2,80,128]{2,1,0:T(8,128)(2,1)S(1)} %collective-permute-done.62.refs_1_, bf16[2,80,128]{2,1,0:T(8,128)(2,1)S(1)} %collective-permute-done.63.refs_2_, ...), custom_call_target="tpu_custom_call" | custom-call | tf_op jit(solution)/shard_map/pallas_call | solution.py:516
  23.4 3.6 %collective-permute-start.67 = (bf16[80,128]{1,0:T(8,128)(2,1)S(1)}, bf16[80,128]{1,0:T(8,128)(2,1)S(1)}, u32[]{:S(2)}, u32[]{:S(2)}) collective-permute-start(bf16[80,128]{1,0:T(8,128)(2,1)S(1)} %get-tuple-element.226.refs_0_), channel_id=1, source_target_pairs={{0,24},{2,26},{4,28},{6,30},{8,16},{10,18},{12,20},{14,22},{16,8},... | collective-permute-start | bytes 61448 | tf_op jit(solution)/shard_map/ppermute | solution.py:527
  27.4 1.6 %collective-permute-done.67.refs_3_ = bf16[80,128]{1,0:T(8,128)(2,1)S(1)} collective-permute-done((bf16[80,128]{1,0:T(8,128)(2,1)S(1)}, bf16[80,128]{1,0:T(8,128)(2,1)S(1)}, u32[]{:S(2)}, u32[]{:S(2)}) %collective-permute-start.67) | collective-permute-done | bytes 20512 | tf_op jit(solution)/shard_map/ppermute | solution.py:527
  31.7 1.7 %collective-permute-done.69.refs_2_ = bf16[2,80,128]{2,1,0:T(8,128)(2,1)S(1)} collective-permute-done((bf16[2,80,128]{2,1,0:T(8,128)(2,1)S(1)}, bf16[2,80,128]{2,1,0:T(8,128)(2,1)S(1)}, u32[]{:S(2)}, u32[]{:S(2)}) %collective-permute-start.69) | collective-permute-done | bytes 40992 | tf_op jit(solution)/shard_map/ppermute | solution.py:527
  33.9 2.2 %shard_map.60 = (bf16[128,128]{1,0:T(8,128)(2,1)S(1)}, bf16[128,128]{1,0:T(8,128)(2,1)S(1)}, bf16[80,128]{1,0:T(8,128)(2,1)S(1)}) custom-call(bf16[2,80,128]{2,1,0:T(8,128)(2,1)S(1)} %get-tuple-element.227.refs_0_, bf16[2,80,128]{2,1,0:T(8,128)(2,1)S(1)} %collective-permute-done.68.refs_1_, bf16[2,80,128]{2,1,0:T(8,128)(2,1)S(1)} %collective-permute-done.69.refs_2_, ...), custom_call_target="tpu_custom_call" | custom-call | tf_op jit(solution)/shard_map/pallas_call | solution.py:516
  36.0 6.0 %conditional.2 = (bf16[2,80,128]{2,1,0:T(8,128)(2,1)S(1)}) conditional(s32[]{:T(128)} %bitcast.1, bf16[80,128]{1,0:T(8,128)(2,1)S(1)} %get-tuple-element.233, bf16[80,128]{1,0:T(8,128)(2,1)S(1)} %get-tuple-element.233, bf16[80,128]{1,0:T(8,128)(2,1)S(1)} %get-tuple-element.233, ...), branch_computations={%region_0.0_spmd, %region_1.0_spmd, %region_2.0_spmd, %region_3.0_... | conditional | bytes 163928 | solution.py:581
  36.5 3.7 %collective-permute-start.7 = (bf16[80,128]{1,0:T(8,128)(2,1)S(1)}, bf16[80,128]{1,0:T(8,128)(2,1)S(1)}, u32[]{:S(2)}, u32[]{:S(2)}) collective-permute-start(bf16[80,128]{1,0:T(8,128)(2,1)S(1)} %param.3), channel_id=1, source_target_pairs={{0,8},{2,10},{4,12},{6,14},{8,0},{10,2},{12,4},{14,6},{16,24},{18,... | collective-permute-start | bytes 61448 | tf_op jit(solution)/shard_map/cond/branch_3_fun/ppermute | solution.py:527
  42.1 3.7 %shard_map.61 = (bf16[2,128,128]{2,1,0:T(8,128)(2,1)S(1)}, bf16[2,80,128]{2,1,0:T(8,128)(2,1)S(1)}) custom-call(bf16[2,80,128]{2,1,0:T(8,128)(2,1)S(1)} %get-tuple-element.278.refs_0_, bf16[64,4096]{1,0:T(8,128)(2,1)S(1)} %get-tuple-element.234.refs_1_.refs_4_, bf16[64,4096]{1,0:T(8,128)(2,1)S(1)} %get-tuple-element.215.refs_0_.refs_4_.refs_2_.refs_5_, ...), custom_call_target="tpu_custom_call" | custom-call | tf_op jit(solution)/shard_map/pallas_call | solution.py:516
  45.8 5.0 %conditional.3 = (bf16[2,80,128]{2,1,0:T(8,128)(2,1)S(1)}) conditional(s32[]{:T(128)} %bitcast.1, (bf16[80,128]{1,0:T(8,128)(2,1)S(1)}, bf16[80,128]{1,0:T(8,128)(2,1)S(1)}) %tuple.102, (bf16[80,128]{1,0:T(8,128)(2,1)S(1)}, bf16[80,128]{1,0:T(8,128)(2,1)S(1)}) %tuple.102, (bf16[80,128]{1,0:T(8,128)(2,1)S(1)}, ...), branch_computations={%region_15.0_spmd, %region_16.0_spmd, %region_17.0_spmd, %region_1... | conditional | bytes 163928 | solution.py:581
  46.7 2.1 %collective-permute-start.36 = (bf16[80,128]{1,0:T(8,128)(2,1)S(1)}, bf16[80,128]{1,0:T(8,128)(2,1)S(1)}, u32[]{:S(2)}, u32[]{:S(2)}) collective-permute-start(bf16[80,128]{1,0:T(8,128)(2,1)S(1)} %get-tuple-element.114), channel_id=1, source_target_pairs={{0,8},{2,10},{4,12},{6,14},{8,0},{10,2},{12,4},{14,6},{16,24},{18,... | collective-permute-start | bytes 61448 | tf_op jit(solution)/shard_map/cond/branch_3_fun/ppermute | solution.py:527
  48.8 1.8 %collective-permute-done.35.refs_0_ = bf16[80,128]{1,0:T(8,128)(2,1)S(1)} collective-permute-done((bf16[80,128]{1,0:T(8,128)(2,1)S(1)}, bf16[80,128]{1,0:T(8,128)(2,1)S(1)}, u32[]{:S(2)}, u32[]{:S(2)}) %collective-permute-start.35) | collective-permute-done | bytes 20512 | tf_op jit(solution)/shard_map/cond/branch_3_fun/ppermute | solution.py:527
  50.8 3.7 %shard_map.62 = (bf16[128,128]{1,0:T(8,128)(2,1)S(1)}, bf16[2,80,128]{2,1,0:T(8,128)(2,1)S(1)}) custom-call(bf16[2,80,128]{2,1,0:T(8,128)(2,1)S(1)} %get-tuple-element.279.refs_0_, bf16[64,4096]{1,0:T(8,128)(2,1)S(1)} %get-tuple-element.234.refs_1_.refs_4_, bf16[64,4096]{1,0:T(8,128)(2,1)S(1)} %get-tuple-element.215.refs_0_.refs_4_.refs_2_.refs_5_, ...), custom_call_target="tpu_custom_call" | custom-call | tf_op jit(solution)/shard_map/pallas_call | solution.py:516
  54.4 1.9 %collective-permute-start.71 = (bf16[2,80,128]{2,1,0:T(8,128)(2,1)S(1)}, bf16[2,80,128]{2,1,0:T(8,128)(2,1)S(1)}, u32[]{:S(2)}, u32[]{:S(2)}) collective-permute-start(bf16[2,80,128]{2,1,0:T(8,128)(2,1)S(1)} %get-tuple-element.242.refs_0_), channel_id=1, source_target_pairs={{0,8},{2,10},{4,12},{6,14},{8,0},{10,2},{12,4},{14,6},{16,24},{18,... | collective-permute-start | bytes 122888 | tf_op jit(solution)/shard_map/ppermute | solution.py:527
  56.3 2.0 %collective-permute-start.72 = (bf16[2,80,128]{2,1,0:T(8,128)(2,1)S(1)}, bf16[2,80,128]{2,1,0:T(8,128)(2,1)S(1)}, u32[]{:S(2)}, u32[]{:S(2)}) collective-permute-start(bf16[2,80,128]{2,1,0:T(8,128)(2,1)S(1)} %get-tuple-element.242.refs_0_), channel_id=1, source_target_pairs={{0,16},{2,18},{4,20},{6,22},{8,24},{10,26},{12,28},{14,30},{16,0},... | collective-permute-start | bytes 122888 | tf_op jit(solution)/shard_map/ppermute | solution.py:527
  61.7 2.4 %collective-permute-done.73.refs_3_ = bf16[2,80,128]{2,1,0:T(8,128)(2,1)S(1)} collective-permute-done((bf16[2,80,128]{2,1,0:T(8,128)(2,1)S(1)}, bf16[2,80,128]{2,1,0:T(8,128)(2,1)S(1)}, u32[]{:S(2)}, u32[]{:S(2)}) %collective-permute-start.73) | collective-permute-done | bytes 40992 | tf_op jit(solution)/shard_map/ppermute | solution.py:527
  68.5 2.8 %shard_map.66 = (bf16[128,128]{1,0:T(8,128)(2,1)S(1)}, bf16[2,80,128]{2,1,0:T(8,128)(2,1)S(1)}) custom-call(bf16[80,128]{1,0:T(8,128)(2,1)S(1)} %get-tuple-element.250.refs_0_, bf16[80,128]{1,0:T(8,128)(2,1)S(1)} %collective-permute-done.74.refs_1_, bf16[80,128]{1,0:T(8,128)(2,1)S(1)} %collective-permute-done.75.refs_2_, ...), custom_call_target="tpu_custom_call" | custom-call | tf_op jit(solution)/shard_map/pallas_call | solution.py:516
  72.7 3.0 %collective-permute-start.79 = (bf16[2,80,128]{2,1,0:T(8,128)(2,1)S(1)}, bf16[2,80,128]{2,1,0:T(8,128)(2,1)S(1)}, u32[]{:S(2)}, u32[]{:S(2)}) collective-permute-start(bf16[2,80,128]{2,1,0:T(8,128)(2,1)S(1)} %get-tuple-element.257.refs_0_), channel_id=1, source_target_pairs={{0,24},{2,26},{4,28},{6,30},{8,16},{10,18},{12,20},{14,22},{16,8},... | collective-permute-start | bytes 122888 | tf_op jit(solution)/shard_map/ppermute | solution.py:527
  85.3 2.0 %collective-permute-done.84.refs_1_ = bf16[128,128]{1,0:T(8,128)(2,1)S(1)} collective-permute-done((bf16[128,128]{1,0:T(8,128)(2,1)S(1)}, bf16[128,128]{1,0:T(8,128)(2,1)S(1)}, u32[]{:S(2)}, u32[]{:S(2)}) %collective-permute-start.84) | collective-permute-done | bytes 32800 | tf_op jit(solution)/shard_map/ppermute | solution.py:563
  (60 shorter events, 30.6 us)
Async XLA Ops:
  3.9 5.7 %collective-permute-start.59 = (bf16[80,128]{1,0:T(8,128)(2,1)S(1)}, bf16[80,128]{1,0:T(8,128)(2,1)S(1)}, u32[]{:S(2)}, u32[]{:S(2)}) collective-permute-start(bf16[80,128]{1,0:T(8,128)(2,1)S(1)} %get-tuple-element.209.refs_0_), channel_id=1, source_target_pairs={{0,8},{2,10},{4,12},{6,14},{8,0},{10,2},{12,4},{14,6},{16,24},{18,... | collective-permute-start | bytes 61448 | tf_op jit(solution)/shard_map/ppermute | solution.py:527
  7.0 4.9 %collective-permute-start.60 = (bf16[80,128]{1,0:T(8,128)(2,1)S(1)}, bf16[80,128]{1,0:T(8,128)(2,1)S(1)}, u32[]{:S(2)}, u32[]{:S(2)}) collective-permute-start(bf16[80,128]{1,0:T(8,128)(2,1)S(1)} %get-tuple-element.209.refs_0_), channel_id=1, source_target_pairs={{0,16},{2,18},{4,20},{6,22},{8,24},{10,26},{12,28},{14,30},{16,0},... | collective-permute-start | bytes 61448 | tf_op jit(solution)/shard_map/ppermute | solution.py:527
  9.6 5.6 %collective-permute-start.61 = (bf16[80,128]{1,0:T(8,128)(2,1)S(1)}, bf16[80,128]{1,0:T(8,128)(2,1)S(1)}, u32[]{:S(2)}, u32[]{:S(2)}) collective-permute-start(bf16[80,128]{1,0:T(8,128)(2,1)S(1)} %get-tuple-element.209.refs_0_), channel_id=1, source_target_pairs={{0,24},{2,26},{4,28},{6,30},{8,16},{10,18},{12,20},{14,22},{16,8},... | collective-permute-start | bytes 61448 | tf_op jit(solution)/shard_map/ppermute | solution.py:527
  15.3 4.1 %collective-permute-start.63 = (bf16[2,80,128]{2,1,0:T(8,128)(2,1)S(1)}, bf16[2,80,128]{2,1,0:T(8,128)(2,1)S(1)}, u32[]{:S(2)}, u32[]{:S(2)}) collective-permute-start(bf16[2,80,128]{2,1,0:T(8,128)(2,1)S(1)} %get-tuple-element.213), channel_id=1, source_target_pairs={{0,4},{2,6},{4,0},{6,2},{8,12},{10,14},{12,8},{14,10},{16,20},{18,... | collective-permute-start | bytes 122888 | tf_op jit(solution)/shard_map/ppermute | solution.py:527
  16.8 3.5 %collective-permute-start.64 = (bf16[2,80,128]{2,1,0:T(8,128)(2,1)S(1)}, bf16[2,80,128]{2,1,0:T(8,128)(2,1)S(1)}, u32[]{:S(2)}, u32[]{:S(2)}) collective-permute-start(bf16[2,80,128]{2,1,0:T(8,128)(2,1)S(1)} %get-tuple-element.214), channel_id=1, source_target_pairs={{0,6},{2,4},{4,2},{6,0},{8,14},{10,12},{12,10},{14,8},{16,22},{18,... | collective-permute-start | bytes 122888 | tf_op jit(solution)/shard_map/ppermute | solution.py:527
  22.5 4.5 %collective-permute-start.65 = (bf16[80,128]{1,0:T(8,128)(2,1)S(1)}, bf16[80,128]{1,0:T(8,128)(2,1)S(1)}, u32[]{:S(2)}, u32[]{:S(2)}) collective-permute-start(bf16[80,128]{1,0:T(8,128)(2,1)S(1)} %get-tuple-element.226.refs_0_), channel_id=1, source_target_pairs={{0,8},{2,10},{4,12},{6,14},{8,0},{10,2},{12,4},{14,6},{16,24},{18,... | collective-permute-start | bytes 61448 | tf_op jit(solution)/shard_map/ppermute | solution.py:527
  22.6 4.7 %collective-permute-start.66 = (bf16[80,128]{1,0:T(8,128)(2,1)S(1)}, bf16[80,128]{1,0:T(8,128)(2,1)S(1)}, u32[]{:S(2)}, u32[]{:S(2)}) collective-permute-start(bf16[80,128]{1,0:T(8,128)(2,1)S(1)} %get-tuple-element.226.refs_0_), channel_id=1, source_target_pairs={{0,16},{2,18},{4,20},{6,22},{8,24},{10,26},{12,28},{14,30},{16,0},... | collective-permute-start | bytes 61448 | tf_op jit(solution)/shard_map/ppermute | solution.py:527
  23.4 5.6 %collective-permute-start.67 = (bf16[80,128]{1,0:T(8,128)(2,1)S(1)}, bf16[80,128]{1,0:T(8,128)(2,1)S(1)}, u32[]{:S(2)}, u32[]{:S(2)}) collective-permute-start(bf16[80,128]{1,0:T(8,128)(2,1)S(1)} %get-tuple-element.226.refs_0_), channel_id=1, source_target_pairs={{0,24},{2,26},{4,28},{6,30},{8,16},{10,18},{12,20},{14,22},{16,8},... | collective-permute-start | bytes 61448 | tf_op jit(solution)/shard_map/ppermute | solution.py:527
  29.1 4.2 %collective-permute-start.69 = (bf16[2,80,128]{2,1,0:T(8,128)(2,1)S(1)}, bf16[2,80,128]{2,1,0:T(8,128)(2,1)S(1)}, u32[]{:S(2)}, u32[]{:S(2)}) collective-permute-start(bf16[2,80,128]{2,1,0:T(8,128)(2,1)S(1)} %get-tuple-element.229), channel_id=1, source_target_pairs={{0,4},{2,6},{4,0},{6,2},{8,12},{10,14},{12,8},{14,10},{16,20},{18,... | collective-permute-start | bytes 122888 | tf_op jit(solution)/shard_map/ppermute | solution.py:527
  30.1 3.8 %collective-permute-start.70 = (bf16[2,80,128]{2,1,0:T(8,128)(2,1)S(1)}, bf16[2,80,128]{2,1,0:T(8,128)(2,1)S(1)}, u32[]{:S(2)}, u32[]{:S(2)}) collective-permute-start(bf16[2,80,128]{2,1,0:T(8,128)(2,1)S(1)} %get-tuple-element.230), channel_id=1, source_target_pairs={{0,6},{2,4},{4,2},{6,0},{8,14},{10,12},{12,10},{14,8},{16,22},{18,... | collective-permute-start | bytes 122888 | tf_op jit(solution)/shard_map/ppermute | solution.py:527
  36.1 5.1 %collective-permute-start.6 = (bf16[80,128]{1,0:T(8,128)(2,1)S(1)}, bf16[80,128]{1,0:T(8,128)(2,1)S(1)}, u32[]{:S(2)}, u32[]{:S(2)}) collective-permute-start(bf16[80,128]{1,0:T(8,128)(2,1)S(1)} %param.3), channel_id=1, source_target_pairs={{0,16},{2,18},{4,20},{6,22},{8,24},{10,26},{12,28},{14,30},{16,0},... | collective-permute-start | bytes 61448 | tf_op jit(solution)/shard_map/cond/branch_3_fun/ppermute | solution.py:527
  36.5 5.5 %collective-permute-start.7 = (bf16[80,128]{1,0:T(8,128)(2,1)S(1)}, bf16[80,128]{1,0:T(8,128)(2,1)S(1)}, u32[]{:S(2)}, u32[]{:S(2)}) collective-permute-start(bf16[80,128]{1,0:T(8,128)(2,1)S(1)} %param.3), channel_id=1, source_target_pairs={{0,8},{2,10},{4,12},{6,14},{8,0},{10,2},{12,4},{14,6},{16,24},{18,... | collective-permute-start | bytes 61448 | tf_op jit(solution)/shard_map/cond/branch_3_fun/ppermute | solution.py:527
  45.8 4.8 %collective-permute-start.35 = (bf16[80,128]{1,0:T(8,128)(2,1)S(1)}, bf16[80,128]{1,0:T(8,128)(2,1)S(1)}, u32[]{:S(2)}, u32[]{:S(2)}) collective-permute-start(bf16[80,128]{1,0:T(8,128)(2,1)S(1)} %get-tuple-element.110), channel_id=1, source_target_pairs={{0,16},{2,18},{4,20},{6,22},{8,24},{10,26},{12,28},{14,30},{16,0},... | collective-permute-start | bytes 61448 | tf_op jit(solution)/shard_map/cond/branch_3_fun/ppermute | solution.py:527
  46.7 4.1 %collective-permute-start.36 = (bf16[80,128]{1,0:T(8,128)(2,1)S(1)}, bf16[80,128]{1,0:T(8,128)(2,1)S(1)}, u32[]{:S(2)}, u32[]{:S(2)}) collective-permute-start(bf16[80,128]{1,0:T(8,128)(2,1)S(1)} %get-tuple-element.114), channel_id=1, source_target_pairs={{0,8},{2,10},{4,12},{6,14},{8,0},{10,2},{12,4},{14,6},{16,24},{18,... | collective-permute-start | bytes 61448 | tf_op jit(solution)/shard_map/cond/branch_3_fun/ppermute | solution.py:527
  54.4 7.2 %collective-permute-start.71 = (bf16[2,80,128]{2,1,0:T(8,128)(2,1)S(1)}, bf16[2,80,128]{2,1,0:T(8,128)(2,1)S(1)}, u32[]{:S(2)}, u32[]{:S(2)}) collective-permute-start(bf16[2,80,128]{2,1,0:T(8,128)(2,1)S(1)} %get-tuple-element.242.refs_0_), channel_id=1, source_target_pairs={{0,8},{2,10},{4,12},{6,14},{8,0},{10,2},{12,4},{14,6},{16,24},{18,... | collective-permute-start | bytes 122888 | tf_op jit(solution)/shard_map/ppermute | solution.py:527
  56.3 5.4 %collective-permute-start.72 = (bf16[2,80,128]{2,1,0:T(8,128)(2,1)S(1)}, bf16[2,80,128]{2,1,0:T(8,128)(2,1)S(1)}, u32[]{:S(2)}, u32[]{:S(2)}) collective-permute-start(bf16[2,80,128]{2,1,0:T(8,128)(2,1)S(1)} %get-tuple-element.242.refs_0_), channel_id=1, source_target_pairs={{0,16},{2,18},{4,20},{6,22},{8,24},{10,26},{12,28},{14,30},{16,0},... | collective-permute-start | bytes 122888 | tf_op jit(solution)/shard_map/ppermute | solution.py:527
  58.3 5.8 %collective-permute-start.73 = (bf16[2,80,128]{2,1,0:T(8,128)(2,1)S(1)}, bf16[2,80,128]{2,1,0:T(8,128)(2,1)S(1)}, u32[]{:S(2)}, u32[]{:S(2)}) collective-permute-start(bf16[2,80,128]{2,1,0:T(8,128)(2,1)S(1)} %get-tuple-element.242.refs_0_), channel_id=1, source_target_pairs={{0,24},{2,26},{4,28},{6,30},{8,16},{10,18},{12,20},{14,22},{16,8},... | collective-permute-start | bytes 122888 | tf_op jit(solution)/shard_map/ppermute | solution.py:527
  58.9 17.9 %collective-permute-start.80 = (bf16[2,128,128]{2,1,0:T(8,128)(2,1)S(1)}, bf16[2,128,128]{2,1,0:T(8,128)(2,1)S(1)}, u32[]{:S(2)}, u32[]{:S(2)}) collective-permute-start(bf16[2,128,128]{2,1,0:T(8,128)(2,1)S(1)} %get-tuple-element.240.refs_5_.refs_1_), channel_id=1, source_target_pairs={{0,1},{1,0},{2,3},{3,2},{4,5},{5,4},{6,7},{7,6},{8,9},{9,8},{10,11... | collective-permute-start | bytes 196616 | tf_op jit(solution)/shard_map/ppermute | solution.py:563
  64.3 3.8 %collective-permute-start.75 = (bf16[80,128]{1,0:T(8,128)(2,1)S(1)}, bf16[80,128]{1,0:T(8,128)(2,1)S(1)}, u32[]{:S(2)}, u32[]{:S(2)}) collective-permute-start(bf16[80,128]{1,0:T(8,128)(2,1)S(1)} %get-tuple-element.248), channel_id=1, source_target_pairs={{0,4},{2,6},{4,0},{6,2},{8,12},{10,14},{12,8},{14,10},{16,20},{18,... | collective-permute-start | bytes 61448 | tf_op jit(solution)/shard_map/ppermute | solution.py:527
  71.3 6.5 %collective-permute-start.77 = (bf16[2,80,128]{2,1,0:T(8,128)(2,1)S(1)}, bf16[2,80,128]{2,1,0:T(8,128)(2,1)S(1)}, u32[]{:S(2)}, u32[]{:S(2)}) collective-permute-start(bf16[2,80,128]{2,1,0:T(8,128)(2,1)S(1)} %get-tuple-element.257.refs_0_), channel_id=1, source_target_pairs={{0,8},{2,10},{4,12},{6,14},{8,0},{10,2},{12,4},{14,6},{16,24},{18,... | collective-permute-start | bytes 122888 | tf_op jit(solution)/shard_map/ppermute | solution.py:527
  71.4 6.5 %collective-permute-start.78 = (bf16[2,80,128]{2,1,0:T(8,128)(2,1)S(1)}, bf16[2,80,128]{2,1,0:T(8,128)(2,1)S(1)}, u32[]{:S(2)}, u32[]{:S(2)}) collective-permute-start(bf16[2,80,128]{2,1,0:T(8,128)(2,1)S(1)} %get-tuple-element.257.refs_0_), channel_id=1, source_target_pairs={{0,16},{2,18},{4,20},{6,22},{8,24},{10,26},{12,28},{14,30},{16,0},... | collective-permute-start | bytes 122888 | tf_op jit(solution)/shard_map/ppermute | solution.py:527
  72.7 5.8 %collective-permute-start.79 = (bf16[2,80,128]{2,1,0:T(8,128)(2,1)S(1)}, bf16[2,80,128]{2,1,0:T(8,128)(2,1)S(1)}, u32[]{:S(2)}, u32[]{:S(2)}) collective-permute-start(bf16[2,80,128]{2,1,0:T(8,128)(2,1)S(1)} %get-tuple-element.257.refs_0_), channel_id=1, source_target_pairs={{0,24},{2,26},{4,28},{6,30},{8,16},{10,18},{12,20},{14,22},{16,8},... | collective-permute-start | bytes 122888 | tf_op jit(solution)/shard_map/ppermute | solution.py:527
  78.8 3.8 %collective-permute-start.82 = (bf16[80,128]{1,0:T(8,128)(2,1)S(1)}, bf16[80,128]{1,0:T(8,128)(2,1)S(1)}, u32[]{:S(2)}, u32[]{:S(2)}) collective-permute-start(bf16[80,128]{1,0:T(8,128)(2,1)S(1)} %get-tuple-element.263), channel_id=1, source_target_pairs={{0,4},{2,6},{4,0},{6,2},{8,12},{10,14},{12,8},{14,10},{16,20},{18,... | collective-permute-start | bytes 61448 | tf_op jit(solution)/shard_map/ppermute | solution.py:527
  83.4 4.0 %collective-permute-start.84 = (bf16[128,128]{1,0:T(8,128)(2,1)S(1)}, bf16[128,128]{1,0:T(8,128)(2,1)S(1)}, u32[]{:S(2)}, u32[]{:S(2)}) collective-permute-start(bf16[128,128]{1,0:T(8,128)(2,1)S(1)} %shard_map.71.refs_0_), channel_id=1, source_target_pairs={{0,1},{1,0},{2,3},{3,2},{4,5},{5,4},{6,7},{7,6},{8,9},{9,8},{10,11... | collective-permute-start | bytes 98312 | tf_op jit(solution)/shard_map/ppermute | solution.py:563
  (6 other events, 18.3 us)

commit v3 on v2

--- a/solution.py
+++ b/solution.py
@@ -553,10 +553,10 @@
     spread = jax.ShapeDtypeStruct((terms, extent * extent * extent // LANES, LANES), jnp.bfloat16)
     part = jax.ShapeDtypeStruct((LANES // extent, extent // groups, extent * extent), jnp.bfloat16)
     per = LANES // extent
-    space = pltpu.VMEM((per, extent * (extent // per + SKEW), LANES), jnp.float32)
+    space = pltpu.VMEM((per, extent * (extent // per + SKEW) + extent, LANES), jnp.float32)
     both = [pltpu.VMEM((2,) + spread.shape, jnp.bfloat16)]
     mixed_space = pltpu.VMEM(spread.shape, jnp.bfloat16)
-    turn_space = pltpu.VMEM((extent // per * (extent + SKEW), LANES), jnp.float32)
+    turn_space = pltpu.VMEM((extent // per * (extent + SKEW) + extent, LANES), jnp.float32)
 
     def others(value):
         return [

time: 89.7 us -> 89 us (level)
  starting transfers between devices: 36.9 us -> 33.1 us
  waiting for transfers between devices: 23.3 us -> 26.4 us
    ppermute x28, starting transfers between devices: 34 us -> 29.9 us  [exchange(): return lax.ppermute(value, 'node', [(i, i ^ mask) for i in range(nodes)])]
    ppermute x28, waiting for transfers between devices: 21.3 us -> 24.6 us  [exchange(): return lax.ppermute(value, 'node', [(i, i ^ mask) for i in range(nodes)])]
  transfers between devices with their start and end apart: 30 -> 30, of which waited for: 19 -> 18; matrix products, arithmetic and copies ran while one was open for 0% -> 0% of each run, Pallas kernels for 11% -> 12%
where the time goes in v3:
time: 89 us; the launch traced here: 87.9 us
  starting transfers between devices  33.1 us (37%)
  Pallas kernels  27.5 us (31%)
  waiting for transfers between devices  26.4 us (30%)
  between operations  0.91 us (1%)
    ppermute x28, starting transfers between devices, exchange(): return lax.ppermute(value, 'node', [(i, i ^ mask) for i in range(nodes)])  29.9 us
    pallas_call x21, Pallas kernels, call(): pl.pallas_call(without, out_shape=shapes if isinstance(out_shape, list) e...  27.5 us
    ppermute x28, waiting for transfers between devices, exchange(): return lax.ppermute(value, 'node', [(i, i ^ mask) for i in range(nodes)])  24.6 us
    ppermute x2, starting transfers between devices, others(): lax.ppermute(value, 'term', [(i, (i + shift) % groups) for i in range(gro...  3.14 us
  transfers between devices with their start and end apart: 30, of which 18 were waited for; matrix products, arithmetic and copies ran while one was open for 0% of the time, Pallas kernels for 12%

profile of v3, /device:TPU:0, one launch (start us, length us, event | category | flops | bytes accessed | tf_op | source)
XLA Modules:
  0.0 87.9 jit_solution(8681232416287769754)
XLA Ops:
  0.0 3.9 %shard_map.55 = (bf16[64,4096]{1,0:T(8,128)(2,1)S(1)}, bf16[64,4096]{1,0:T(8,128)(2,1)S(1)}, bf16[64,4096]{1,0:T(8,128)(2,1)S(1)}, bf16[128,128]{1,0:T(8,128)(2,...) custom-call(bf16[1,64,4096]{2,1,0:T(8,128)(2,1)} %refs_0_.1, ...), custom_call_target="tpu_custom_call" | custom-call | tf_op jit(solution)/shard_map/pallas_call | solution.py:516
  3.9 3.1 %collective-permute-start.59 = (bf16[80,128]{1,0:T(8,128)(2,1)S(1)}, bf16[80,128]{1,0:T(8,128)(2,1)S(1)}, u32[]{:S(2)}, u32[]{:S(2)}) collective-permute-start(bf16[80,128]{1,0:T(8,128)(2,1)S(1)} %get-tuple-element.209.refs_0_), channel_id=1, source_target_pairs={{0,8},{2,10},{4,12},{6,14},{8,0},{10,2},{12,4},{14,6},{16,24},{18,... | collective-permute-start | bytes 61448 | tf_op jit(solution)/shard_map/ppermute | solution.py:527
  7.0 2.6 %collective-permute-start.60 = (bf16[80,128]{1,0:T(8,128)(2,1)S(1)}, bf16[80,128]{1,0:T(8,128)(2,1)S(1)}, u32[]{:S(2)}, u32[]{:S(2)}) collective-permute-start(bf16[80,128]{1,0:T(8,128)(2,1)S(1)} %get-tuple-element.209.refs_0_), channel_id=1, source_target_pairs={{0,16},{2,18},{4,20},{6,22},{8,24},{10,26},{12,28},{14,30},{16,0},... | collective-permute-start | bytes 61448 | tf_op jit(solution)/shard_map/ppermute | solution.py:527
  9.6 2.3 %collective-permute-done.60.refs_2_ = bf16[80,128]{1,0:T(8,128)(2,1)S(1)} collective-permute-done((bf16[80,128]{1,0:T(8,128)(2,1)S(1)}, bf16[80,128]{1,0:T(8,128)(2,1)S(1)}, u32[]{:S(2)}, u32[]{:S(2)}) %collective-permute-start.60) | collective-permute-done | bytes 20512 | tf_op jit(solution)/shard_map/ppermute | solution.py:527
  11.8 3.3 %collective-permute-done.61.refs_3_ = bf16[80,128]{1,0:T(8,128)(2,1)S(1)} collective-permute-done((bf16[80,128]{1,0:T(8,128)(2,1)S(1)}, bf16[80,128]{1,0:T(8,128)(2,1)S(1)}, u32[]{:S(2)}, u32[]{:S(2)}) %collective-permute-start.61) | collective-permute-done | bytes 20512 | tf_op jit(solution)/shard_map/ppermute | solution.py:527
  15.3 1.5 %collective-permute-start.63 = (bf16[2,80,128]{2,1,0:T(8,128)(2,1)S(1)}, bf16[2,80,128]{2,1,0:T(8,128)(2,1)S(1)}, u32[]{:S(2)}, u32[]{:S(2)}) collective-permute-start(bf16[2,80,128]{2,1,0:T(8,128)(2,1)S(1)} %get-tuple-element.213), channel_id=1, source_target_pairs={{0,4},{2,6},{4,0},{6,2},{8,12},{10,14},{12,8},{14,10},{16,20},{18,... | collective-permute-start | bytes 122888 | tf_op jit(solution)/shard_map/ppermute | solution.py:527
  20.3 2.2 %shard_map.58 = (bf16[128,128]{1,0:T(8,128)(2,1)S(1)}, bf16[128,128]{1,0:T(8,128)(2,1)S(1)}, bf16[80,128]{1,0:T(8,128)(2,1)S(1)}) custom-call(bf16[2,80,128]{2,1,0:T(8,128)(2,1)S(1)} %get-tuple-element.220.refs_0_, bf16[2,80,128]{2,1,0:T(8,128)(2,1)S(1)} %collective-permute-done.62.refs_1_, bf16[2,80,128]{2,1,0:T(8,128)(2,1)S(1)} %collective-permute-done.63.refs_2_, ...), custom_call_target="tpu_custom_call" | custom-call | tf_op jit(solution)/shard_map/pallas_call | solution.py:516
  23.4 3.6 %collective-permute-start.67 = (bf16[80,128]{1,0:T(8,128)(2,1)S(1)}, bf16[80,128]{1,0:T(8,128)(2,1)S(1)}, u32[]{:S(2)}, u32[]{:S(2)}) collective-permute-start(bf16[80,128]{1,0:T(8,128)(2,1)S(1)} %get-tuple-element.226.refs_0_), channel_id=1, source_target_pairs={{0,24},{2,26},{4,28},{6,30},{8,16},{10,18},{12,20},{14,22},{16,8},... | collective-permute-start | bytes 61448 | tf_op jit(solution)/shard_map/ppermute | solution.py:527
  27.4 1.6 %collective-permute-done.67.refs_3_ = bf16[80,128]{1,0:T(8,128)(2,1)S(1)} collective-permute-done((bf16[80,128]{1,0:T(8,128)(2,1)S(1)}, bf16[80,128]{1,0:T(8,128)(2,1)S(1)}, u32[]{:S(2)}, u32[]{:S(2)}) %collective-permute-start.67) | collective-permute-done | bytes 20512 | tf_op jit(solution)/shard_map/ppermute | solution.py:527
  31.7 1.7 %collective-permute-done.69.refs_2_ = bf16[2,80,128]{2,1,0:T(8,128)(2,1)S(1)} collective-permute-done((bf16[2,80,128]{2,1,0:T(8,128)(2,1)S(1)}, bf16[2,80,128]{2,1,0:T(8,128)(2,1)S(1)}, u32[]{:S(2)}, u32[]{:S(2)}) %collective-permute-start.69) | collective-permute-done | bytes 40992 | tf_op jit(solution)/shard_map/ppermute | solution.py:527
  33.9 2.2 %shard_map.60 = (bf16[128,128]{1,0:T(8,128)(2,1)S(1)}, bf16[128,128]{1,0:T(8,128)(2,1)S(1)}, bf16[80,128]{1,0:T(8,128)(2,1)S(1)}) custom-call(bf16[2,80,128]{2,1,0:T(8,128)(2,1)S(1)} %get-tuple-element.227.refs_0_, bf16[2,80,128]{2,1,0:T(8,128)(2,1)S(1)} %collective-permute-done.68.refs_1_, bf16[2,80,128]{2,1,0:T(8,128)(2,1)S(1)} %collective-permute-done.69.refs_2_, ...), custom_call_target="tpu_custom_call" | custom-call | tf_op jit(solution)/shard_map/pallas_call | solution.py:516
  36.0 5.0 %conditional.2 = (bf16[2,80,128]{2,1,0:T(8,128)(2,1)S(1)}) conditional(s32[]{:T(128)} %bitcast.1, bf16[80,128]{1,0:T(8,128)(2,1)S(1)} %get-tuple-element.233, bf16[80,128]{1,0:T(8,128)(2,1)S(1)} %get-tuple-element.233, bf16[80,128]{1,0:T(8,128)(2,1)S(1)} %get-tuple-element.233, ...), branch_computations={%region_0.0_spmd, %region_1.0_spmd, %region_2.0_spmd, %region_3.0_... | conditional | bytes 163928 | solution.py:581
  36.9 4.1 %collective-permute-done.4.refs_0_ = bf16[80,128]{1,0:T(8,128)(2,1)S(1)} collective-permute-done((bf16[80,128]{1,0:T(8,128)(2,1)S(1)}, bf16[80,128]{1,0:T(8,128)(2,1)S(1)}, u32[]{:S(2)}, u32[]{:S(2)}) %collective-permute-start.4) | collective-permute-done | bytes 20512 | tf_op jit(solution)/shard_map/cond/branch_2_fun/ppermute | solution.py:527
  41.1 3.7 %shard_map.61 = (bf16[2,128,128]{2,1,0:T(8,128)(2,1)S(1)}, bf16[2,80,128]{2,1,0:T(8,128)(2,1)S(1)}) custom-call(bf16[2,80,128]{2,1,0:T(8,128)(2,1)S(1)} %get-tuple-element.278.refs_0_, bf16[64,4096]{1,0:T(8,128)(2,1)S(1)} %get-tuple-element.234.refs_1_.refs_4_, bf16[64,4096]{1,0:T(8,128)(2,1)S(1)} %get-tuple-element.215.refs_0_.refs_4_.refs_2_.refs_5_, ...), custom_call_target="tpu_custom_call" | custom-call | tf_op jit(solution)/shard_map/pallas_call | solution.py:516
  44.8 5.0 %conditional.3 = (bf16[2,80,128]{2,1,0:T(8,128)(2,1)S(1)}) conditional(s32[]{:T(128)} %bitcast.1, (bf16[80,128]{1,0:T(8,128)(2,1)S(1)}, bf16[80,128]{1,0:T(8,128)(2,1)S(1)}) %tuple.102, (bf16[80,128]{1,0:T(8,128)(2,1)S(1)}, bf16[80,128]{1,0:T(8,128)(2,1)S(1)}) %tuple.102, (bf16[80,128]{1,0:T(8,128)(2,1)S(1)}, ...), branch_computations={%region_15.0_spmd, %region_16.0_spmd, %region_17.0_spmd, %region_1... | conditional | bytes 163928 | solution.py:581
  46.6 3.0 %collective-permute-done.33.refs_0_ = bf16[80,128]{1,0:T(8,128)(2,1)S(1)} collective-permute-done((bf16[80,128]{1,0:T(8,128)(2,1)S(1)}, bf16[80,128]{1,0:T(8,128)(2,1)S(1)}, u32[]{:S(2)}, u32[]{:S(2)}) %collective-permute-start.33) | collective-permute-done | bytes 20512 | tf_op jit(solution)/shard_map/cond/branch_2_fun/ppermute | solution.py:527
  49.7 3.7 %shard_map.62 = (bf16[128,128]{1,0:T(8,128)(2,1)S(1)}, bf16[2,80,128]{2,1,0:T(8,128)(2,1)S(1)}) custom-call(bf16[2,80,128]{2,1,0:T(8,128)(2,1)S(1)} %get-tuple-element.279.refs_0_, bf16[64,4096]{1,0:T(8,128)(2,1)S(1)} %get-tuple-element.234.refs_1_.refs_4_, bf16[64,4096]{1,0:T(8,128)(2,1)S(1)} %get-tuple-element.215.refs_0_.refs_4_.refs_2_.refs_5_, ...), custom_call_target="tpu_custom_call" | custom-call | tf_op jit(solution)/shard_map/pallas_call | solution.py:516
  53.4 2.6 %collective-permute-start.71 = (bf16[2,80,128]{2,1,0:T(8,128)(2,1)S(1)}, bf16[2,80,128]{2,1,0:T(8,128)(2,1)S(1)}, u32[]{:S(2)}, u32[]{:S(2)}) collective-permute-start(bf16[2,80,128]{2,1,0:T(8,128)(2,1)S(1)} %get-tuple-element.242.refs_0_), channel_id=1, source_target_pairs={{0,8},{2,10},{4,12},{6,14},{8,0},{10,2},{12,4},{14,6},{16,24},{18,... | collective-permute-start | bytes 122888 | tf_op jit(solution)/shard_map/ppermute | solution.py:527
  56.0 1.6 %collective-permute-start.72 = (bf16[2,80,128]{2,1,0:T(8,128)(2,1)S(1)}, bf16[2,80,128]{2,1,0:T(8,128)(2,1)S(1)}, u32[]{:S(2)}, u32[]{:S(2)}) collective-permute-start(bf16[2,80,128]{2,1,0:T(8,128)(2,1)S(1)} %get-tuple-element.242.refs_0_), channel_id=1, source_target_pairs={{0,16},{2,18},{4,20},{6,22},{8,24},{10,26},{12,28},{14,30},{16,0},... | collective-permute-start | bytes 122888 | tf_op jit(solution)/shard_map/ppermute | solution.py:527
  61.2 2.2 %collective-permute-done.73.refs_3_ = bf16[2,80,128]{2,1,0:T(8,128)(2,1)S(1)} collective-permute-done((bf16[2,80,128]{2,1,0:T(8,128)(2,1)S(1)}, bf16[2,80,128]{2,1,0:T(8,128)(2,1)S(1)}, u32[]{:S(2)}, u32[]{:S(2)}) %collective-permute-start.73) | collective-permute-done | bytes 40992 | tf_op jit(solution)/shard_map/ppermute | solution.py:527
  67.7 2.8 %shard_map.66 = (bf16[128,128]{1,0:T(8,128)(2,1)S(1)}, bf16[2,80,128]{2,1,0:T(8,128)(2,1)S(1)}) custom-call(bf16[80,128]{1,0:T(8,128)(2,1)S(1)} %get-tuple-element.250.refs_0_, bf16[80,128]{1,0:T(8,128)(2,1)S(1)} %collective-permute-done.74.refs_1_, bf16[80,128]{1,0:T(8,128)(2,1)S(1)} %collective-permute-done.75.refs_2_, ...), custom_call_target="tpu_custom_call" | custom-call | tf_op jit(solution)/shard_map/pallas_call | solution.py:516
  72.0 3.0 %collective-permute-start.79 = (bf16[2,80,128]{2,1,0:T(8,128)(2,1)S(1)}, bf16[2,80,128]{2,1,0:T(8,128)(2,1)S(1)}, u32[]{:S(2)}, u32[]{:S(2)}) collective-permute-start(bf16[2,80,128]{2,1,0:T(8,128)(2,1)S(1)} %get-tuple-element.257.refs_0_), channel_id=1, source_target_pairs={{0,24},{2,26},{4,28},{6,30},{8,16},{10,18},{12,20},{14,22},{16,8},... | collective-permute-start | bytes 122888 | tf_op jit(solution)/shard_map/ppermute | solution.py:527
  82.6 1.6 %collective-permute-start.84 = (bf16[128,128]{1,0:T(8,128)(2,1)S(1)}, bf16[128,128]{1,0:T(8,128)(2,1)S(1)}, u32[]{:S(2)}, u32[]{:S(2)}) collective-permute-start(bf16[128,128]{1,0:T(8,128)(2,1)S(1)} %shard_map.71.refs_0_), channel_id=1, source_target_pairs={{0,1},{1,0},{2,3},{3,2},{4,5},{5,4},{6,7},{7,6},{8,9},{9,8},{10,11... | collective-permute-start | bytes 98312 | tf_op jit(solution)/shard_map/ppermute | solution.py:563
  84.8 1.8 %collective-permute-done.84.refs_1_ = bf16[128,128]{1,0:T(8,128)(2,1)S(1)} collective-permute-done((bf16[128,128]{1,0:T(8,128)(2,1)S(1)}, bf16[128,128]{1,0:T(8,128)(2,1)S(1)}, u32[]{:S(2)}, u32[]{:S(2)}) %collective-permute-start.84) | collective-permute-done | bytes 32800 | tf_op jit(solution)/shard_map/ppermute | solution.py:563
  (60 shorter events, 29.0 us)
Async XLA Ops:
  3.9 5.7 %collective-permute-start.59 = (bf16[80,128]{1,0:T(8,128)(2,1)S(1)}, bf16[80,128]{1,0:T(8,128)(2,1)S(1)}, u32[]{:S(2)}, u32[]{:S(2)}) collective-permute-start(bf16[80,128]{1,0:T(8,128)(2,1)S(1)} %get-tuple-element.209.refs_0_), channel_id=1, source_target_pairs={{0,8},{2,10},{4,12},{6,14},{8,0},{10,2},{12,4},{14,6},{16,24},{18,... | collective-permute-start | bytes 61448 | tf_op jit(solution)/shard_map/ppermute | solution.py:527
  7.0 4.9 %collective-permute-start.60 = (bf16[80,128]{1,0:T(8,128)(2,1)S(1)}, bf16[80,128]{1,0:T(8,128)(2,1)S(1)}, u32[]{:S(2)}, u32[]{:S(2)}) collective-permute-start(bf16[80,128]{1,0:T(8,128)(2,1)S(1)} %get-tuple-element.209.refs_0_), channel_id=1, source_target_pairs={{0,16},{2,18},{4,20},{6,22},{8,24},{10,26},{12,28},{14,30},{16,0},... | collective-permute-start | bytes 61448 | tf_op jit(solution)/shard_map/ppermute | solution.py:527
  9.6 5.6 %collective-permute-start.61 = (bf16[80,128]{1,0:T(8,128)(2,1)S(1)}, bf16[80,128]{1,0:T(8,128)(2,1)S(1)}, u32[]{:S(2)}, u32[]{:S(2)}) collective-permute-start(bf16[80,128]{1,0:T(8,128)(2,1)S(1)} %get-tuple-element.209.refs_0_), channel_id=1, source_target_pairs={{0,24},{2,26},{4,28},{6,30},{8,16},{10,18},{12,20},{14,22},{16,8},... | collective-permute-start | bytes 61448 | tf_op jit(solution)/shard_map/ppermute | solution.py:527
  15.3 4.1 %collective-permute-start.63 = (bf16[2,80,128]{2,1,0:T(8,128)(2,1)S(1)}, bf16[2,80,128]{2,1,0:T(8,128)(2,1)S(1)}, u32[]{:S(2)}, u32[]{:S(2)}) collective-permute-start(bf16[2,80,128]{2,1,0:T(8,128)(2,1)S(1)} %get-tuple-element.213), channel_id=1, source_target_pairs={{0,4},{2,6},{4,0},{6,2},{8,12},{10,14},{12,8},{14,10},{16,20},{18,... | collective-permute-start | bytes 122888 | tf_op jit(solution)/shard_map/ppermute | solution.py:527
  16.8 3.5 %collective-permute-start.64 = (bf16[2,80,128]{2,1,0:T(8,128)(2,1)S(1)}, bf16[2,80,128]{2,1,0:T(8,128)(2,1)S(1)}, u32[]{:S(2)}, u32[]{:S(2)}) collective-permute-start(bf16[2,80,128]{2,1,0:T(8,128)(2,1)S(1)} %get-tuple-element.214), channel_id=1, source_target_pairs={{0,6},{2,4},{4,2},{6,0},{8,14},{10,12},{12,10},{14,8},{16,22},{18,... | collective-permute-start | bytes 122888 | tf_op jit(solution)/shard_map/ppermute | solution.py:527
  22.5 4.5 %collective-permute-start.65 = (bf16[80,128]{1,0:T(8,128)(2,1)S(1)}, bf16[80,128]{1,0:T(8,128)(2,1)S(1)}, u32[]{:S(2)}, u32[]{:S(2)}) collective-permute-start(bf16[80,128]{1,0:T(8,128)(2,1)S(1)} %get-tuple-element.226.refs_0_), channel_id=1, source_target_pairs={{0,8},{2,10},{4,12},{6,14},{8,0},{10,2},{12,4},{14,6},{16,24},{18,... | collective-permute-start | bytes 61448 | tf_op jit(solution)/shard_map/ppermute | solution.py:527
  22.6 4.7 %collective-permute-start.66 = (bf16[80,128]{1,0:T(8,128)(2,1)S(1)}, bf16[80,128]{1,0:T(8,128)(2,1)S(1)}, u32[]{:S(2)}, u32[]{:S(2)}) collective-permute-start(bf16[80,128]{1,0:T(8,128)(2,1)S(1)} %get-tuple-element.226.refs_0_), channel_id=1, source_target_pairs={{0,16},{2,18},{4,20},{6,22},{8,24},{10,26},{12,28},{14,30},{16,0},... | collective-permute-start | bytes 61448 | tf_op jit(solution)/shard_map/ppermute | solution.py:527
  23.4 5.6 %collective-permute-start.67 = (bf16[80,128]{1,0:T(8,128)(2,1)S(1)}, bf16[80,128]{1,0:T(8,128)(2,1)S(1)}, u32[]{:S(2)}, u32[]{:S(2)}) collective-permute-start(bf16[80,128]{1,0:T(8,128)(2,1)S(1)} %get-tuple-element.226.refs_0_), channel_id=1, source_target_pairs={{0,24},{2,26},{4,28},{6,30},{8,16},{10,18},{12,20},{14,22},{16,8},... | collective-permute-start | bytes 61448 | tf_op jit(solution)/shard_map/ppermute | solution.py:527
  29.1 4.2 %collective-permute-start.69 = (bf16[2,80,128]{2,1,0:T(8,128)(2,1)S(1)}, bf16[2,80,128]{2,1,0:T(8,128)(2,1)S(1)}, u32[]{:S(2)}, u32[]{:S(2)}) collective-permute-start(bf16[2,80,128]{2,1,0:T(8,128)(2,1)S(1)} %get-tuple-element.229), channel_id=1, source_target_pairs={{0,4},{2,6},{4,0},{6,2},{8,12},{10,14},{12,8},{14,10},{16,20},{18,... | collective-permute-start | bytes 122888 | tf_op jit(solution)/shard_map/ppermute | solution.py:527
  30.1 3.8 %collective-permute-start.70 = (bf16[2,80,128]{2,1,0:T(8,128)(2,1)S(1)}, bf16[2,80,128]{2,1,0:T(8,128)(2,1)S(1)}, u32[]{:S(2)}, u32[]{:S(2)}) collective-permute-start(bf16[2,80,128]{2,1,0:T(8,128)(2,1)S(1)} %get-tuple-element.230), channel_id=1, source_target_pairs={{0,6},{2,4},{4,2},{6,0},{8,14},{10,12},{12,10},{14,8},{16,22},{18,... | collective-permute-start | bytes 122888 | tf_op jit(solution)/shard_map/ppermute | solution.py:527
  36.1 5.0 %collective-permute-start.4 = (bf16[80,128]{1,0:T(8,128)(2,1)S(1)}, bf16[80,128]{1,0:T(8,128)(2,1)S(1)}, u32[]{:S(2)}, u32[]{:S(2)}) collective-permute-start(bf16[80,128]{1,0:T(8,128)(2,1)S(1)} %param.2), channel_id=1, source_target_pairs={{0,16},{2,18},{4,20},{6,22},{8,24},{10,26},{12,28},{14,30},{16,0},... | collective-permute-start | bytes 61448 | tf_op jit(solution)/shard_map/cond/branch_2_fun/ppermute | solution.py:527
  36.6 4.5 %collective-permute-start.5 = (bf16[80,128]{1,0:T(8,128)(2,1)S(1)}, bf16[80,128]{1,0:T(8,128)(2,1)S(1)}, u32[]{:S(2)}, u32[]{:S(2)}) collective-permute-start(bf16[80,128]{1,0:T(8,128)(2,1)S(1)} %param.2), channel_id=1, source_target_pairs={{0,6},{2,4},{4,2},{6,0},{8,14},{10,12},{12,10},{14,8},{16,22},{18,... | collective-permute-start | bytes 61448 | tf_op jit(solution)/shard_map/cond/branch_2_fun/ppermute | solution.py:527
  44.8 4.7 %collective-permute-start.33 = (bf16[80,128]{1,0:T(8,128)(2,1)S(1)}, bf16[80,128]{1,0:T(8,128)(2,1)S(1)}, u32[]{:S(2)}, u32[]{:S(2)}) collective-permute-start(bf16[80,128]{1,0:T(8,128)(2,1)S(1)} %get-tuple-element.108), channel_id=1, source_target_pairs={{0,16},{2,18},{4,20},{6,22},{8,24},{10,26},{12,28},{14,30},{16,0},... | collective-permute-start | bytes 61448 | tf_op jit(solution)/shard_map/cond/branch_2_fun/ppermute | solution.py:527
  46.3 3.4 %collective-permute-start.34 = (bf16[80,128]{1,0:T(8,128)(2,1)S(1)}, bf16[80,128]{1,0:T(8,128)(2,1)S(1)}, u32[]{:S(2)}, u32[]{:S(2)}) collective-permute-start(bf16[80,128]{1,0:T(8,128)(2,1)S(1)} %get-tuple-element.109), channel_id=1, source_target_pairs={{0,6},{2,4},{4,2},{6,0},{8,14},{10,12},{12,10},{14,8},{16,22},{18,... | collective-permute-start | bytes 61448 | tf_op jit(solution)/shard_map/cond/branch_2_fun/ppermute | solution.py:527
  53.4 7.8 %collective-permute-start.71 = (bf16[2,80,128]{2,1,0:T(8,128)(2,1)S(1)}, bf16[2,80,128]{2,1,0:T(8,128)(2,1)S(1)}, u32[]{:S(2)}, u32[]{:S(2)}) collective-permute-start(bf16[2,80,128]{2,1,0:T(8,128)(2,1)S(1)} %get-tuple-element.242.refs_0_), channel_id=1, source_target_pairs={{0,8},{2,10},{4,12},{6,14},{8,0},{10,2},{12,4},{14,6},{16,24},{18,... | collective-permute-start | bytes 122888 | tf_op jit(solution)/shard_map/ppermute | solution.py:527
  56.0 5.2 %collective-permute-start.72 = (bf16[2,80,128]{2,1,0:T(8,128)(2,1)S(1)}, bf16[2,80,128]{2,1,0:T(8,128)(2,1)S(1)}, u32[]{:S(2)}, u32[]{:S(2)}) collective-permute-start(bf16[2,80,128]{2,1,0:T(8,128)(2,1)S(1)} %get-tuple-element.242.refs_0_), channel_id=1, source_target_pairs={{0,16},{2,18},{4,20},{6,22},{8,24},{10,26},{12,28},{14,30},{16,0},... | collective-permute-start | bytes 122888 | tf_op jit(solution)/shard_map/ppermute | solution.py:527
  57.6 5.8 %collective-permute-start.73 = (bf16[2,80,128]{2,1,0:T(8,128)(2,1)S(1)}, bf16[2,80,128]{2,1,0:T(8,128)(2,1)S(1)}, u32[]{:S(2)}, u32[]{:S(2)}) collective-permute-start(bf16[2,80,128]{2,1,0:T(8,128)(2,1)S(1)} %get-tuple-element.242.refs_0_), channel_id=1, source_target_pairs={{0,24},{2,26},{4,28},{6,30},{8,16},{10,18},{12,20},{14,22},{16,8},... | collective-permute-start | bytes 122888 | tf_op jit(solution)/shard_map/ppermute | solution.py:527
  58.4 17.6 %collective-permute-start.80 = (bf16[2,128,128]{2,1,0:T(8,128)(2,1)S(1)}, bf16[2,128,128]{2,1,0:T(8,128)(2,1)S(1)}, u32[]{:S(2)}, u32[]{:S(2)}) collective-permute-start(bf16[2,128,128]{2,1,0:T(8,128)(2,1)S(1)} %get-tuple-element.240.refs_5_.refs_1_), channel_id=1, source_target_pairs={{0,1},{1,0},{2,3},{3,2},{4,5},{5,4},{6,7},{7,6},{8,9},{9,8},{10,11... | collective-permute-start | bytes 196616 | tf_op jit(solution)/shard_map/ppermute | solution.py:563
  63.6 3.8 %collective-permute-start.75 = (bf16[80,128]{1,0:T(8,128)(2,1)S(1)}, bf16[80,128]{1,0:T(8,128)(2,1)S(1)}, u32[]{:S(2)}, u32[]{:S(2)}) collective-permute-start(bf16[80,128]{1,0:T(8,128)(2,1)S(1)} %get-tuple-element.248), channel_id=1, source_target_pairs={{0,4},{2,6},{4,0},{6,2},{8,12},{10,14},{12,8},{14,10},{16,20},{18,... | collective-permute-start | bytes 61448 | tf_op jit(solution)/shard_map/ppermute | solution.py:527
  70.5 6.5 %collective-permute-start.77 = (bf16[2,80,128]{2,1,0:T(8,128)(2,1)S(1)}, bf16[2,80,128]{2,1,0:T(8,128)(2,1)S(1)}, u32[]{:S(2)}, u32[]{:S(2)}) collective-permute-start(bf16[2,80,128]{2,1,0:T(8,128)(2,1)S(1)} %get-tuple-element.257.refs_0_), channel_id=1, source_target_pairs={{0,8},{2,10},{4,12},{6,14},{8,0},{10,2},{12,4},{14,6},{16,24},{18,... | collective-permute-start | bytes 122888 | tf_op jit(solution)/shard_map/ppermute | solution.py:527
  70.6 6.5 %collective-permute-start.78 = (bf16[2,80,128]{2,1,0:T(8,128)(2,1)S(1)}, bf16[2,80,128]{2,1,0:T(8,128)(2,1)S(1)}, u32[]{:S(2)}, u32[]{:S(2)}) collective-permute-start(bf16[2,80,128]{2,1,0:T(8,128)(2,1)S(1)} %get-tuple-element.257.refs_0_), channel_id=1, source_target_pairs={{0,16},{2,18},{4,20},{6,22},{8,24},{10,26},{12,28},{14,30},{16,0},... | collective-permute-start | bytes 122888 | tf_op jit(solution)/shard_map/ppermute | solution.py:527
  72.0 5.8 %collective-permute-start.79 = (bf16[2,80,128]{2,1,0:T(8,128)(2,1)S(1)}, bf16[2,80,128]{2,1,0:T(8,128)(2,1)S(1)}, u32[]{:S(2)}, u32[]{:S(2)}) collective-permute-start(bf16[2,80,128]{2,1,0:T(8,128)(2,1)S(1)} %get-tuple-element.257.refs_0_), channel_id=1, source_target_pairs={{0,24},{2,26},{4,28},{6,30},{8,16},{10,18},{12,20},{14,22},{16,8},... | collective-permute-start | bytes 122888 | tf_op jit(solution)/shard_map/ppermute | solution.py:527
  78.0 3.8 %collective-permute-start.82 = (bf16[80,128]{1,0:T(8,128)(2,1)S(1)}, bf16[80,128]{1,0:T(8,128)(2,1)S(1)}, u32[]{:S(2)}, u32[]{:S(2)}) collective-permute-start(bf16[80,128]{1,0:T(8,128)(2,1)S(1)} %get-tuple-element.263), channel_id=1, source_target_pairs={{0,4},{2,6},{4,0},{6,2},{8,12},{10,14},{12,8},{14,10},{16,20},{18,... | collective-permute-start | bytes 61448 | tf_op jit(solution)/shard_map/ppermute | solution.py:527
  82.6 4.0 %collective-permute-start.84 = (bf16[128,128]{1,0:T(8,128)(2,1)S(1)}, bf16[128,128]{1,0:T(8,128)(2,1)S(1)}, u32[]{:S(2)}, u32[]{:S(2)}) collective-permute-start(bf16[128,128]{1,0:T(8,128)(2,1)S(1)} %shard_map.71.refs_0_), channel_id=1, source_target_pairs={{0,1},{1,0},{2,3},{3,2},{4,5},{5,4},{6,7},{7,6},{8,9},{9,8},{10,11... | collective-permute-start | bytes 98312 | tf_op jit(solution)/shard_map/ppermute | solution.py:563
  (6 other events, 18.2 us)

commit v4 on v3

--- a/solution.py
+++ b/solution.py
@@ -443,8 +443,11 @@
 
 
 def last_kernel(depth, pairs, *refs):
-    came, (old_ref, table_ref, field_ref) = refs[:LOW], refs[LOW:]
+    came, (old_ref, table_ref, field_ref, message_ref) = refs[:LOW], refs[LOW:]
     arrive(depth, pairs, came, old_ref, table_ref, field_ref)
+    wide = field_ref[...].astype(jnp.float32)
+    extent = wide.shape[0] // pairs
+    message_ref[...] = fold([wide[k * extent : (k + 1) * extent] for k in range(pairs)])
 
 
 def part_kernel(field_ref, *refs):
@@ -460,7 +463,7 @@
     fields, weighed = refs[: groups - 1], refs[groups - 1 : -2]
     for g, field_ref in enumerate(fields):
         pairs = len(weighed) // len(fields)
-        part = weighted_sum(weighed[g * pairs : (g + 1) * pairs], field_ref[...], math.isqrt(width))
+        part = weighted_sum(weighed[g * pairs : (g + 1) * pairs], unfold(field_ref[...], pairs), math.isqrt(width))
         total = total + part.astype(jnp.bfloat16).astype(jnp.float32)
     real = jnp.concatenate([entry(table_ref, DEPTH)] * (WIDE // LANES), axis=1) >= 0
     total = jnp.where(real, total, 0.0).astype(jnp.bfloat16)
@@ -676,10 +679,10 @@
                 mixed,
                 table,
             )
-    field = call(functools.partial(last_kernel, depths - 1, pairs), mats, *came, field, table)
+    field, sent = call(functools.partial(last_kernel, depths - 1, pairs), [mats, message], *came, field, table)
     out = jax.ShapeDtypeStruct((1, extent // groups, extent * extent), jnp.bfloat16)
     tall_part = jax.ShapeDtypeStruct((extent * extent * extent // groups // WIDE, WIDE), jnp.bfloat16)
-    fields = others(field)
+    fields = others(sent)
     own = call(part_kernel, tall_part, field, *weighed[:pairs], kept=False)
     own, fields = lax.optimization_barrier((own, fields))
     rest = weighed[pairs:]

time: 89 us -> 88.5 us (level); the launches traced: 87.9 us -> 88.7 us
  starting transfers between devices: 33.1 us -> 36.9 us
  waiting for transfers between devices: 26.4 us -> 23.2 us
    ppermute x28, starting transfers between devices: 29.9 us -> 34 us  [exchange(): return lax.ppermute(value, 'node', [(i, i ^ mask) for i in range(nodes)])]
    ppermute x28, waiting for transfers between devices: 24.6 us -> 21.3 us  [exchange(): return lax.ppermute(value, 'node', [(i, i ^ mask) for i in range(nodes)])]
  transfers between devices with their start and end apart: 30 -> 30, of which waited for: 18 -> 19; matrix products, arithmetic and copies ran while one was open for 0% -> 0% of each run, Pallas kernels for 12% -> 11%
where the time goes in v4:
time: 88.5 us; the launch traced here: 88.7 us
  starting transfers between devices  36.9 us (42%)
  Pallas kernels  27.6 us (31%)
  waiting for transfers between devices  23.2 us (26%)
  between operations  0.9 us (1%)
    ppermute x28, starting transfers between devices, exchange(): return lax.ppermute(value, 'node', [(i, i ^ mask) for i in range(nodes)])  34 us
    pallas_call x21, Pallas kernels, call(): pl.pallas_call(without, out_shape=shapes if isinstance(out_shape, list) e...  27.6 us
    ppermute x28, waiting for transfers between devices, exchange(): return lax.ppermute(value, 'node', [(i, i ^ mask) for i in range(nodes)])  21.3 us
    ppermute x2, starting transfers between devices, others(): lax.ppermute(value, 'term', [(i, (i + shift) % groups) for i in range(gro...  2.9 us
    ppermute x2, waiting for transfers between devices, others(): lax.ppermute(value, 'term', [(i, (i + shift) % groups) for i in range(gro...  1.88 us
  transfers between devices with their start and end apart: 30, of which 19 were waited for; matrix products, arithmetic and copies ran while one was open for 0% of the time, Pallas kernels for 11%

profile of v4, /device:TPU:0, one launch (start us, length us, event | category | flops | bytes accessed | tf_op | source)
XLA Modules:
  0.0 88.7 jit_solution(4698511734353742995)
XLA Ops:
  0.0 3.9 %shard_map.55 = (bf16[64,4096]{1,0:T(8,128)(2,1)S(1)}, bf16[64,4096]{1,0:T(8,128)(2,1)S(1)}, bf16[64,4096]{1,0:T(8,128)(2,1)S(1)}, bf16[128,128]{1,0:T(8,128)(2,...) custom-call(bf16[1,64,4096]{2,1,0:T(8,128)(2,1)} %refs_0_.1, ...), custom_call_target="tpu_custom_call" | custom-call | tf_op jit(solution)/shard_map/pallas_call | solution.py:519
  3.9 3.1 %collective-permute-start.59 = (bf16[80,128]{1,0:T(8,128)(2,1)S(1)}, bf16[80,128]{1,0:T(8,128)(2,1)S(1)}, u32[]{:S(2)}, u32[]{:S(2)}) collective-permute-start(bf16[80,128]{1,0:T(8,128)(2,1)S(1)} %get-tuple-element.211.refs_0_), channel_id=1, source_target_pairs={{0,8},{2,10},{4,12},{6,14},{8,0},{10,2},{12,4},{14,6},{16,24},{18,... | collective-permute-start | bytes 61448 | tf_op jit(solution)/shard_map/ppermute | solution.py:530
  7.0 2.6 %collective-permute-start.60 = (bf16[80,128]{1,0:T(8,128)(2,1)S(1)}, bf16[80,128]{1,0:T(8,128)(2,1)S(1)}, u32[]{:S(2)}, u32[]{:S(2)}) collective-permute-start(bf16[80,128]{1,0:T(8,128)(2,1)S(1)} %get-tuple-element.211.refs_0_), channel_id=1, source_target_pairs={{0,16},{2,18},{4,20},{6,22},{8,24},{10,26},{12,28},{14,30},{16,0},... | collective-permute-start | bytes 61448 | tf_op jit(solution)/shard_map/ppermute | solution.py:530
  9.6 2.3 %collective-permute-done.60.refs_2_ = bf16[80,128]{1,0:T(8,128)(2,1)S(1)} collective-permute-done((bf16[80,128]{1,0:T(8,128)(2,1)S(1)}, bf16[80,128]{1,0:T(8,128)(2,1)S(1)}, u32[]{:S(2)}, u32[]{:S(2)}) %collective-permute-start.60) | collective-permute-done | bytes 20512 | tf_op jit(solution)/shard_map/ppermute | solution.py:530
  11.8 3.3 %collective-permute-done.61.refs_3_ = bf16[80,128]{1,0:T(8,128)(2,1)S(1)} collective-permute-done((bf16[80,128]{1,0:T(8,128)(2,1)S(1)}, bf16[80,128]{1,0:T(8,128)(2,1)S(1)}, u32[]{:S(2)}, u32[]{:S(2)}) %collective-permute-start.61) | collective-permute-done | bytes 20512 | tf_op jit(solution)/shard_map/ppermute | solution.py:530
  15.3 1.5 %collective-permute-start.63 = (bf16[2,80,128]{2,1,0:T(8,128)(2,1)S(1)}, bf16[2,80,128]{2,1,0:T(8,128)(2,1)S(1)}, u32[]{:S(2)}, u32[]{:S(2)}) collective-permute-start(bf16[2,80,128]{2,1,0:T(8,128)(2,1)S(1)} %get-tuple-element.215), channel_id=1, source_target_pairs={{0,4},{2,6},{4,0},{6,2},{8,12},{10,14},{12,8},{14,10},{16,20},{18,... | collective-permute-start | bytes 122888 | tf_op jit(solution)/shard_map/ppermute | solution.py:530
  20.3 2.2 %shard_map.58 = (bf16[128,128]{1,0:T(8,128)(2,1)S(1)}, bf16[128,128]{1,0:T(8,128)(2,1)S(1)}, bf16[80,128]{1,0:T(8,128)(2,1)S(1)}) custom-call(bf16[2,80,128]{2,1,0:T(8,128)(2,1)S(1)} %get-tuple-element.222.refs_0_, bf16[2,80,128]{2,1,0:T(8,128)(2,1)S(1)} %collective-permute-done.62.refs_1_, bf16[2,80,128]{2,1,0:T(8,128)(2,1)S(1)} %collective-permute-done.63.refs_2_, ...), custom_call_target="tpu_custom_call" | custom-call | tf_op jit(solution)/shard_map/pallas_call | solution.py:519
  23.4 3.6 %collective-permute-start.67 = (bf16[80,128]{1,0:T(8,128)(2,1)S(1)}, bf16[80,128]{1,0:T(8,128)(2,1)S(1)}, u32[]{:S(2)}, u32[]{:S(2)}) collective-permute-start(bf16[80,128]{1,0:T(8,128)(2,1)S(1)} %get-tuple-element.228.refs_0_), channel_id=1, source_target_pairs={{0,24},{2,26},{4,28},{6,30},{8,16},{10,18},{12,20},{14,22},{16,8},... | collective-permute-start | bytes 61448 | tf_op jit(solution)/shard_map/ppermute | solution.py:530
  27.4 1.6 %collective-permute-done.67.refs_3_ = bf16[80,128]{1,0:T(8,128)(2,1)S(1)} collective-permute-done((bf16[80,128]{1,0:T(8,128)(2,1)S(1)}, bf16[80,128]{1,0:T(8,128)(2,1)S(1)}, u32[]{:S(2)}, u32[]{:S(2)}) %collective-permute-start.67) | collective-permute-done | bytes 20512 | tf_op jit(solution)/shard_map/ppermute | solution.py:530
  31.7 1.7 %collective-permute-done.69.refs_2_ = bf16[2,80,128]{2,1,0:T(8,128)(2,1)S(1)} collective-permute-done((bf16[2,80,128]{2,1,0:T(8,128)(2,1)S(1)}, bf16[2,80,128]{2,1,0:T(8,128)(2,1)S(1)}, u32[]{:S(2)}, u32[]{:S(2)}) %collective-permute-start.69) | collective-permute-done | bytes 40992 | tf_op jit(solution)/shard_map/ppermute | solution.py:530
  33.9 2.2 %shard_map.60 = (bf16[128,128]{1,0:T(8,128)(2,1)S(1)}, bf16[128,128]{1,0:T(8,128)(2,1)S(1)}, bf16[80,128]{1,0:T(8,128)(2,1)S(1)}) custom-call(bf16[2,80,128]{2,1,0:T(8,128)(2,1)S(1)} %get-tuple-element.229.refs_0_, bf16[2,80,128]{2,1,0:T(8,128)(2,1)S(1)} %collective-permute-done.68.refs_1_, bf16[2,80,128]{2,1,0:T(8,128)(2,1)S(1)} %collective-permute-done.69.refs_2_, ...), custom_call_target="tpu_custom_call" | custom-call | tf_op jit(solution)/shard_map/pallas_call | solution.py:519
  36.0 6.0 %conditional.2 = (bf16[2,80,128]{2,1,0:T(8,128)(2,1)S(1)}) conditional(s32[]{:T(128)} %bitcast.1, bf16[80,128]{1,0:T(8,128)(2,1)S(1)} %get-tuple-element.235, bf16[80,128]{1,0:T(8,128)(2,1)S(1)} %get-tuple-element.235, bf16[80,128]{1,0:T(8,128)(2,1)S(1)} %get-tuple-element.235, ...), branch_computations={%region_0.0_spmd, %region_1.0_spmd, %region_2.0_spmd, %region_3.0_... | conditional | bytes 163928 | solution.py:584
  36.5 3.7 %collective-permute-start.7 = (bf16[80,128]{1,0:T(8,128)(2,1)S(1)}, bf16[80,128]{1,0:T(8,128)(2,1)S(1)}, u32[]{:S(2)}, u32[]{:S(2)}) collective-permute-start(bf16[80,128]{1,0:T(8,128)(2,1)S(1)} %param.3), channel_id=1, source_target_pairs={{0,8},{2,10},{4,12},{6,14},{8,0},{10,2},{12,4},{14,6},{16,24},{18,... | collective-permute-start | bytes 61448 | tf_op jit(solution)/shard_map/cond/branch_3_fun/ppermute | solution.py:530
  42.1 3.7 %shard_map.61 = (bf16[2,128,128]{2,1,0:T(8,128)(2,1)S(1)}, bf16[2,80,128]{2,1,0:T(8,128)(2,1)S(1)}) custom-call(bf16[2,80,128]{2,1,0:T(8,128)(2,1)S(1)} %get-tuple-element.282.refs_0_, bf16[64,4096]{1,0:T(8,128)(2,1)S(1)} %get-tuple-element.236.refs_1_.refs_4_, bf16[64,4096]{1,0:T(8,128)(2,1)S(1)} %get-tuple-element.217.refs_0_.refs_4_.refs_2_.refs_5_, ...), custom_call_target="tpu_custom_call" | custom-call | tf_op jit(solution)/shard_map/pallas_call | solution.py:519
  45.8 5.0 %conditional.3 = (bf16[2,80,128]{2,1,0:T(8,128)(2,1)S(1)}) conditional(s32[]{:T(128)} %bitcast.1, (bf16[80,128]{1,0:T(8,128)(2,1)S(1)}, bf16[80,128]{1,0:T(8,128)(2,1)S(1)}) %tuple.102, (bf16[80,128]{1,0:T(8,128)(2,1)S(1)}, bf16[80,128]{1,0:T(8,128)(2,1)S(1)}) %tuple.102, (bf16[80,128]{1,0:T(8,128)(2,1)S(1)}, ...), branch_computations={%region_15.0_spmd, %region_16.0_spmd, %region_17.0_spmd, %region_1... | conditional | bytes 163928 | solution.py:584
  46.7 2.1 %collective-permute-start.36 = (bf16[80,128]{1,0:T(8,128)(2,1)S(1)}, bf16[80,128]{1,0:T(8,128)(2,1)S(1)}, u32[]{:S(2)}, u32[]{:S(2)}) collective-permute-start(bf16[80,128]{1,0:T(8,128)(2,1)S(1)} %get-tuple-element.114), channel_id=1, source_target_pairs={{0,8},{2,10},{4,12},{6,14},{8,0},{10,2},{12,4},{14,6},{16,24},{18,... | collective-permute-start | bytes 61448 | tf_op jit(solution)/shard_map/cond/branch_3_fun/ppermute | solution.py:530
  48.8 1.8 %collective-permute-done.35.refs_0_ = bf16[80,128]{1,0:T(8,128)(2,1)S(1)} collective-permute-done((bf16[80,128]{1,0:T(8,128)(2,1)S(1)}, bf16[80,128]{1,0:T(8,128)(2,1)S(1)}, u32[]{:S(2)}, u32[]{:S(2)}) %collective-permute-start.35) | collective-permute-done | bytes 20512 | tf_op jit(solution)/shard_map/cond/branch_3_fun/ppermute | solution.py:530
  50.8 3.7 %shard_map.62 = (bf16[128,128]{1,0:T(8,128)(2,1)S(1)}, bf16[2,80,128]{2,1,0:T(8,128)(2,1)S(1)}) custom-call(bf16[2,80,128]{2,1,0:T(8,128)(2,1)S(1)} %get-tuple-element.283.refs_0_, bf16[64,4096]{1,0:T(8,128)(2,1)S(1)} %get-tuple-element.236.refs_1_.refs_4_, bf16[64,4096]{1,0:T(8,128)(2,1)S(1)} %get-tuple-element.217.refs_0_.refs_4_.refs_2_.refs_5_, ...), custom_call_target="tpu_custom_call" | custom-call | tf_op jit(solution)/shard_map/pallas_call | solution.py:519
  54.4 1.9 %collective-permute-start.71 = (bf16[2,80,128]{2,1,0:T(8,128)(2,1)S(1)}, bf16[2,80,128]{2,1,0:T(8,128)(2,1)S(1)}, u32[]{:S(2)}, u32[]{:S(2)}) collective-permute-start(bf16[2,80,128]{2,1,0:T(8,128)(2,1)S(1)} %get-tuple-element.244.refs_0_), channel_id=1, source_target_pairs={{0,8},{2,10},{4,12},{6,14},{8,0},{10,2},{12,4},{14,6},{16,24},{18,... | collective-permute-start | bytes 122888 | tf_op jit(solution)/shard_map/ppermute | solution.py:530
  56.3 2.0 %collective-permute-start.72 = (bf16[2,80,128]{2,1,0:T(8,128)(2,1)S(1)}, bf16[2,80,128]{2,1,0:T(8,128)(2,1)S(1)}, u32[]{:S(2)}, u32[]{:S(2)}) collective-permute-start(bf16[2,80,128]{2,1,0:T(8,128)(2,1)S(1)} %get-tuple-element.244.refs_0_), channel_id=1, source_target_pairs={{0,16},{2,18},{4,20},{6,22},{8,24},{10,26},{12,28},{14,30},{16,0},... | collective-permute-start | bytes 122888 | tf_op jit(solution)/shard_map/ppermute | solution.py:530
  61.7 2.4 %collective-permute-done.73.refs_3_ = bf16[2,80,128]{2,1,0:T(8,128)(2,1)S(1)} collective-permute-done((bf16[2,80,128]{2,1,0:T(8,128)(2,1)S(1)}, bf16[2,80,128]{2,1,0:T(8,128)(2,1)S(1)}, u32[]{:S(2)}, u32[]{:S(2)}) %collective-permute-start.73) | collective-permute-done | bytes 40992 | tf_op jit(solution)/shard_map/ppermute | solution.py:530
  68.5 2.8 %shard_map.66 = (bf16[128,128]{1,0:T(8,128)(2,1)S(1)}, bf16[2,80,128]{2,1,0:T(8,128)(2,1)S(1)}) custom-call(bf16[80,128]{1,0:T(8,128)(2,1)S(1)} %get-tuple-element.252.refs_0_, bf16[80,128]{1,0:T(8,128)(2,1)S(1)} %collective-permute-done.74.refs_1_, bf16[80,128]{1,0:T(8,128)(2,1)S(1)} %collective-permute-done.75.refs_2_, ...), custom_call_target="tpu_custom_call" | custom-call | tf_op jit(solution)/shard_map/pallas_call | solution.py:519
  72.7 3.0 %collective-permute-start.79 = (bf16[2,80,128]{2,1,0:T(8,128)(2,1)S(1)}, bf16[2,80,128]{2,1,0:T(8,128)(2,1)S(1)}, u32[]{:S(2)}, u32[]{:S(2)}) collective-permute-start(bf16[2,80,128]{2,1,0:T(8,128)(2,1)S(1)} %get-tuple-element.259.refs_0_), channel_id=1, source_target_pairs={{0,24},{2,26},{4,28},{6,30},{8,16},{10,18},{12,20},{14,22},{16,8},... | collective-permute-start | bytes 122888 | tf_op jit(solution)/shard_map/ppermute | solution.py:530
  85.3 1.9 %collective-permute-done.84.refs_1_ = bf16[80,128]{1,0:T(8,128)(2,1)S(1)} collective-permute-done((bf16[80,128]{1,0:T(8,128)(2,1)S(1)}, bf16[80,128]{1,0:T(8,128)(2,1)S(1)}, u32[]{:S(2)}, u32[]{:S(2)}) %collective-permute-start.84) | collective-permute-done | bytes 20512 | tf_op jit(solution)/shard_map/ppermute | solution.py:566
  (60 shorter events, 30.8 us)
Async XLA Ops:
  3.9 5.7 %collective-permute-start.59 = (bf16[80,128]{1,0:T(8,128)(2,1)S(1)}, bf16[80,128]{1,0:T(8,128)(2,1)S(1)}, u32[]{:S(2)}, u32[]{:S(2)}) collective-permute-start(bf16[80,128]{1,0:T(8,128)(2,1)S(1)} %get-tuple-element.211.refs_0_), channel_id=1, source_target_pairs={{0,8},{2,10},{4,12},{6,14},{8,0},{10,2},{12,4},{14,6},{16,24},{18,... | collective-permute-start | bytes 61448 | tf_op jit(solution)/shard_map/ppermute | solution.py:530
  7.0 4.9 %collective-permute-start.60 = (bf16[80,128]{1,0:T(8,128)(2,1)S(1)}, bf16[80,128]{1,0:T(8,128)(2,1)S(1)}, u32[]{:S(2)}, u32[]{:S(2)}) collective-permute-start(bf16[80,128]{1,0:T(8,128)(2,1)S(1)} %get-tuple-element.211.refs_0_), channel_id=1, source_target_pairs={{0,16},{2,18},{4,20},{6,22},{8,24},{10,26},{12,28},{14,30},{16,0},... | collective-permute-start | bytes 61448 | tf_op jit(solution)/shard_map/ppermute | solution.py:530
  9.6 5.6 %collective-permute-start.61 = (bf16[80,128]{1,0:T(8,128)(2,1)S(1)}, bf16[80,128]{1,0:T(8,128)(2,1)S(1)}, u32[]{:S(2)}, u32[]{:S(2)}) collective-permute-start(bf16[80,128]{1,0:T(8,128)(2,1)S(1)} %get-tuple-element.211.refs_0_), channel_id=1, source_target_pairs={{0,24},{2,26},{4,28},{6,30},{8,16},{10,18},{12,20},{14,22},{16,8},... | collective-permute-start | bytes 61448 | tf_op jit(solution)/shard_map/ppermute | solution.py:530
  15.3 4.1 %collective-permute-start.63 = (bf16[2,80,128]{2,1,0:T(8,128)(2,1)S(1)}, bf16[2,80,128]{2,1,0:T(8,128)(2,1)S(1)}, u32[]{:S(2)}, u32[]{:S(2)}) collective-permute-start(bf16[2,80,128]{2,1,0:T(8,128)(2,1)S(1)} %get-tuple-element.215), channel_id=1, source_target_pairs={{0,4},{2,6},{4,0},{6,2},{8,12},{10,14},{12,8},{14,10},{16,20},{18,... | collective-permute-start | bytes 122888 | tf_op jit(solution)/shard_map/ppermute | solution.py:530
  16.8 3.5 %collective-permute-start.64 = (bf16[2,80,128]{2,1,0:T(8,128)(2,1)S(1)}, bf16[2,80,128]{2,1,0:T(8,128)(2,1)S(1)}, u32[]{:S(2)}, u32[]{:S(2)}) collective-permute-start(bf16[2,80,128]{2,1,0:T(8,128)(2,1)S(1)} %get-tuple-element.216), channel_id=1, source_target_pairs={{0,6},{2,4},{4,2},{6,0},{8,14},{10,12},{12,10},{14,8},{16,22},{18,... | collective-permute-start | bytes 122888 | tf_op jit(solution)/shard_map/ppermute | solution.py:530
  22.5 4.5 %collective-permute-start.65 = (bf16[80,128]{1,0:T(8,128)(2,1)S(1)}, bf16[80,128]{1,0:T(8,128)(2,1)S(1)}, u32[]{:S(2)}, u32[]{:S(2)}) collective-permute-start(bf16[80,128]{1,0:T(8,128)(2,1)S(1)} %get-tuple-element.228.refs_0_), channel_id=1, source_target_pairs={{0,8},{2,10},{4,12},{6,14},{8,0},{10,2},{12,4},{14,6},{16,24},{18,... | collective-permute-start | bytes 61448 | tf_op jit(solution)/shard_map/ppermute | solution.py:530
  22.6 4.7 %collective-permute-start.66 = (bf16[80,128]{1,0:T(8,128)(2,1)S(1)}, bf16[80,128]{1,0:T(8,128)(2,1)S(1)}, u32[]{:S(2)}, u32[]{:S(2)}) collective-permute-start(bf16[80,128]{1,0:T(8,128)(2,1)S(1)} %get-tuple-element.228.refs_0_), channel_id=1, source_target_pairs={{0,16},{2,18},{4,20},{6,22},{8,24},{10,26},{12,28},{14,30},{16,0},... | collective-permute-start | bytes 61448 | tf_op jit(solution)/shard_map/ppermute | solution.py:530
  23.4 5.6 %collective-permute-start.67 = (bf16[80,128]{1,0:T(8,128)(2,1)S(1)}, bf16[80,128]{1,0:T(8,128)(2,1)S(1)}, u32[]{:S(2)}, u32[]{:S(2)}) collective-permute-start(bf16[80,128]{1,0:T(8,128)(2,1)S(1)} %get-tuple-element.228.refs_0_), channel_id=1, source_target_pairs={{0,24},{2,26},{4,28},{6,30},{8,16},{10,18},{12,20},{14,22},{16,8},... | collective-permute-start | bytes 61448 | tf_op jit(solution)/shard_map/ppermute | solution.py:530
  29.1 4.2 %collective-permute-start.69 = (bf16[2,80,128]{2,1,0:T(8,128)(2,1)S(1)}, bf16[2,80,128]{2,1,0:T(8,128)(2,1)S(1)}, u32[]{:S(2)}, u32[]{:S(2)}) collective-permute-start(bf16[2,80,128]{2,1,0:T(8,128)(2,1)S(1)} %get-tuple-element.231), channel_id=1, source_target_pairs={{0,4},{2,6},{4,0},{6,2},{8,12},{10,14},{12,8},{14,10},{16,20},{18,... | collective-permute-start | bytes 122888 | tf_op jit(solution)/shard_map/ppermute | solution.py:530
  30.1 3.8 %collective-permute-start.70 = (bf16[2,80,128]{2,1,0:T(8,128)(2,1)S(1)}, bf16[2,80,128]{2,1,0:T(8,128)(2,1)S(1)}, u32[]{:S(2)}, u32[]{:S(2)}) collective-permute-start(bf16[2,80,128]{2,1,0:T(8,128)(2,1)S(1)} %get-tuple-element.232), channel_id=1, source_target_pairs={{0,6},{2,4},{4,2},{6,0},{8,14},{10,12},{12,10},{14,8},{16,22},{18,... | collective-permute-start | bytes 122888 | tf_op jit(solution)/shard_map/ppermute | solution.py:530
  36.1 5.1 %collective-permute-start.6 = (bf16[80,128]{1,0:T(8,128)(2,1)S(1)}, bf16[80,128]{1,0:T(8,128)(2,1)S(1)}, u32[]{:S(2)}, u32[]{:S(2)}) collective-permute-start(bf16[80,128]{1,0:T(8,128)(2,1)S(1)} %param.3), channel_id=1, source_target_pairs={{0,16},{2,18},{4,20},{6,22},{8,24},{10,26},{12,28},{14,30},{16,0},... | collective-permute-start | bytes 61448 | tf_op jit(solution)/shard_map/cond/branch_3_fun/ppermute | solution.py:530
  36.5 5.5 %collective-permute-start.7 = (bf16[80,128]{1,0:T(8,128)(2,1)S(1)}, bf16[80,128]{1,0:T(8,128)(2,1)S(1)}, u32[]{:S(2)}, u32[]{:S(2)}) collective-permute-start(bf16[80,128]{1,0:T(8,128)(2,1)S(1)} %param.3), channel_id=1, source_target_pairs={{0,8},{2,10},{4,12},{6,14},{8,0},{10,2},{12,4},{14,6},{16,24},{18,... | collective-permute-start | bytes 61448 | tf_op jit(solution)/shard_map/cond/branch_3_fun/ppermute | solution.py:530
  45.8 4.8 %collective-permute-start.35 = (bf16[80,128]{1,0:T(8,128)(2,1)S(1)}, bf16[80,128]{1,0:T(8,128)(2,1)S(1)}, u32[]{:S(2)}, u32[]{:S(2)}) collective-permute-start(bf16[80,128]{1,0:T(8,128)(2,1)S(1)} %get-tuple-element.110), channel_id=1, source_target_pairs={{0,16},{2,18},{4,20},{6,22},{8,24},{10,26},{12,28},{14,30},{16,0},... | collective-permute-start | bytes 61448 | tf_op jit(solution)/shard_map/cond/branch_3_fun/ppermute | solution.py:530
  46.7 4.1 %collective-permute-start.36 = (bf16[80,128]{1,0:T(8,128)(2,1)S(1)}, bf16[80,128]{1,0:T(8,128)(2,1)S(1)}, u32[]{:S(2)}, u32[]{:S(2)}) collective-permute-start(bf16[80,128]{1,0:T(8,128)(2,1)S(1)} %get-tuple-element.114), channel_id=1, source_target_pairs={{0,8},{2,10},{4,12},{6,14},{8,0},{10,2},{12,4},{14,6},{16,24},{18,... | collective-permute-start | bytes 61448 | tf_op jit(solution)/shard_map/cond/branch_3_fun/ppermute | solution.py:530
  54.4 7.2 %collective-permute-start.71 = (bf16[2,80,128]{2,1,0:T(8,128)(2,1)S(1)}, bf16[2,80,128]{2,1,0:T(8,128)(2,1)S(1)}, u32[]{:S(2)}, u32[]{:S(2)}) collective-permute-start(bf16[2,80,128]{2,1,0:T(8,128)(2,1)S(1)} %get-tuple-element.244.refs_0_), channel_id=1, source_target_pairs={{0,8},{2,10},{4,12},{6,14},{8,0},{10,2},{12,4},{14,6},{16,24},{18,... | collective-permute-start | bytes 122888 | tf_op jit(solution)/shard_map/ppermute | solution.py:530
  56.3 5.4 %collective-permute-start.72 = (bf16[2,80,128]{2,1,0:T(8,128)(2,1)S(1)}, bf16[2,80,128]{2,1,0:T(8,128)(2,1)S(1)}, u32[]{:S(2)}, u32[]{:S(2)}) collective-permute-start(bf16[2,80,128]{2,1,0:T(8,128)(2,1)S(1)} %get-tuple-element.244.refs_0_), channel_id=1, source_target_pairs={{0,16},{2,18},{4,20},{6,22},{8,24},{10,26},{12,28},{14,30},{16,0},... | collective-permute-start | bytes 122888 | tf_op jit(solution)/shard_map/ppermute | solution.py:530
  58.3 5.8 %collective-permute-start.73 = (bf16[2,80,128]{2,1,0:T(8,128)(2,1)S(1)}, bf16[2,80,128]{2,1,0:T(8,128)(2,1)S(1)}, u32[]{:S(2)}, u32[]{:S(2)}) collective-permute-start(bf16[2,80,128]{2,1,0:T(8,128)(2,1)S(1)} %get-tuple-element.244.refs_0_), channel_id=1, source_target_pairs={{0,24},{2,26},{4,28},{6,30},{8,16},{10,18},{12,20},{14,22},{16,8},... | collective-permute-start | bytes 122888 | tf_op jit(solution)/shard_map/ppermute | solution.py:530
  58.9 17.9 %collective-permute-start.80 = (bf16[2,128,128]{2,1,0:T(8,128)(2,1)S(1)}, bf16[2,128,128]{2,1,0:T(8,128)(2,1)S(1)}, u32[]{:S(2)}, u32[]{:S(2)}) collective-permute-start(bf16[2,128,128]{2,1,0:T(8,128)(2,1)S(1)} %get-tuple-element.242.refs_5_.refs_1_), channel_id=1, source_target_pairs={{0,1},{1,0},{2,3},{3,2},{4,5},{5,4},{6,7},{7,6},{8,9},{9,8},{10,11... | collective-permute-start | bytes 196616 | tf_op jit(solution)/shard_map/ppermute | solution.py:566
  64.3 3.8 %collective-permute-start.75 = (bf16[80,128]{1,0:T(8,128)(2,1)S(1)}, bf16[80,128]{1,0:T(8,128)(2,1)S(1)}, u32[]{:S(2)}, u32[]{:S(2)}) collective-permute-start(bf16[80,128]{1,0:T(8,128)(2,1)S(1)} %get-tuple-element.250), channel_id=1, source_target_pairs={{0,4},{2,6},{4,0},{6,2},{8,12},{10,14},{12,8},{14,10},{16,20},{18,... | collective-permute-start | bytes 61448 | tf_op jit(solution)/shard_map/ppermute | solution.py:530
  71.3 6.5 %collective-permute-start.77 = (bf16[2,80,128]{2,1,0:T(8,128)(2,1)S(1)}, bf16[2,80,128]{2,1,0:T(8,128)(2,1)S(1)}, u32[]{:S(2)}, u32[]{:S(2)}) collective-permute-start(bf16[2,80,128]{2,1,0:T(8,128)(2,1)S(1)} %get-tuple-element.259.refs_0_), channel_id=1, source_target_pairs={{0,8},{2,10},{4,12},{6,14},{8,0},{10,2},{12,4},{14,6},{16,24},{18,... | collective-permute-start | bytes 122888 | tf_op jit(solution)/shard_map/ppermute | solution.py:530
  71.4 6.5 %collective-permute-start.78 = (bf16[2,80,128]{2,1,0:T(8,128)(2,1)S(1)}, bf16[2,80,128]{2,1,0:T(8,128)(2,1)S(1)}, u32[]{:S(2)}, u32[]{:S(2)}) collective-permute-start(bf16[2,80,128]{2,1,0:T(8,128)(2,1)S(1)} %get-tuple-element.259.refs_0_), channel_id=1, source_target_pairs={{0,16},{2,18},{4,20},{6,22},{8,24},{10,26},{12,28},{14,30},{16,0},... | collective-permute-start | bytes 122888 | tf_op jit(solution)/shard_map/ppermute | solution.py:530
  72.7 5.8 %collective-permute-start.79 = (bf16[2,80,128]{2,1,0:T(8,128)(2,1)S(1)}, bf16[2,80,128]{2,1,0:T(8,128)(2,1)S(1)}, u32[]{:S(2)}, u32[]{:S(2)}) collective-permute-start(bf16[2,80,128]{2,1,0:T(8,128)(2,1)S(1)} %get-tuple-element.259.refs_0_), channel_id=1, source_target_pairs={{0,24},{2,26},{4,28},{6,30},{8,16},{10,18},{12,20},{14,22},{16,8},... | collective-permute-start | bytes 122888 | tf_op jit(solution)/shard_map/ppermute | solution.py:530
  78.8 3.8 %collective-permute-start.82 = (bf16[80,128]{1,0:T(8,128)(2,1)S(1)}, bf16[80,128]{1,0:T(8,128)(2,1)S(1)}, u32[]{:S(2)}, u32[]{:S(2)}) collective-permute-start(bf16[80,128]{1,0:T(8,128)(2,1)S(1)} %get-tuple-element.265), channel_id=1, source_target_pairs={{0,4},{2,6},{4,0},{6,2},{8,12},{10,14},{12,8},{14,10},{16,20},{18,... | collective-permute-start | bytes 61448 | tf_op jit(solution)/shard_map/ppermute | solution.py:530
  83.4 3.8 %collective-permute-start.84 = (bf16[80,128]{1,0:T(8,128)(2,1)S(1)}, bf16[80,128]{1,0:T(8,128)(2,1)S(1)}, u32[]{:S(2)}, u32[]{:S(2)}) collective-permute-start(bf16[80,128]{1,0:T(8,128)(2,1)S(1)} %get-tuple-element.275), channel_id=1, source_target_pairs={{0,1},{1,0},{2,3},{3,2},{4,5},{5,4},{6,7},{7,6},{8,9},{9,8},{10,11... | collective-permute-start | bytes 61448 | tf_op jit(solution)/shard_map/ppermute | solution.py:566
  (6 other events, 18.3 us)
